TPU v7x, 128 devices: a whole 4x4x4 slice. The times are simulated.
128 devices in a mesh: ifg: 4 (over y_lo, core), rows: 32 (over x, z, y_hi).
Axes of the slice: x: 4, y: 4 (y_hi: 2, y_lo: 2; y = y_hi * 2 + y_lo), z: 4, core: 2. Of those that a mesh axis runs over, the one named last changes fastest.
Arguments:
- phase_samples: bfloat16 [300, 64, 32768], P('ifg', 'rows'), may hold values from -6 to 6
- sample_weights: bfloat16 [300, 64, 32768], P('ifg', 'rows'), may hold values from 0.099609375 to 10
- reference_date: int32 [300], replicated, may hold values from 0 to 158, as said below
- secondary_date: int32 [300], replicated, may hold values from 1 to 159, as said below
- window_rows: int32 [9], replicated, may hold values from -1 to 1, as said below
- window_cols: int32 [9], replicated, may hold values from -4 to 4, as said below
Outputs:
- coherence: float32 [300, 32, 4096], P('ifg', 'rows')
- residual: float32 [300, 32, 4096], P('ifg', 'rows')
- displacement: float32 [159, 32, 4096], P(None, None, ('ifg', 'rows'))
Inputs may be any that keep to these rules, and one draw needn't show every extreme that they name: reference_date[k] < secondary_date[k] and secondary_date[k] - reference_date[k] <= 24 for every k; for every date d < 159 some interferogram has reference d and secondary d + 1. `secondary_date`: pairs with reference_date as stated there. `window_rows`: entry 0 is 0 and both -1 and 1 occur. `window_cols`: entry 0 is 0 and both -4 and 4 occur.
All inputs are finite; a program needn't handle non-finite values.
Results may differ from a plain program's by a relative error of at most 0.0003.
Values sent between devices are 32-bit elements; how exact they have to be, the bound alone decides.
No kernel may reach another device: no remote copies, remote signals or barrier semaphores. Data moves between devices by JAX's collectives and lax.ppermute only.
A program may use at most 192 MiB of HBM per device.

v0:
```python
import jax
import jax.numpy as jnp
from jax import lax
from jax.sharding import PartitionSpec as P

DATES = 160
AZ_LOOKS = 2
RG_LOOKS = 8
HALF_WIN = 1
COL_REACH = 4
OFFSETS = 9


damping = 0.25


def padded_2(x, sides, width):
    for axis, dim in sides:
        size, length = (lax.axis_size(axis), x.shape[dim])
        up = [(i, (i + 1) % size) for i in range(size - 1)]
        down = [(j, i) for i, j in up]
        last = lax.slice_in_dim(x, length - width, length, axis=dim)
        initial = lax.slice_in_dim(x, 0, width, axis=dim)
        before = lax.ppermute(last, axis, up)
        after = lax.ppermute(initial, axis, down)
        x = jnp.concatenate([before, x, after], axis=dim)
    return x


def network_solve(reference_date, secondary_date):
    date_index = jnp.arange(DATES, dtype=jnp.int32)
    signed = (secondary_date[:, None] == date_index[None, :]).astype(jnp.float32) - (
        reference_date[:, None] == date_index[None, :]
    ).astype(jnp.float32)
    design = signed[:, 1:]
    normal_matrix = jnp.dot(
        design.T, design, precision=lax.Precision.HIGHEST, preferred_element_type=jnp.float32
    )
    normal_matrix = normal_matrix + damping * jnp.eye(DATES - 1, dtype=jnp.float32)
    factor = jnp.linalg.cholesky(normal_matrix)
    inverse = jax.scipy.linalg.cho_solve((factor, True), design.T)
    return (design, inverse)


def pool_looks(values):
    group_size = values.shape[0]
    look_rows = values.shape[1] // AZ_LOOKS
    look_cols = values.shape[2] // RG_LOOKS
    return values.reshape(group_size, look_rows, AZ_LOOKS, look_cols, RG_LOOKS).sum(axis=(2, 4))


def window_coherence(padded, window_rows, window_cols, look_shape):
    total = jnp.zeros(look_shape, jnp.float32)
    zero_index = jnp.zeros((), jnp.int32)
    for offset_index in range(OFFSETS):
        start_row = HALF_WIN + window_rows[offset_index]
        start_col = COL_REACH + window_cols[offset_index]
        total = total + lax.dynamic_slice(
            padded, (zero_index, zero_index, start_row, start_col), look_shape
        )
    return jnp.sqrt(total[0] * total[0] + total[1] * total[1]) / total[2]


def invert_tile(tiled, design, inverse):
    flat_phase = tiled.reshape(tiled.shape[0], -1)
    solution = jnp.dot(
        inverse, flat_phase, precision=lax.Precision.HIGHEST, preferred_element_type=jnp.float32
    )
    fitted = jnp.dot(
        design, solution, precision=lax.Precision.HIGHEST, preferred_element_type=jnp.float32
    )
    return (
        (flat_phase - fitted).reshape(tiled.shape),
        solution.reshape(DATES - 1, tiled.shape[1], tiled.shape[2]),
    )


def local(phase_samples, sample_weights, reference_date, secondary_date, window_rows, window_cols):
    design, inverse = network_solve(reference_date, secondary_date)
    phase_float = phase_samples.astype(jnp.float32)
    weight_float = sample_weights.astype(jnp.float32)
    look_weight = pool_looks(weight_float)
    look_phase = pool_looks(weight_float * phase_float)
    look_cos = pool_looks(weight_float * jnp.cos(phase_float))
    look_sin = pool_looks(weight_float * jnp.sin(phase_float))
    multilooked = look_phase / look_weight
    group_size, look_rows, look_cols = multilooked.shape
    stacked = jnp.stack([look_cos, look_sin, look_weight])
    with_rims = padded_2(stacked, (("rows", 2),), HALF_WIN)
    padded = jnp.pad(with_rims, ((0, 0), (0, 0), (0, 0), (COL_REACH, COL_REACH)))
    coherence = window_coherence(padded, window_rows, window_cols, stacked.shape)
    ifg_count = lax.axis_size("ifg")
    row_count = lax.axis_size("rows")
    tile_cols = look_cols // (ifg_count * row_count)
    moved = lax.all_to_all(
        multilooked[None], ("ifg", "rows"), split_axis=3, concat_axis=0, tiled=True
    )
    tiled = moved.reshape(ifg_count, row_count, group_size, look_rows, tile_cols)
    tiled = tiled.transpose(0, 2, 1, 3, 4).reshape(
        ifg_count * group_size, row_count * look_rows, tile_cols
    )
    residual_tile, displacement = invert_tile(tiled, design, inverse)
    outgoing = residual_tile.reshape(ifg_count, group_size, row_count, look_rows, tile_cols)
    outgoing = outgoing.transpose(0, 2, 1, 3, 4).reshape(
        ifg_count * row_count, group_size, look_rows, tile_cols
    )
    residual = lax.all_to_all(outgoing, ("ifg", "rows"), split_axis=0, concat_axis=3, tiled=True)[0]
    return (coherence, residual, displacement)


def solution(mesh):
    placed = (P("ifg", "rows", None), P("ifg", "rows", None), P(), P(), P(), P())
    return jax.shard_map(
        local,
        mesh=mesh,
        in_specs=placed,
        out_specs=(P("ifg", "rows", None), P("ifg", "rows", None), P(None, None, ("ifg", "rows"))),
        check_vma=False,
    )
```

profile of v0, /device:TPU:6, one launch (start us, length us, event | category | flops | bytes accessed | tf_op | source)
XLA Modules:
  0.0 873.0 jit_solution(109876593809350029)
XLA Ops:
  0.6 395.3 %fusion.2 = (f32[75,32768]{1,0:T(8,128)}, f32[75,32768]{1,0:T(8,128)}, f32[75,32768]{1,0:T(8,128)}, f32[75,32768]{1,0:T(8,128)}) fusion(bf16[75,2,32768]{2,1,0:T(2,128)(2,1)} %param.6, bf16[75,2,32768]{2,1,0:T(2,128)(2,1)} %param.7), kind=kLoop, calls=%fused_computation.10 | loop fusion | flops 34406400 | bytes 58982400 | tf_op jit(solution)/shard_map/reduce_sum | solution.py:49
  396.0 14.1 %copy.41 = f32[75,32768]{0,1:T(8,128)} copy(f32[75,32768]{1,0:T(8,128)} %get-tuple-element.35) | data formatting | bytes 19660800 | tf_op jit(solution)/shard_map/reduce_sum | solution.py:49
  410.0 14.1 %copy.36 = f32[75,32768]{0,1:T(8,128)} copy(f32[75,32768]{1,0:T(8,128)} %get-tuple-element.38) | data formatting | bytes 19660800 | tf_op jit(solution)/shard_map/reduce_sum | solution.py:49
  424.1 14.1 %copy.35 = f32[75,32768]{0,1:T(8,128)} copy(f32[75,32768]{1,0:T(8,128)} %get-tuple-element.36) | data formatting | bytes 19660800 | tf_op jit(solution)/shard_map/reduce_sum | solution.py:49
  438.2 25.3 %bitcast_reduce_fusion.2 = f32[75,4096]{0,1:T(8,128)} fusion(f32[75,32768]{0,1:T(8,128)} %copy.35), kind=kLoop, calls=%fused_computation.18 | loop fusion | flops 2150400 | bytes 11059200 | tf_op jit(solution)/shard_map/reduce_sum | solution.py:49
  463.5 14.1 %copy.34 = f32[75,32768]{0,1:T(8,128)} copy(f32[75,32768]{1,0:T(8,128)} %get-tuple-element.37) | data formatting | bytes 19660800 | tf_op jit(solution)/shard_map/reduce_sum | solution.py:49
  477.6 23.8 %bitcast_reduce_fusion.3 = f32[75,4096]{0,1:T(8,128)S(1)} fusion(f32[75,32768]{0,1:T(8,128)} %copy.34), kind=kLoop, calls=%fused_computation.19 | loop fusion | flops 2150400 | bytes 11059200 | tf_op jit(solution)/shard_map/reduce_sum | solution.py:49
  501.4 27.8 %bitcast_reduce_fusion = (f32[75,4096]{0,1:T(8,128)}, f32[75,4096]{0,1:T(8,128)S(1)}) fusion(f32[75,32768]{0,1:T(8,128)} %copy.41, f32[75,32768]{0,1:T(8,128)} %copy.36), kind=kLoop, calls=%fused_computation.16 | loop fusion | flops 4300800 | bytes 22118400 | tf_op jit(solution)/shard_map/reduce_sum | solution.py:49
  532.5 9.7 %copy.37 = f32[3,75,1,4096]{3,2,1,0:T(1,128)} copy(f32[3,75,1,4096]{1,3,2,0:T(8,128)} %pad_maximum_fusion) | data formatting | bytes 7372800 | tf_op jit(solution)/shard_map/stack | solution.py:88
  542.3 9.0 %collective-permute-start.1 = (f32[3,75,1,4096]{3,2,1,0:T(1,128)}, f32[3,75,1,4096]{3,2,1,0:T(1,128)}, u32[]{:S(2)}, u32[]{:S(2)}) collective-permute-start(f32[3,75,1,4096]{3,2,1,0:T(1,128)} %copy.37), channel_id=1, source_target_pairs={{1,0},{2,1},{3,2},{4,3},{5,4},{6,5},{7,6},{8,7},{9,8},{10,9},{11,1... | collective-permute-start | bytes 11059208 | tf_op jit(solution)/shard_map/ppermute | solution.py:25
  556.4 10.9 %all-to-all-start = ((f32[1,75,1,4096]{1,2,0,3:T(1,128)}), f32[1,75,1,4096]{1,2,0,3:T(1,128)}, u32[]{:S(2)}, u32[]{:S(2)}) async-start(f32[1,75,1,4096]{1,2,0,3:T(1,128)} %bitcast.116), calls=%async_computation | async-start | bytes 4194304 | tf_op jit(solution)/shard_map/all_to_all | solution.py:95
  567.9 11.7 %cholesky.50 = f32[128,128]{1,0:T(8,128)S(1)} custom-call(f32[128,128]{1,0:T(8,128)S(1)} %cholesky.121), custom_call_target="Cholesky" | custom-call | tf_op jit(solution)/shard_map/jit(cholesky)/cholesky | solution.py:40
  579.7 9.8 %custom-call.18 = f32[1,128,128]{1,2,0:T(8,128)S(1)} custom-call(f32[1,128,128]{2,1,0:T(8,128)S(1)} %get-tuple-element.40), custom_call_target="InvertDiagBlocksLowerTriangular" | custom-call | tf_op jit(solution)/shard_map/jit(cholesky)/cholesky | solution.py:40
  595.4 19.9 %custom-call.19 = f32[2,128,128]{1,2,0:T(8,128)S(1)} custom-call(f32[2,128,128]{2,1,0:T(8,128)S(1)} %pad_maximum_fusion.1), custom_call_target="InvertDiagBlocksLowerTriangular" | custom-call | tf_op jit(solution)/shard_map/jit(_cho_solve)/triangular_solve | solution.py:41
  617.5 118.1 %all-to-all-done = f32[1,75,1,4096]{1,2,0,3:T(1,128)} async-done(((f32[1,75,1,4096]{1,2,0,3:T(1,128)}), f32[1,75,1,4096]{1,2,0,3:T(1,128)}, u32[]{:S(2)}, u32[]{:S(2)}) %all-to-all-start) | async-done | bytes 1228832 | tf_op jit(solution)/shard_map/all_to_all | solution.py:95
  735.6 4.7 copy.43
  746.4 3.8 fusion.7
  750.2 3.5 convolution_subtract_fusion
  763.4 17.4 %all-to-all-start.1 = ((f32[128,75,1,32]{1,3,2,0:T(8,128)}), f32[128,75,1,32]{1,3,2,0:T(8,128)}, u32[]{:S(2)}, u32[]{:S(2)}) async-start(f32[128,75,1,32]{1,3,2,0:T(8,128)} %bitcast.118), calls=%async_computation.1 | async-start | bytes 4194304 | tf_op jit(solution)/shard_map/all_to_all | solution.py:107
  808.6 4.0 copy.52
  812.6 9.6 %copy.40 = f32[3,75,1,4096]{1,3,2,0:T(8,128)} copy(f32[3,75,1,4096]{3,2,1,0:T(1,128)} %collective-permute-done.1) | data formatting | bytes 7372800 | tf_op jit(solution)/shard_map/ppermute | solution.py:25
  822.2 9.6 %copy.39 = f32[3,75,1,4096]{1,3,2,0:T(8,128)} copy(f32[3,75,1,4096]{3,2,1,0:T(1,128)} %collective-permute-done) | data formatting | bytes 7372800 | tf_op jit(solution)/shard_map/ppermute | solution.py:24
  831.9 15.4 %select_maximum_fusion = f32[3,75,3,4104]{1,3,2,0:T(8,128)} fusion(f32[3,75,1,4096]{1,3,2,0:T(8,128)} %copy.40, f32[3,75,1,4096]{1,3,2,0:T(8,128)} %copy.39, f32[1,75,1,4096]{1,3,2,0:T(8,128)S(1)} %bitcast.111, f32[1,75,1,4096]{1,3,2,0:T(8,128)} %bitcast.112, f32[1,75,1,4096]{1,3,2,0:T(8,128)} %bitcast.115), kind=kLoop, calls=%fused_computation.11 | loop fusion | flops 33242400 | bytes 22140000 | tf_op jit(solution)/shard_map/concatenate | solution.py:26
  847.3 22.3 %dynamic-slice_add_fusion = f32[3,75,1,4096]{1,3,2,0:T(8,128)S(1)} fusion(f32[3,75,3,4104]{1,3,2,0:T(8,128)} %select_maximum_fusion, s32[]{:T(128)S(6)} %select_n.74, s32[]{:T(128)S(6)} %select_n.75, s32[]{:T(128)S(6)} %select_n.72, s32[]{:T(128)S(6)} %select_n.73, s32[]{:T(128)S(6)} %select_n.70, s32[]{:T(128)S(6)} %select_n.71, s32[]{:T(128)S(6)} %select_n.68, ...), kind=kLoop, calls=%fused_computation.21 | loop fusion | flops 7372800 | bytes 36864072 | tf_op jit(solution)/shard_map/add | solution.py:58
  (54 shorter events, 39.6 us)
Async XLA Ops:
  501.4 27.8 %copy-start.1 = (f32[75,4096]{0,1:T(8,128)}, f32[75,4096]{0,1:T(8,128)S(1)}, u32[]{:S(2)}) copy-start(f32[75,4096]{0,1:T(8,128)S(1)} %bitcast_reduce_fusion.3) | copy-start | bytes 3686404
  501.4 27.8 %copy-start = (f32[75,4096]{0,1:T(8,128)S(1)}, f32[75,4096]{0,1:T(8,128)}, u32[]{:S(2)}) copy-start(f32[75,4096]{0,1:T(8,128)} %bitcast_reduce_fusion.2) | copy-start | bytes 3686404
  542.3 25.0 %copy-start.4 = (s32[300]{0:T(512)S(1)}, s32[300]{0:T(512)}, u32[]{:S(2)}) copy-start(s32[300]{0:T(512)} %param.8) | copy-start | bytes 3604
  542.3 25.0 %copy-start.5 = (s32[300]{0:T(512)S(1)}, s32[300]{0:T(512)}, u32[]{:S(2)}) copy-start(s32[300]{0:T(512)} %param.9) | copy-start | bytes 3604
  542.3 270.3 %collective-permute-start.1 = (f32[3,75,1,4096]{3,2,1,0:T(1,128)}, f32[3,75,1,4096]{3,2,1,0:T(1,128)}, u32[]{:S(2)}, u32[]{:S(2)}) collective-permute-start(f32[3,75,1,4096]{3,2,1,0:T(1,128)} %copy.37), channel_id=1, source_target_pairs={{1,0},{2,1},{3,2},{4,3},{5,4},{6,5},{7,6},{8,7},{9,8},{10,9},{11,1... | collective-permute-start | bytes 11059208 | tf_op jit(solution)/shard_map/ppermute | solution.py:25
  551.3 271.0 %collective-permute-start = (f32[3,75,1,4096]{3,2,1,0:T(1,128)}, f32[3,75,1,4096]{3,2,1,0:T(1,128)}, u32[]{:S(2)}, u32[]{:S(2)}) collective-permute-start(f32[3,75,1,4096]{3,2,1,0:T(1,128)} %copy.37), channel_id=1, source_target_pairs={{0,1},{1,2},{2,3},{3,4},{4,5},{5,6},{6,7},{7,8},{8,9},{9,10},{10,1... | collective-permute-start | bytes 11059208 | tf_op jit(solution)/shard_map/ppermute | solution.py:24
  556.4 179.2 %all-to-all-start = ((f32[1,75,1,4096]{1,2,0,3:T(1,128)}), f32[1,75,1,4096]{1,2,0,3:T(1,128)}, u32[]{:S(2)}, u32[]{:S(2)}) async-start(f32[1,75,1,4096]{1,2,0,3:T(1,128)} %bitcast.116), calls=%async_computation | async-start | bytes 4194304 | tf_op jit(solution)/shard_map/all_to_all | solution.py:95
  756.7 24.1 %copy-start.2 = (s32[9]{0:T(128)S(1)}, s32[9]{0:T(128)}, u32[]{:S(2)}) copy-start(s32[9]{0:T(128)} %param.10) | copy-start | bytes 112
  756.7 27.2 %copy-start.3 = (s32[9]{0:T(128)S(1)}, s32[9]{0:T(128)}, u32[]{:S(2)}) copy-start(s32[9]{0:T(128)} %param.11) | copy-start | bytes 112
  763.4 45.2 %all-to-all-start.1 = ((f32[128,75,1,32]{1,3,2,0:T(8,128)}), f32[128,75,1,32]{1,3,2,0:T(8,128)}, u32[]{:S(2)}, u32[]{:S(2)}) async-start(f32[128,75,1,32]{1,3,2,0:T(8,128)} %bitcast.118), calls=%async_computation.1 | async-start | bytes 4194304 | tf_op jit(solution)/shard_map/all_to_all | solution.py:107
where the time goes:
time: 887 us; the launch traced here: 873 us
  other arithmetic  563 us (63%)
  waiting for transfers between devices  121 us (14%)
  local copies, waits for them, and re-layouts  115 us (13%)
  starting transfers between devices  39.2 us (4%)
  between operations  25.4 us (3%)
  matrix products  10.1 us (1%)
    reduce_sum x4, other arithmetic, pool_looks(): values.reshape(group_size, look_rows, AZ_LOOKS, look_cols, RG_LOOKS)  472 us
    all_to_all x1, waiting for transfers between devices, local(): lax.all_to_all(multilooked[None], ('ifg', 'rows'), split_axis=3, concat_a...  118 us
    reduce_sum x4, local copies, waits for them, and re-layouts, pool_looks(): values.reshape(group_size, look_rows, AZ_LOOKS, look_cols, RG_LOOKS)  56.3 us
    another operation x7, other arithmetic, network_solve(): factor = jnp.linalg.cholesky(normal_matrix)  25.7 us
    add x1, other arithmetic, window_coherence(): total + lax.dynamic_slice(padded, (zero_index, zero_index, start_row, sta...  22.3 us
    another operation x6, other arithmetic, network_solve(): inverse = jax.scipy.linalg.cho_solve((factor, True), design.T)  20 us
  transfers between devices with their start and end apart: 4, of which 2 were waited for; matrix products, arithmetic and copies ran while one was open for 11% of the time, Pallas kernels for 0%

commit v1 on v0

v1 whole, which is shorter than its diff:
```python
import math

import jax
import jax.numpy as jnp
from jax import lax
from jax.experimental import pallas as pl
from jax.experimental.pallas import tpu as pltpu
from jax.sharding import PartitionSpec as P

DATES = 160
AZ_LOOKS = 2
RG_LOOKS = 8
COL_REACH = 4
OFFSETS = 9
LANES = 128

damping = 0.25

SIN_QUARTER = (
    0.3535533845424652,
    -0.0036828448064625263,
    1.1508434909046628e-05,
    -1.7096880355893518e-08,
    1.4046378643550739e-11,
)
COS_QUARTER = (
    0.9999999403953552,
    -0.031249957159161568,
    0.00016275106463581324,
    -3.383578359716921e-07,
    3.553040917037009e-10,
)
SIN_SCALE = 2.0 * math.sqrt(2.0)

PIECES = 16
GROUP = 16


def network_solve(reference_date, secondary_date):
    date_index = jnp.arange(DATES, dtype=jnp.int32)
    signed = (secondary_date[:, None] == date_index[None, :]).astype(jnp.float32) - (
        reference_date[:, None] == date_index[None, :]
    ).astype(jnp.float32)
    design = signed[:, 1:]
    normal_matrix = jnp.dot(
        design.T, design, precision=lax.Precision.HIGHEST, preferred_element_type=jnp.float32
    )
    normal_matrix = normal_matrix + damping * jnp.eye(DATES - 1, dtype=jnp.float32)
    factor = jnp.linalg.cholesky(normal_matrix)
    inverse = jax.scipy.linalg.cho_solve((factor, True), design.T)
    return (design, inverse)


def pooling_matrix():
    row = lax.broadcasted_iota(jnp.int32, (LANES * RG_LOOKS, LANES), 0)
    col = lax.broadcasted_iota(jnp.int32, (LANES * RG_LOOKS, LANES), 1)
    return (row // RG_LOOKS == col).astype(jnp.bfloat16)


def horner(coefficients, z):
    total = coefficients[-1] * z + coefficients[-2]
    for c in coefficients[-3::-1]:
        total = total * z + c
    return total


def regroup(ref, held, rows):
    held[...] = ref[rows].astype(jnp.float32).reshape(GROUP * PIECES, LANES)


def piece(held, q):
    return held[pl.ds(q, GROUP, stride=PIECES), :]


def split_store(high, low, rows, c, value):
    top = value.astype(jnp.bfloat16)
    high[rows, c * LANES : (c + 1) * LANES] = top
    low[rows, c * LANES : (c + 1) * LANES] = (value - top.astype(jnp.float32)).astype(jnp.bfloat16)


def pooled(high, low, pool):
    return jnp.dot(high[...], pool[...], preferred_element_type=jnp.float32) + jnp.dot(
        low[...], pool[...], preferred_element_type=jnp.float32
    )


def phase_kernel(phase, weight, pool, look_weight, looked, p_held, w_held, wh, wl, ph, plo):
    block = phase.shape[0]

    def step(g, carry):
        rows = pl.ds(pl.multiple_of(g * GROUP, GROUP), GROUP)
        regroup(phase, p_held, rows)
        regroup(weight, w_held, rows)
        for c in range(RG_LOOKS):
            w0, w1 = piece(w_held, 2 * c), piece(w_held, 2 * c + 1)
            p0, p1 = piece(p_held, 2 * c), piece(p_held, 2 * c + 1)
            split_store(wh, wl, rows, c, w0 + w1)
            split_store(ph, plo, rows, c, w0 * p0 + w1 * p1)
        return carry

    lax.fori_loop(0, block // GROUP, step, 0)
    total = pooled(wh, wl, pool)
    look_weight[...] = total
    mean = pooled(ph, plo, pool) / total
    looked[...] = jnp.transpose(mean.reshape(block // 32, 4, 8, LANES), (1, 0, 2, 3))


def phase_looks(phase, weight, pool):
    rows = phase.shape[0]
    block = 480
    return pl.pallas_call(
        phase_kernel,
        grid=(rows // block,),
        in_specs=[
            pl.BlockSpec((block, PIECES, LANES), lambda i: (i, 0, 0)),
            pl.BlockSpec((block, PIECES, LANES), lambda i: (i, 0, 0)),
            pl.BlockSpec(pool.shape, lambda i: (0, 0)),
        ],
        out_specs=[
            pl.BlockSpec((block, LANES), lambda i: (i, 0)),
            pl.BlockSpec((4, block // 32, 8, LANES), lambda i: (0, i, 0, 0)),
        ],
        out_shape=[
            jax.ShapeDtypeStruct((rows, LANES), jnp.float32),
            jax.ShapeDtypeStruct((4, rows // 32, 8, LANES), jnp.float32),
        ],
        scratch_shapes=[pltpu.VMEM((GROUP * PIECES, LANES), jnp.float32)] * 2
        + [pltpu.VMEM((block, RG_LOOKS * LANES), jnp.bfloat16)] * 4,
        compiler_params=pltpu.CompilerParams(vmem_limit_bytes=48 * 1024 * 1024),
        cost_estimate=pl.CostEstimate(
            flops=2 * rows * 2048 * 128, bytes_accessed=2 * rows * 4096 + rows * 1024, transcendentals=0
        ),
        name="phase_looks",
    )(phase, weight, pool)


def wave_kernel(start, phase, weight, pool, look_weight, out, p_held, w_held, sh, sl, qh, ql):
    block = phase.shape[0]

    def step(g, carry):
        rows = pl.ds(pl.multiple_of(g * GROUP, GROUP), GROUP)
        regroup(phase, p_held, rows)
        regroup(weight, w_held, rows)
        for c in range(RG_LOOKS):
            s_sum = q_sum = None
            for a in range(AZ_LOOKS):
                x = piece(p_held, 2 * c + a)
                w = piece(w_held, 2 * c + a)
                z = x * x
                s = x * horner(SIN_QUARTER, z)
                k = horner(COS_QUARTER, z)
                half = s * k
                sine = w * (half * (1.0 - s * s))
                versed = w * (half * half)
                s_sum = sine if s_sum is None else s_sum + sine
                q_sum = versed if q_sum is None else q_sum + versed
            split_store(sh, sl, rows, c, s_sum)
            split_store(qh, ql, rows, c, q_sum)
        return carry

    lax.fori_loop(0, block // GROUP, step, 0)
    out[0] = look_weight[...] - 4.0 * pooled(qh, ql, pool)
    out[1] = SIN_SCALE * pooled(sh, sl, pool)


def wave_looks(start, count, phase, weight, pool, look_weight):
    block = 304
    element = pl.Element
    return pl.pallas_call(
        wave_kernel,
        grid_spec=pltpu.PrefetchScalarGridSpec(
            num_scalar_prefetch=1,
            grid=(count // block,),
            in_specs=[
                pl.BlockSpec(
                    (element(block), element(PIECES), element(LANES)),
                    lambda i, s: (pl.multiple_of(s[0] + i * block, 16), 0, 0),
                ),
                pl.BlockSpec(
                    (element(block), element(PIECES), element(LANES)),
                    lambda i, s: (pl.multiple_of(s[0] + i * block, 16), 0, 0),
                ),
                pl.BlockSpec(pool.shape, lambda i, s: (0, 0)),
                pl.BlockSpec(
                    (element(block), element(LANES)),
                    lambda i, s: (pl.multiple_of(s[0] + i * block, 16), 0),
                ),
            ],
            out_specs=pl.BlockSpec((2, block, LANES), lambda i, s: (0, i, 0)),
            scratch_shapes=[pltpu.VMEM((GROUP * PIECES, LANES), jnp.float32)] * 2
            + [pltpu.VMEM((block, RG_LOOKS * LANES), jnp.bfloat16)] * 4,
        ),
        out_shape=jax.ShapeDtypeStruct((2, count, LANES), jnp.float32),
        compiler_params=pltpu.CompilerParams(vmem_limit_bytes=48 * 1024 * 1024),
        cost_estimate=pl.CostEstimate(
            flops=40 * count * 2048, bytes_accessed=2 * count * 4096 + count * 1024, transcendentals=0
        ),
        name="wave_looks",
    )(start, phase, weight, pool, look_weight)


def window_kernel(
    row_off, col_off, flip, own_cs, own_w, mate_cs, mate_w, near_cs, near_w, far_cs, far_w,
    own_out, mate_out, held, cre, cim, sems,
):
    copies = []
    for i, (cs, w) in enumerate(
        ((near_cs, near_w), (own_cs, own_w), (mate_cs, mate_w), (far_cs, far_w))
    ):
        copies.append(pltpu.make_async_copy(cs, held.at[i, pl.ds(0, 2)], sems.at[i, 0]))
        copies.append(pltpu.make_async_copy(w, held.at[i, 2], sems.at[i, 1]))
    for c in copies:
        c.start()
    for c in copies:
        c.wait()
    cols = held.shape[2] // 32
    lane = lax.broadcasted_iota(jnp.int32, (8, LANES), 1)
    shifts = [col_off[k] for k in range(OFFSETS)]
    rolls = [lax.rem(LANES - d, LANES) for d in shifts]
    groups = (cols + 7) // 8

    def one(t, carry):
        side, g = t // groups, lax.rem(t, groups)
        first = jnp.minimum(g * 8, cols - 8) * 32
        sources = [1 + side + row_off[k] * flip[0] for k in range(OFFSETS)]
        after = [lane + d >= LANES for d in shifts]
        before = [lane + d < 0 for d in shifts]
        for quantity in range(3):
            def rolled(c):
                if c < 0 or c > 31:
                    return [jnp.zeros((8, LANES), jnp.float32)] * OFFSETS
                out = []
                for k in range(OFFSETS):
                    v = held[sources[k], quantity, pl.ds(first + c, 8, stride=32), :]
                    out.append(pltpu.roll(v, rolls[k], 1))
                return out

            last, now = rolled(-1), rolled(0)
            for c in range(32):
                following = rolled(c + 1)
                total = None
                for k in range(OFFSETS):
                    term = jnp.where(after[k], following[k], jnp.where(before[k], last[k], now[k]))
                    total = term if total is None else total + term
                last, now = now, following
                if quantity == 0:
                    cre[c] = total
                elif quantity == 1:
                    cim[c] = total
                else:
                    re, im = cre[c], cim[c]
                    value = jnp.sqrt(re * re + im * im) / total
                    @pl.when(side == 0)
                    def _():
                        own_out[pl.ds(first + c, 8, stride=32), :] = value
                    @pl.when(side == 1)
                    def _():
                        mate_out[pl.ds(first + c, 8, stride=32), :] = value
        return carry

    lax.fori_loop(0, 2 * groups, one, 0)


def window_coherence(row_off, col_off, flip, own_cs, own_w, mate_cs, mate_w, near_cs, near_w, far_cs, far_w):
    rows = own_w.shape[0]
    smem = pl.BlockSpec(memory_space=pltpu.SMEM)
    hbm = pl.BlockSpec(memory_space=pl.ANY)
    vmem = pl.BlockSpec(memory_space=pltpu.VMEM)
    shape = jax.ShapeDtypeStruct((rows, LANES), jnp.float32)
    return pl.pallas_call(
        window_kernel,
        in_specs=[smem] * 3 + [hbm] * 8,
        out_specs=[vmem, vmem],
        out_shape=[shape, shape],
        scratch_shapes=[
            pltpu.VMEM((4, 3, rows, LANES), jnp.float32),
            pltpu.VMEM((32, 8, LANES), jnp.float32),
            pltpu.VMEM((32, 8, LANES), jnp.float32),
            pltpu.SemaphoreType.DMA((4, 2)),
        ],
        compiler_params=pltpu.CompilerParams(vmem_limit_bytes=32 * 1024 * 1024),
        cost_estimate=pl.CostEstimate(
            flops=200 * rows * LANES, bytes_accessed=14 * rows * LANES * 4, transcendentals=0
        ),
        name="window_coherence",
    )(row_off, col_off, flip, own_cs, own_w, mate_cs, mate_w, near_cs, near_w, far_cs, far_w)


def invert_kernel(looked, inverse, design, residual, history, flat):
    ifgs = design.shape[0]
    for j in range(8):
        flat[:, j * LANES : (j + 1) * LANES] = looked[pl.ds(j, ifgs, stride=8), :]
    phase = flat[...]
    solved = jnp.dot(
        inverse[...], phase, precision=lax.Precision.HIGHEST, preferred_element_type=jnp.float32
    )
    fitted = jnp.dot(
        design[...], solved, precision=lax.Precision.HIGHEST, preferred_element_type=jnp.float32
    )
    history[...] = jnp.transpose(solved)[:, : DATES - 1]
    rest = phase - fitted
    for j in range(8):
        residual[pl.ds(j, ifgs, stride=8), :] = rest[:, j * LANES : (j + 1) * LANES]


def invert(looked, inverse, design):
    ifgs = design.shape[0]
    vmem = pl.BlockSpec(memory_space=pltpu.VMEM)
    return pl.pallas_call(
        invert_kernel,
        in_specs=[vmem] * 3,
        out_specs=[vmem] * 2,
        out_shape=[
            jax.ShapeDtypeStruct(looked.shape, jnp.float32),
            jax.ShapeDtypeStruct((8 * LANES, DATES - 1), jnp.float32),
        ],
        scratch_shapes=[pltpu.VMEM((ifgs, 8 * LANES), jnp.float32)],
        compiler_params=pltpu.CompilerParams(vmem_limit_bytes=32 * 1024 * 1024),
        cost_estimate=pl.CostEstimate(
            flops=24 * ifgs * DATES * 1024, bytes_accessed=4 * 3 * ifgs * 1024, transcendentals=0
        ),
        name="invert",
    )(looked, inverse, design)


def tiles(samples):
    ifgs, az, cols = samples.shape
    split = samples.reshape(ifgs, az, cols // LANES, LANES).transpose(0, 2, 1, 3)
    return split.reshape(ifgs * cols // (LANES * RG_LOOKS), PIECES, LANES)


def local(phase_samples, sample_weights, reference_date, secondary_date, window_rows, window_cols):
    ifgs = phase_samples.shape[0]
    row_count = lax.axis_size("rows")
    odd = lax.rem(lax.axis_index("rows"), 2)
    share = (ifgs + 1) // 2
    rest = ifgs - share
    mates = [(r, r ^ 1) for r in range(row_count)]
    outward = [(r, r + 2 if r % 2 else r - 2) for r in range(row_count)]
    outward = [(s, d) for s, d in outward if 0 <= d < row_count]
    across = [(r, r - 2 if r % 2 else r + 2) for r in range(row_count)]
    across = [(s, d) for s, d in across if 0 <= d < row_count]

    phase = tiles(phase_samples)
    weight = tiles(sample_weights)
    pool = pooling_matrix()
    look_weight, looked = phase_looks(phase, weight, pool)
    moved = lax.all_to_all(looked, "ifg", split_axis=0, concat_axis=0, tiled=True)

    mine = rest * 32 * odd
    other = rest * 32 * (1 - odd)
    size = share * 32
    own_w = lax.dynamic_slice_in_dim(look_weight, mine, size)
    sent_w = lax.dynamic_slice_in_dim(look_weight, other, size)
    mate_w = lax.ppermute(sent_w, "rows", mates)
    sent_cs = wave_looks(other.reshape(1), size, phase, weight, pool, look_weight)
    mate_cs = lax.ppermute(sent_cs, "rows", mates)
    own_cs = wave_looks(mine.reshape(1), size, phase, weight, pool, look_weight)
    far_w = lax.ppermute(own_w, "rows", outward)
    far_cs = lax.ppermute(own_cs, "rows", outward)
    near_w = lax.ppermute(mate_w, "rows", across)
    near_cs = lax.ppermute(mate_cs, "rows", across)
    flip = (1 - 2 * odd).reshape(1)
    own_part, mate_part = window_coherence(
        window_rows, window_cols, flip, own_cs, own_w, mate_cs, mate_w, near_cs, near_w, far_cs, far_w
    )
    back = lax.ppermute(mate_part, "rows", mates)
    extra = (share - rest) * 32
    coherence = jnp.where(
        odd == 0,
        jnp.concatenate([own_part, back[extra:]]),
        jnp.concatenate([back, own_part[extra:]]),
    )

    design, inverse = network_solve(reference_date, secondary_date)
    tile_rows = moved.shape[0] * moved.shape[1] * moved.shape[2]
    residual, history = invert(moved.reshape(tile_rows, LANES), inverse, design)
    residual = lax.all_to_all(
        residual.reshape(moved.shape), "ifg", split_axis=0, concat_axis=0, tiled=True
    )
    residual = residual.transpose(1, 0, 2, 3)
    history = history.reshape(row_count, -1, DATES - 1)
    history = lax.all_to_all(history, "rows", split_axis=0, concat_axis=0, tiled=True)
    shape = (ifgs, 1, 32 * LANES)
    return (coherence.reshape(shape), residual.reshape(shape), history.transpose(2, 0, 1))


def solution(mesh):
    placed = (P("ifg", "rows", None), P("ifg", "rows", None), P(), P(), P(), P())
    return jax.shard_map(
        local,
        mesh=mesh,
        in_specs=placed,
        out_specs=(P("ifg", "rows", None), P("ifg", "rows", None), P(None, None, ("ifg", "rows"))),
        check_vma=False,
    )
```

time: 887 us -> 294 us (0.33); the launches traced: 873 us -> 293 us
  other arithmetic: 563 us -> 54.3 us
  Pallas kernels: 0 us -> 125 us
  local copies, waits for them, and re-layouts: 115 us -> 14.2 us
  waiting for transfers between devices: 121 us -> 52.9 us
  between operations: 25.4 us -> 2.28 us
    reduce_sum x4 -> x0, other arithmetic: 472 us -> none  [pool_looks(): values.reshape(group_size, look_rows, AZ_LOOKS, look_cols, RG_LOOKS)]
    pallas_call x0 -> x5, Pallas kernels: none -> 125 us  [the longest x1 57.4 us: window_coherence(): pl.pallas_call(window_kernel, in_specs=[smem] * 3 + [hbm] * 8, out_specs=...]
    all_to_all x2 -> x3, waiting for transfers between devices: 121 us -> 25.7 us  [the longest x1 25.7 us: local(): lax.all_to_all(history, 'rows', split_axis=0, concat_axis=0, tiled=True)]
    reduce_sum x4 -> x0, local copies, waits for them, and re-layouts: 56.3 us -> none  [pool_looks(): values.reshape(group_size, look_rows, AZ_LOOKS, look_cols, RG_LOOKS)]
    ppermute x2 -> x7, waiting for transfers between devices: 0.01 us -> 27.2 us  [the longest x1 14.6 us: local(): back = lax.ppermute(mate_part, 'rows', mates)]
    add x1 -> x0, other arithmetic: 22.3 us -> none  [window_coherence(): total + lax.dynamic_slice(padded, (zero_index, zero_index, start_row, sta...]
    another operation x4 -> x0, local copies, waits for them, and re-layouts: 19.3 us -> none  [the longest x1 9.74 us: local(): stacked = jnp.stack([look_cos, look_sin, look_weight])]
    ppermute x2 -> x0, local copies, waits for them, and re-layouts: 19.3 us -> none  [the longest x1 9.64 us: padded_2(): after = lax.ppermute(initial, axis, down)]
  transfers between devices with their start and end apart: 4 -> 10, of which waited for: 2 -> 3; matrix products, arithmetic and copies ran while one was open for 11% -> 23% of each run, Pallas kernels for 0% -> 27%
where the time goes in v1:
time: 294 us; the launch traced here: 293 us
  Pallas kernels  125 us (43%)
  other arithmetic  54.3 us (18%)
  waiting for transfers between devices  52.9 us (18%)
  starting transfers between devices  36.3 us (12%)
  local copies, waits for them, and re-layouts  14.2 us (5%)
  matrix products  8.32 us (3%)
    pallas_call x1, Pallas kernels, window_coherence(): pl.pallas_call(window_kernel, in_specs=[smem] * 3 + [hbm] * 8, out_specs=...  57.4 us
    pallas_call x2, Pallas kernels, wave_looks(): pl.pallas_call(wave_kernel, grid_spec=pltpu.PrefetchScalarGridSpec(num_sc...  39.1 us
    another operation x7, other arithmetic, network_solve(): factor = jnp.linalg.cholesky(normal_matrix)  27.4 us
    all_to_all x1, waiting for transfers between devices, local(): lax.all_to_all(history, 'rows', split_axis=0, concat_axis=0, tiled=True)  25.7 us
    pallas_call x1, Pallas kernels, phase_looks(): pl.pallas_call(phase_kernel, grid=(rows // block,), in_specs=[pl.BlockSpe...  24.7 us
    another operation x7, other arithmetic, network_solve(): inverse = jax.scipy.linalg.cho_solve((factor, True), design.T)  22.9 us
    ppermute x1, waiting for transfers between devices, local(): back = lax.ppermute(mate_part, 'rows', mates)  14.6 us
    ppermute x1, waiting for transfers between devices, local(): near_w = lax.ppermute(mate_w, 'rows', across)  12.6 us
  transfers between devices with their start and end apart: 10, of which 3 were waited for; matrix products, arithmetic and copies ran while one was open for 23% of the time, Pallas kernels for 27%

profile of v1, /device:TPU:6, one launch (start us, length us, event | category | flops | bytes accessed | tf_op | source)
XLA Modules:
  0.0 293.0 jit_solution(12507114448447624175)
XLA Ops:
  1.5 24.7 %phase_looks.1 = (f32[2400,128]{1,0:T(8,128)S(1)}, f32[4,75,8,128]{3,2,1,0:T(8,128)S(1)}) custom-call(bf16[2400,16,128]{2,1,0:T(8,128)(2,1)} %bitcast.56, bf16[2400,16,128]{2,1,0:T(8,128)(2,1)} %bitcast.59, bf16[1024,128]{1,0:T(8,128)(2,1)S(1)} %fusion.pool), custom_call_target="tpu_custom_call" | custom-call | flops 1258291200 | bytes 22118400 | tf_op jit(solution)/shard_map/phase_looks/pallas_call | solution.py:111
  27.3 19.9 %wave_looks.3 = f32[2,1216,128]{2,1,0:T(8,128)} custom-call(s32[1]{0:T(128)} %bitcast.12.start, bf16[2400,16,128]{2,1,0:T(8,128)(2,1)} %bitcast.57, bf16[2400,16,128]{2,1,0:T(8,128)(2,1)} %bitcast.60, bf16[1024,128]{1,0:T(8,128)(2,1)S(1)} %fusion.pool, f32[2400,128]{1,0:T(8,128)S(1)} %get-tuple-element.9.look_weight), custom_call_target="tpu_custom_call" | custom-call | flops 99614720 | bytes 11206656 | tf_op jit(solution)/shard_map/wave_looks/pallas_call | solution.py:169
  47.2 3.2 %collective-permute-start = (f32[2,1216,128]{2,1,0:T(8,128)}, f32[2,1216,128]{2,1,0:T(8,128)}, u32[]{:S(2)}, u32[]{:S(2)}) collective-permute-start(f32[2,1216,128]{2,1,0:T(8,128)} %wave_looks.3), channel_id=1, source_target_pairs={{0,1},{1,0},{2,3},{3,2},{4,5},{5,4},{6,7},{7,6},{8,9},{9,8},{10,11... | collective-permute-start | bytes 3735560 | tf_op jit(solution)/shard_map/ppermute | solution.py:357
  51.6 19.2 %wave_looks.2.own_cs = f32[2,1216,128]{2,1,0:T(8,128)S(1)} custom-call(s32[1]{0:T(128)} %bitcast.1.start, bf16[2400,16,128]{2,1,0:T(8,128)(2,1)} %bitcast.58, bf16[2400,16,128]{2,1,0:T(8,128)(2,1)} %bitcast.61, bf16[1024,128]{1,0:T(8,128)(2,1)S(1)} %fusion.pool, f32[2400,128]{1,0:T(8,128)S(1)} %get-tuple-element.9.look_weight), custom_call_target="tpu_custom_call" | custom-call | flops 99614720 | bytes 11206656 | tf_op jit(solution)/shard_map/wave_looks/pallas_call | solution.py:169
  70.8 6.2 %collective-permute-start.4 = (f32[2,1216,128]{2,1,0:T(8,128)S(1)}, f32[2,1216,128]{2,1,0:T(8,128)}, u32[]{:S(2)}, u32[]{:S(2)}) collective-permute-start(f32[2,1216,128]{2,1,0:T(8,128)S(1)} %wave_looks.2.own_cs), channel_id=1, source_target_pairs={{1,3},{2,0},{3,5},{4,2},{5,7},{6,4},{7,9},{8,6},{9,11},{10,8},{11,... | collective-permute-start | bytes 3735560 | tf_op jit(solution)/shard_map/ppermute | solution.py:360
  77.1 3.7 %all-to-all-start = ((f32[4,75,8,128]{3,2,1,0:T(8,128)}), f32[4,75,8,128]{3,2,1,0:T(8,128)S(1)}, u32[]{:S(2)}, u32[]{:S(2)}) async-start(f32[4,75,8,128]{3,2,1,0:T(8,128)} %copy-done), calls=%async_computation | async-start | bytes 2457600 | tf_op jit(solution)/shard_map/all_to_all | solution.py:348
  81.7 1.6 fusion.8
  83.3 1.7 copy.17
  86.7 11.7 %cholesky.50 = f32[128,128]{1,0:T(8,128)S(1)} custom-call(f32[128,128]{1,0:T(8,128)S(1)} %cholesky.121), custom_call_target="Cholesky" | custom-call | tf_op jit(solution)/shard_map/jit(cholesky)/cholesky | solution.py:49
  99.6 9.8 %custom-call.18 = f32[1,128,128]{1,2,0:T(8,128)S(1)} custom-call(f32[1,128,128]{2,1,0:T(8,128)S(1)} %get-tuple-element.44), custom_call_target="InvertDiagBlocksLowerTriangular" | custom-call | tf_op jit(solution)/shard_map/jit(cholesky)/cholesky | solution.py:49
  111.8 2.8 cholesky.108
  120.8 20.5 %custom-call.19 = f32[2,128,128]{1,2,0:T(8,128)S(1)} custom-call(f32[2,128,128]{2,1,0:T(8,128)} %pad_maximum_fusion.1), custom_call_target="InvertDiagBlocksLowerTriangular" | custom-call | tf_op jit(solution)/shard_map/jit(_cho_solve)/triangular_solve | solution.py:50
  145.4 2.1 collective-permute-start.2
  149.6 3.5 %invert.1 = (f32[2400,128]{1,0:T(8,128)}, f32[1024,159]{1,0:T(8,128)S(1)}) custom-call(f32[2400,128]{1,0:T(8,128)S(1)} %bitcast.54, f32[159,300]{1,0:T(8,128)S(1)} %copy-done.4, f32[300,159]{1,0:T(8,128)S(1)} %get-tuple-element.47.design), custom_call_target="tpu_custom_call" | custom-call | flops 1179648000 | bytes 3686400 | tf_op jit(solution)/shard_map/invert/pallas_call | solution.py:309
  154.0 9.4 %all-to-all-start.2 = ((f32[32,32,159]{2,1,0:T(8,128)}), f32[32,32,159]{2,1,0:T(8,128)}, u32[]{:S(2)}, u32[]{:S(2)}) async-start(f32[32,32,159]{2,1,0:T(8,128)} %bitcast.55), calls=%async_computation.2 | async-start | bytes 2097152 | tf_op jit(solution)/shard_map/all_to_all | solution.py:383
  163.4 4.9 %collective-permute-start.5 = (f32[1216,128]{1,0:T(8,128)S(1)}, f32[1216,128]{1,0:T(8,128)S(1)}, u32[]{:S(2)}, u32[]{:S(2)}) collective-permute-start(f32[1216,128]{1,0:T(8,128)S(1)} %get-tuple-element.42.own_w), channel_id=1, source_target_pairs={{1,3},{2,0},{3,5},{4,2},{5,7},{6,4},{7,9},{8,6},{9,11},{10,8},{11,... | collective-permute-start | bytes 1867784 | tf_op jit(solution)/shard_map/ppermute | solution.py:359
  168.3 1.9 collective-permute-start.3
  170.2 25.7 %all-to-all-done.2 = f32[32,32,159]{2,1,0:T(8,128)} async-done(((f32[32,32,159]{2,1,0:T(8,128)}), f32[32,32,159]{2,1,0:T(8,128)}, u32[]{:S(2)}, u32[]{:S(2)}) %all-to-all-start.2) | async-done | bytes 651296 | tf_op jit(solution)/shard_map/all_to_all | solution.py:383
  195.9 4.4 %all-to-all-start.1 = ((f32[4,75,8,128]{3,2,1,0:T(8,128)}), f32[4,75,8,128]{3,2,1,0:T(8,128)}, u32[]{:S(2)}, u32[]{:S(2)}) async-start(f32[4,75,8,128]{3,2,1,0:T(8,128)} %bitcast.23), calls=%async_computation.1 | async-start | bytes 2457600 | tf_op jit(solution)/shard_map/all_to_all | solution.py:378
  200.3 12.6 %collective-permute-done.3.near_w = f32[1216,128]{1,0:T(8,128)S(1)} collective-permute-done((f32[1216,128]{1,0:T(8,128)}, f32[1216,128]{1,0:T(8,128)S(1)}, u32[]{:S(2)}, u32[]{:S(2)}) %collective-permute-start.3) | collective-permute-done | bytes 622624 | tf_op jit(solution)/shard_map/ppermute | solution.py:361
  214.9 57.4 %window_coherence.1 = (f32[1216,128]{1,0:T(8,128)S(1)}, f32[1216,128]{1,0:T(8,128)}) custom-call(s32[9]{0:T(128)S(1)} %copy-done.5, s32[9]{0:T(128)S(1)} %copy-done.6, s32[1]{0:T(128)} %bitcast.flip, f32[2,1216,128]{2,1,0:T(8,128)S(1)} %wave_looks.2.own_cs, f32[1216,128]{1,0:T(8,128)S(1)} %get-tuple-element.42.own_w, ...), custom_call_target="tpu_custom_call" | custom-call | flops 31129600 | bytes 8716288 | tf_op jit(solution)/shard_map/window_coherence/pallas_call | solution.py:270
  272.4 2.5 copy.19
  274.9 14.6 %collective-permute-done.6 = f32[1216,128]{1,0:T(8,128)S(1)} collective-permute-done((f32[1216,128]{1,0:T(8,128)}, f32[1216,128]{1,0:T(8,128)S(1)}, u32[]{:S(2)}, u32[]{:S(2)}) %collective-permute-start.6) | collective-permute-done | bytes 622624 | tf_op jit(solution)/shard_map/ppermute | solution.py:367
  290.7 2.3 copy.25
  (61 shorter events, 24.4 us)
Async XLA Ops:
  26.3 1.0 copy-start
  47.2 98.2 %collective-permute-start = (f32[2,1216,128]{2,1,0:T(8,128)}, f32[2,1216,128]{2,1,0:T(8,128)}, u32[]{:S(2)}, u32[]{:S(2)}) collective-permute-start(f32[2,1216,128]{2,1,0:T(8,128)} %wave_looks.3), channel_id=1, source_target_pairs={{0,1},{1,0},{2,3},{3,2},{4,5},{5,4},{6,7},{7,6},{8,9},{9,8},{10,11... | collective-permute-start | bytes 3735560 | tf_op jit(solution)/shard_map/ppermute | solution.py:357
  51.3 117.0 %collective-permute-start.1 = (f32[1216,128]{1,0:T(8,128)}, f32[1216,128]{1,0:T(8,128)}, u32[]{:S(2)}, u32[]{:S(2)}) collective-permute-start(f32[1216,128]{1,0:T(8,128)} %get-tuple-element.41), channel_id=1, source_target_pairs={{0,1},{1,0},{2,3},{3,2},{4,5},{5,4},{6,7},{7,6},{8,9},{9,8},{10,11... | collective-permute-start | bytes 1867784 | tf_op jit(solution)/shard_map/ppermute | solution.py:355
  70.8 142.9 %collective-permute-start.4 = (f32[2,1216,128]{2,1,0:T(8,128)S(1)}, f32[2,1216,128]{2,1,0:T(8,128)}, u32[]{:S(2)}, u32[]{:S(2)}) collective-permute-start(f32[2,1216,128]{2,1,0:T(8,128)S(1)} %wave_looks.2.own_cs), channel_id=1, source_target_pairs={{1,3},{2,0},{3,5},{4,2},{5,7},{6,4},{7,9},{8,6},{9,11},{10,8},{11,... | collective-permute-start | bytes 3735560 | tf_op jit(solution)/shard_map/ppermute | solution.py:360
  77.1 3.8 %copy-start.9 = (s32[300]{0:T(512)S(1)}, s32[300]{0:T(512)}, u32[]{:S(2)}) copy-start(s32[300]{0:T(512)} %param.8) | copy-start | bytes 3604
  77.1 3.8 %copy-start.10 = (s32[300]{0:T(512)S(1)}, s32[300]{0:T(512)}, u32[]{:S(2)}) copy-start(s32[300]{0:T(512)} %param.9) | copy-start | bytes 3604
  77.1 71.5 %all-to-all-start = ((f32[4,75,8,128]{3,2,1,0:T(8,128)}), f32[4,75,8,128]{3,2,1,0:T(8,128)S(1)}, u32[]{:S(2)}, u32[]{:S(2)}) async-start(f32[4,75,8,128]{3,2,1,0:T(8,128)} %copy-done), calls=%async_computation | async-start | bytes 2457600 | tf_op jit(solution)/shard_map/all_to_all | solution.py:348
  86.0 0.7 copy-start.8
  119.4 0.7 copy-start.7
  145.4 68.3 %collective-permute-start.2 = (f32[2,1216,128]{2,1,0:T(8,128)}, f32[2,1216,128]{2,1,0:T(8,128)}, u32[]{:S(2)}, u32[]{:S(2)}) collective-permute-start(f32[2,1216,128]{2,1,0:T(8,128)} %collective-permute-done.mate_cs), channel_id=1, source_target_pairs={{0,2},{2,4},{3,1},{4,6},{5,3},{6,8},{7,5},{8,10},{9,7},{10,12},{11... | collective-permute-start | bytes 3735560 | tf_op jit(solution)/shard_map/ppermute | solution.py:362
  148.6 0.9 copy-start.4
  153.0 1.0 copy-start.1
  154.0 41.9 %all-to-all-start.2 = ((f32[32,32,159]{2,1,0:T(8,128)}), f32[32,32,159]{2,1,0:T(8,128)}, u32[]{:S(2)}, u32[]{:S(2)}) async-start(f32[32,32,159]{2,1,0:T(8,128)} %bitcast.55), calls=%async_computation.2 | async-start | bytes 2097152 | tf_op jit(solution)/shard_map/all_to_all | solution.py:383
  163.4 36.9 %collective-permute-start.5 = (f32[1216,128]{1,0:T(8,128)S(1)}, f32[1216,128]{1,0:T(8,128)S(1)}, u32[]{:S(2)}, u32[]{:S(2)}) collective-permute-start(f32[1216,128]{1,0:T(8,128)S(1)} %get-tuple-element.42.own_w), channel_id=1, source_target_pairs={{1,3},{2,0},{3,5},{4,2},{5,7},{6,4},{7,9},{8,6},{9,11},{10,8},{11,... | collective-permute-start | bytes 1867784 | tf_op jit(solution)/shard_map/ppermute | solution.py:359
  168.3 44.6 %collective-permute-start.3 = (f32[1216,128]{1,0:T(8,128)}, f32[1216,128]{1,0:T(8,128)S(1)}, u32[]{:S(2)}, u32[]{:S(2)}) collective-permute-start(f32[1216,128]{1,0:T(8,128)} %collective-permute-done.1.mate_w), channel_id=1, source_target_pairs={{0,2},{2,4},{3,1},{4,6},{5,3},{6,8},{7,5},{8,10},{9,7},{10,12},{11... | collective-permute-start | bytes 1867784 | tf_op jit(solution)/shard_map/ppermute | solution.py:361
  195.9 17.9 %copy-start.5 = (s32[9]{0:T(128)S(1)}, s32[9]{0:T(128)}, u32[]{:S(2)}) copy-start(s32[9]{0:T(128)} %row_off.1) | copy-start | bytes 112
  195.9 17.9 %copy-start.6 = (s32[9]{0:T(128)S(1)}, s32[9]{0:T(128)}, u32[]{:S(2)}) copy-start(s32[9]{0:T(128)} %col_off.1) | copy-start | bytes 112
  195.9 76.5 %all-to-all-start.1 = ((f32[4,75,8,128]{3,2,1,0:T(8,128)}), f32[4,75,8,128]{3,2,1,0:T(8,128)}, u32[]{:S(2)}, u32[]{:S(2)}) async-start(f32[4,75,8,128]{3,2,1,0:T(8,128)} %bitcast.23), calls=%async_computation.1 | async-start | bytes 2457600 | tf_op jit(solution)/shard_map/all_to_all | solution.py:378
  212.9 0.8 copy-start.2
  213.8 1.1 copy-start.3
  272.3 17.2 %collective-permute-start.6 = (f32[1216,128]{1,0:T(8,128)}, f32[1216,128]{1,0:T(8,128)S(1)}, u32[]{:S(2)}, u32[]{:S(2)}) collective-permute-start(f32[1216,128]{1,0:T(8,128)} %get-tuple-element.11), channel_id=1, source_target_pairs={{0,1},{1,0},{2,3},{3,2},{4,5},{5,4},{6,7},{7,6},{8,9},{9,8},{10,11... | collective-permute-start | bytes 1867784 | tf_op jit(solution)/shard_map/ppermute | solution.py:367

commit v2 on v1

--- a/solution.py
+++ b/solution.py
@@ -10,7 +10,7 @@
 DATES = 160
 AZ_LOOKS = 2
 RG_LOOKS = 8
-COL_REACH = 4
+REACH = 24
 OFFSETS = 9
 LANES = 128
 
@@ -33,22 +33,8 @@
 SIN_SCALE = 2.0 * math.sqrt(2.0)
 
 PIECES = 16
+PITCH = 17
 GROUP = 16
-
-
-def network_solve(reference_date, secondary_date):
-    date_index = jnp.arange(DATES, dtype=jnp.int32)
-    signed = (secondary_date[:, None] == date_index[None, :]).astype(jnp.float32) - (
-        reference_date[:, None] == date_index[None, :]
-    ).astype(jnp.float32)
-    design = signed[:, 1:]
-    normal_matrix = jnp.dot(
-        design.T, design, precision=lax.Precision.HIGHEST, preferred_element_type=jnp.float32
-    )
-    normal_matrix = normal_matrix + damping * jnp.eye(DATES - 1, dtype=jnp.float32)
-    factor = jnp.linalg.cholesky(normal_matrix)
-    inverse = jax.scipy.linalg.cho_solve((factor, True), design.T)
-    return (design, inverse)
 
 
 def pooling_matrix():
@@ -65,11 +51,13 @@
 
 
 def regroup(ref, held, rows):
-    held[...] = ref[rows].astype(jnp.float32).reshape(GROUP * PIECES, LANES)
+    tiles = ref[rows].astype(jnp.float32)
+    for m in range(GROUP):
+        held[m * PITCH : m * PITCH + PIECES, :] = tiles[m]
 
 
 def piece(held, q):
-    return held[pl.ds(q, GROUP, stride=PIECES), :]
+    return held[pl.ds(q, GROUP, stride=PITCH), :]
 
 
 def split_store(high, low, rows, c, value):
@@ -124,7 +112,7 @@
             jax.ShapeDtypeStruct((rows, LANES), jnp.float32),
             jax.ShapeDtypeStruct((4, rows // 32, 8, LANES), jnp.float32),
         ],
-        scratch_shapes=[pltpu.VMEM((GROUP * PIECES, LANES), jnp.float32)] * 2
+        scratch_shapes=[pltpu.VMEM((GROUP * PITCH, LANES), jnp.float32)] * 2
         + [pltpu.VMEM((block, RG_LOOKS * LANES), jnp.bfloat16)] * 4,
         compiler_params=pltpu.CompilerParams(vmem_limit_bytes=48 * 1024 * 1024),
         cost_estimate=pl.CostEstimate(
@@ -187,7 +175,7 @@
                 ),
             ],
             out_specs=pl.BlockSpec((2, block, LANES), lambda i, s: (0, i, 0)),
-            scratch_shapes=[pltpu.VMEM((GROUP * PIECES, LANES), jnp.float32)] * 2
+            scratch_shapes=[pltpu.VMEM((GROUP * PITCH, LANES), jnp.float32)] * 2
             + [pltpu.VMEM((block, RG_LOOKS * LANES), jnp.bfloat16)] * 4,
         ),
         out_shape=jax.ShapeDtypeStruct((2, count, LANES), jnp.float32),
@@ -200,90 +188,147 @@
 
 
 def window_kernel(
-    row_off, col_off, flip, own_cs, own_w, mate_cs, mate_w, near_cs, near_w, far_cs, far_w,
-    own_out, mate_out, held, cre, cim, sems,
+    near_cs, near_w, own_cs, own_w, mate_cs, mate_w, far_cs, far_w, bands, own_out, mate_out, parts
 ):
-    copies = []
-    for i, (cs, w) in enumerate(
-        ((near_cs, near_w), (own_cs, own_w), (mate_cs, mate_w), (far_cs, far_w))
-    ):
-        copies.append(pltpu.make_async_copy(cs, held.at[i, pl.ds(0, 2)], sems.at[i, 0]))
-        copies.append(pltpu.make_async_copy(w, held.at[i, 2], sems.at[i, 1]))
-    for c in copies:
-        c.start()
-    for c in copies:
-        c.wait()
-    cols = held.shape[2] // 32
-    lane = lax.broadcasted_iota(jnp.int32, (8, LANES), 1)
-    shifts = [col_off[k] for k in range(OFFSETS)]
-    rolls = [lax.rem(LANES - d, LANES) for d in shifts]
-    groups = (cols + 7) // 8
-
-    def one(t, carry):
-        side, g = t // groups, lax.rem(t, groups)
-        first = jnp.minimum(g * 8, cols - 8) * 32
-        sources = [1 + side + row_off[k] * flip[0] for k in range(OFFSETS)]
-        after = [lane + d >= LANES for d in shifts]
-        before = [lane + d < 0 for d in shifts]
+    rows = own_w.shape[0]
+    pairs = ((near_cs, near_w), (own_cs, own_w), (mate_cs, mate_w), (far_cs, far_w))
+
+    def divide(g, carry):
+        r = pl.ds(pl.multiple_of(g * 32, 32), 32)
+        for source, (cs, w) in enumerate(pairs):
+            for quantity in range(3):
+                value = cs[quantity, r, :] if quantity < 2 else w[r, :]
+                high = value.astype(jnp.bfloat16)
+                low = (value - high.astype(jnp.float32)).astype(jnp.bfloat16)
+                at = source * 2 * LANES
+                parts[quantity, r, at : at + LANES] = high
+                parts[quantity, r, at + LANES : at + 2 * LANES] = low
+        return carry
+
+    lax.fori_loop(0, rows // 32, divide, 0)
+    lane = lax.broadcasted_iota(jnp.int32, (rows, LANES), 1)
+    row = lax.rem(lax.broadcasted_iota(jnp.int32, (rows, LANES), 0), 32)
+    upper = lane >= LANES // 2
+    valid = (upper & (row < 31)) | (jnp.logical_not(upper) & (row > 0))
+    for side, out in enumerate((own_out, mate_out)):
+        sums = []
         for quantity in range(3):
-            def rolled(c):
-                if c < 0 or c > 31:
-                    return [jnp.zeros((8, LANES), jnp.float32)] * OFFSETS
-                out = []
-                for k in range(OFFSETS):
-                    v = held[sources[k], quantity, pl.ds(first + c, 8, stride=32), :]
-                    out.append(pltpu.roll(v, rolls[k], 1))
-                return out
-
-            last, now = rolled(-1), rolled(0)
-            for c in range(32):
-                following = rolled(c + 1)
-                total = None
-                for k in range(OFFSETS):
-                    term = jnp.where(after[k], following[k], jnp.where(before[k], last[k], now[k]))
-                    total = term if total is None else total + term
-                last, now = now, following
-                if quantity == 0:
-                    cre[c] = total
-                elif quantity == 1:
-                    cim[c] = total
-                else:
-                    re, im = cre[c], cim[c]
-                    value = jnp.sqrt(re * re + im * im) / total
-                    @pl.when(side == 0)
-                    def _():
-                        own_out[pl.ds(first + c, 8, stride=32), :] = value
-                    @pl.when(side == 1)
-                    def _():
-                        mate_out[pl.ds(first + c, 8, stride=32), :] = value
-        return carry
-
-    lax.fori_loop(0, 2 * groups, one, 0)
-
-
-def window_coherence(row_off, col_off, flip, own_cs, own_w, mate_cs, mate_w, near_cs, near_w, far_cs, far_w):
+            left = parts[quantity, :, side * 2 * LANES : (side + 3) * 2 * LANES]
+            both = jnp.dot(left, bands[...], preferred_element_type=jnp.float32)
+            edge = both[:, LANES:]
+            edge = jnp.where(upper, pltpu.roll(edge, rows - 1, 0), pltpu.roll(edge, 1, 0))
+            sums.append(both[:, :LANES] + jnp.where(valid, edge, 0.0))
+        re, im, w = sums
+        out[...] = jnp.sqrt(re * re + im * im) / w
+
+
+def window_coherence(bands, own_cs, own_w, mate_cs, mate_w, near_cs, near_w, far_cs, far_w):
     rows = own_w.shape[0]
-    smem = pl.BlockSpec(memory_space=pltpu.SMEM)
-    hbm = pl.BlockSpec(memory_space=pl.ANY)
-    vmem = pl.BlockSpec(memory_space=pltpu.VMEM)
+    block = rows // 2
+    cs = pl.BlockSpec((2, block, LANES), lambda i: (0, i, 0))
+    w = pl.BlockSpec((block, LANES), lambda i: (i, 0))
     shape = jax.ShapeDtypeStruct((rows, LANES), jnp.float32)
     return pl.pallas_call(
         window_kernel,
-        in_specs=[smem] * 3 + [hbm] * 8,
-        out_specs=[vmem, vmem],
+        grid=(2,),
+        in_specs=[cs, w] * 4 + [pl.BlockSpec(bands.shape, lambda i: (0, 0))],
+        out_specs=[w, w],
         out_shape=[shape, shape],
-        scratch_shapes=[
-            pltpu.VMEM((4, 3, rows, LANES), jnp.float32),
-            pltpu.VMEM((32, 8, LANES), jnp.float32),
-            pltpu.VMEM((32, 8, LANES), jnp.float32),
-            pltpu.SemaphoreType.DMA((4, 2)),
+        scratch_shapes=[pltpu.VMEM((3, block, 8 * LANES), jnp.bfloat16)],
+        compiler_params=pltpu.CompilerParams(vmem_limit_bytes=40 * 1024 * 1024),
+        cost_estimate=pl.CostEstimate(
+            flops=6 * rows * 768 * 512, bytes_accessed=14 * rows * LANES * 4, transcendentals=0
+        ),
+        name="window_coherence",
+    )(near_cs, near_w, own_cs, own_w, mate_cs, mate_w, far_cs, far_w, bands)
+
+
+def window_bands(row_off, col_off, flip, bands):
+    gap = lax.broadcasted_iota(jnp.int32, (LANES, LANES), 1) - lax.broadcasted_iota(
+        jnp.int32, (LANES, LANES), 0
+    )
+    for e in range(3):
+        same = jnp.zeros((LANES, LANES), jnp.float32)
+        next_to = jnp.zeros((LANES, LANES), jnp.float32)
+        for k in range(OFFSETS):
+            amount = jnp.where(row_off[k] * flip[0] == e - 1, 1.0, 0.0)
+            moved = gap + col_off[k]
+            same = same + jnp.where(moved == 0, amount, 0.0)
+            next_to = next_to + jnp.where(jnp.abs(moved) == LANES, amount, 0.0)
+        for half in range(2):
+            rows = slice((2 * e + half) * LANES, (2 * e + half + 1) * LANES)
+            bands[rows, :LANES] = same.astype(jnp.bfloat16)
+            bands[rows, LANES:] = next_to.astype(jnp.bfloat16)
+
+
+def network_kernel(
+    row_off, col_off, flip, reference, secondary, inverse, design, bands, grid
+):
+    count = inverse.shape[0]
+    window_bands(row_off, col_off, flip, bands)
+    date = lax.broadcasted_iota(jnp.int32, inverse.shape, 0) + 1
+    signed = (secondary[...] == date).astype(jnp.float32) - (reference[...] == date).astype(jnp.float32)
+    design[...] = jnp.transpose(signed)
+    exact = signed.astype(jnp.bfloat16)
+    normal = lax.dot_general(
+        exact, exact, (((1,), (1,)), ((), ())), preferred_element_type=jnp.float32
+    )
+    i = lax.broadcasted_iota(jnp.int32, (count, count), 0)
+    j = lax.broadcasted_iota(jnp.int32, (count, count), 1)
+    normal = normal + jnp.where(i == j, jnp.where(i == DATES - 1, 1.0, damping), 0.0)
+    grid[0] = normal[:, :LANES]
+    grid[1] = jnp.zeros((count, LANES), jnp.float32)
+    grid[1, :, : count - LANES] = normal[:, LANES:]
+    lane = lax.broadcasted_iota(jnp.int32, (1, LANES), 1)
+    for first in range(0, count, 32):
+        rows = min(first + 32 + REACH, count)
+        tiles = range(1 if rows <= LANES else 2)
+        half = first // LANES
+
+        def sweep(k, carry):
+            here = k - half * LANES
+            picked = lane == here
+            lines = [grid[t, pl.ds(k, 1), :] for t in tiles]
+            values = [grid[t, :rows, :] for t in tiles]
+            scale = 1.0 / jnp.sum(jnp.where(picked, lines[half], 0.0), axis=1, keepdims=True)
+            lines = [line * scale for line in lines]
+            lines[half] = jnp.where(picked, -scale, lines[half])
+            index = jnp.full((rows, LANES), here, jnp.int32)
+            column = jnp.take_along_axis(values[half], index, axis=1)
+            values[half] = jnp.where(picked, 0.0, values[half])
+            for t in tiles:
+                grid[t, :rows, :] = values[t] - column * lines[t]
+            for t in tiles:
+                grid[t, pl.ds(k, 1), :] = lines[t]
+            return carry
+
+        lax.fori_loop(first, first + 32, sweep, 0)
+    swept = jnp.concatenate([grid[0], grid[1, :, : count - LANES]], axis=1)
+    inverse[...] = -jnp.dot(
+        swept, signed, precision=lax.Precision.HIGHEST, preferred_element_type=jnp.float32
+    )
+
+
+def network_solve(window_rows, window_cols, flip, reference_date, secondary_date):
+    pairs = reference_date.shape[0]
+    vmem = pl.BlockSpec(memory_space=pltpu.VMEM)
+    smem = pl.BlockSpec(memory_space=pltpu.SMEM)
+    return pl.pallas_call(
+        network_kernel,
+        in_specs=[smem] * 3 + [vmem] * 2,
+        out_specs=[vmem] * 3,
+        out_shape=[
+            jax.ShapeDtypeStruct((DATES, pairs), jnp.float32),
+            jax.ShapeDtypeStruct((pairs, DATES), jnp.float32),
+            jax.ShapeDtypeStruct((6 * LANES, 2 * LANES), jnp.bfloat16),
         ],
-        compiler_params=pltpu.CompilerParams(vmem_limit_bytes=32 * 1024 * 1024),
+        scratch_shapes=[pltpu.VMEM((2, DATES, LANES), jnp.float32)],
+        compiler_params=pltpu.CompilerParams(vmem_limit_bytes=16 * 1024 * 1024),
         cost_estimate=pl.CostEstimate(
-            flops=200 * rows * LANES, bytes_accessed=14 * rows * LANES * 4, transcendentals=0
-        ),
-        name="window_coherence",
-    )(row_off, col_off, flip, own_cs, own_w, mate_cs, mate_w, near_cs, near_w, far_cs, far_w)
+            flops=20_000_000, bytes_accessed=80_000_000, transcendentals=0
+        ),
+        name="network_solve",
+    )(window_rows, window_cols, flip, reference_date[None, :], secondary_date[None, :])
 
 
 def invert_kernel(looked, inverse, design, residual, history, flat):
@@ -291,14 +336,13 @@
     for j in range(8):
         flat[:, j * LANES : (j + 1) * LANES] = looked[pl.ds(j, ifgs, stride=8), :]
     phase = flat[...]
-    solved = jnp.dot(
-        inverse[...], phase, precision=lax.Precision.HIGHEST, preferred_element_type=jnp.float32
-    )
-    fitted = jnp.dot(
-        design[...], solved, precision=lax.Precision.HIGHEST, preferred_element_type=jnp.float32
-    )
+
+    def product(a, b):
+        return jnp.dot(a, b, precision=lax.Precision.HIGHEST, preferred_element_type=jnp.float32)
+
+    solved = product(inverse[...], phase)
     history[...] = jnp.transpose(solved)[:, : DATES - 1]
-    rest = phase - fitted
+    rest = phase - product(design[...], solved)
     for j in range(8):
         residual[pl.ds(j, ifgs, stride=8), :] = rest[:, j * LANES : (j + 1) * LANES]
 
@@ -344,6 +388,10 @@
     phase = tiles(phase_samples)
     weight = tiles(sample_weights)
     pool = pooling_matrix()
+    flip = (1 - 2 * odd).reshape(1)
+    inverse, design, bands = network_solve(
+        window_rows, window_cols, flip, reference_date, secondary_date
+    )
     look_weight, looked = phase_looks(phase, weight, pool)
     moved = lax.all_to_all(looked, "ifg", split_axis=0, concat_axis=0, tiled=True)
 
@@ -360,9 +408,8 @@
     far_cs = lax.ppermute(own_cs, "rows", outward)
     near_w = lax.ppermute(mate_w, "rows", across)
     near_cs = lax.ppermute(mate_cs, "rows", across)
-    flip = (1 - 2 * odd).reshape(1)
     own_part, mate_part = window_coherence(
-        window_rows, window_cols, flip, own_cs, own_w, mate_cs, mate_w, near_cs, near_w, far_cs, far_w
+        bands, own_cs, own_w, mate_cs, mate_w, near_cs, near_w, far_cs, far_w
     )
     back = lax.ppermute(mate_part, "rows", mates)
     extra = (share - rest) * 32
@@ -372,7 +419,6 @@
         jnp.concatenate([back, own_part[extra:]]),
     )
 
-    design, inverse = network_solve(reference_date, secondary_date)
     tile_rows = moved.shape[0] * moved.shape[1] * moved.shape[2]
     residual, history = invert(moved.reshape(tile_rows, LANES), inverse, design)
     residual = lax.all_to_all(

time: 294 us -> 168 us (0.57)
  other arithmetic: 54.3 us -> 2.06 us
  Pallas kernels: 125 us -> 83.4 us
  waiting for transfers between devices: 52.9 us -> 27.4 us
  matrix products: 8.32 us -> 0 us
  starting transfers between devices: 36.3 us -> 41.2 us
    another operation x14 -> x0, other arithmetic: 50.3 us -> none  [the longest x7 27.4 us: network_solve(): factor = jnp.linalg.cholesky(normal_matrix)]
    pallas_call x1 -> x2, Pallas kernels: 57.4 us -> 26.3 us  [the longest x1 19.8 us: network_solve(): pl.pallas_call(network_kernel, in_specs=[smem] * 3 + [vmem] * 2, out_spec...]
    all_to_all x1, waiting for transfers between devices: 25.7 us -> 9.03 us  [local(): lax.all_to_all(history, 'rows', split_axis=0, concat_axis=0, tiled=True)]
    ppermute x1, waiting for transfers between devices: 12.6 us -> 3 us  [local(): near_w = lax.ppermute(mate_w, 'rows', across)]
    pallas_call x1, Pallas kernels: 24.7 us -> 17.7 us  [phase_looks(): pl.pallas_call(phase_kernel, grid=(rows // block,), in_specs=[pl.BlockSpe...]
    another operation x8 -> x0, matrix products: 6.71 us -> none  [the longest x6 4.37 us: network_solve(): inverse = jax.scipy.linalg.cho_solve((factor, True), design.T)]
    pallas_call x2, Pallas kernels: 39.1 us -> 34.3 us  [wave_looks(): pl.pallas_call(wave_kernel, grid_spec=pltpu.PrefetchScalarGridSpec(num_sc...]
    ppermute x1, waiting for transfers between devices: 0.01 us -> 4.48 us  [local(): far_w = lax.ppermute(own_w, 'rows', outward)]
  transfers between devices with their start and end apart: 10 -> 10, of which waited for: 3 -> 5; matrix products, arithmetic and copies ran while one was open for 23% -> 2% of each run, Pallas kernels for 27% -> 29%
where the time goes in v2:
time: 168 us; the launch traced here: 167 us
  Pallas kernels  83.4 us (50%)
  starting transfers between devices  41.2 us (25%)
  waiting for transfers between devices  27.4 us (16%)
  local copies, waits for them, and re-layouts  11.6 us (7%)
  other arithmetic  2.06 us (1%)
    pallas_call x2, Pallas kernels, wave_looks(): pl.pallas_call(wave_kernel, grid_spec=pltpu.PrefetchScalarGridSpec(num_sc...  34.3 us
    pallas_call x1, Pallas kernels, network_solve(): pl.pallas_call(network_kernel, in_specs=[smem] * 3 + [vmem] * 2, out_spec...  19.8 us
    pallas_call x1, Pallas kernels, phase_looks(): pl.pallas_call(phase_kernel, grid=(rows // block,), in_specs=[pl.BlockSpe...  17.7 us
    ppermute x1, waiting for transfers between devices, local(): back = lax.ppermute(mate_part, 'rows', mates)  10.7 us
    all_to_all x1, starting transfers between devices, local(): lax.all_to_all(history, 'rows', split_axis=0, concat_axis=0, tiled=True)  10.4 us
    all_to_all x1, waiting for transfers between devices, local(): lax.all_to_all(history, 'rows', split_axis=0, concat_axis=0, tiled=True)  9.03 us
    unnamed x21, local copies, waits for them, and re-layouts  8.12 us
    pallas_call x1, Pallas kernels, window_coherence(): pl.pallas_call(window_kernel, grid=(2,), in_specs=[cs, w] * 4 + [pl.Block...  6.56 us
  transfers between devices with their start and end apart: 10, of which 5 were waited for; matrix products, arithmetic and copies ran while one was open for 2% of the time, Pallas kernels for 29%

profile of v2, /device:TPU:6, one launch (start us, length us, event | category | flops | bytes accessed | tf_op | source)
XLA Modules:
  0.0 166.5 jit_solution(6982045587788708562)
XLA Ops:
  1.5 17.7 %phase_looks.1 = (f32[2400,128]{1,0:T(8,128)S(1)}, f32[4,75,8,128]{3,2,1,0:T(8,128)}) custom-call(bf16[2400,16,128]{2,1,0:T(8,128)(2,1)} %bitcast.20, bf16[2400,16,128]{2,1,0:T(8,128)(2,1)} %bitcast.23, bf16[1024,128]{1,0:T(8,128)(2,1)S(1)} %fusion.pool), custom_call_target="tpu_custom_call" | custom-call | flops 1258291200 | bytes 22118400 | tf_op jit(solution)/shard_map/phase_looks/pallas_call | solution.py:99
  19.2 17.5 %wave_looks.2 = f32[2,1216,128]{2,1,0:T(8,128)} custom-call(s32[1]{0:T(128)} %bitcast.start, bf16[2400,16,128]{2,1,0:T(8,128)(2,1)} %bitcast.21, bf16[2400,16,128]{2,1,0:T(8,128)(2,1)} %bitcast.24, bf16[1024,128]{1,0:T(8,128)(2,1)S(1)} %fusion.pool, f32[2400,128]{1,0:T(8,128)S(1)} %get-tuple-element.12.look_weight), custom_call_target="tpu_custom_call" | custom-call | flops 99614720 | bytes 11206656 | tf_op jit(solution)/shard_map/wave_looks/pallas_call | solution.py:157
  36.7 3.2 %collective-permute-start = (f32[2,1216,128]{2,1,0:T(8,128)}, f32[2,1216,128]{2,1,0:T(8,128)}, u32[]{:S(2)}, u32[]{:S(2)}) collective-permute-start(f32[2,1216,128]{2,1,0:T(8,128)} %wave_looks.2), channel_id=1, source_target_pairs={{0,1},{1,0},{2,3},{3,2},{4,5},{5,4},{6,7},{7,6},{8,9},{9,8},{10,11... | collective-permute-start | bytes 3735560 | tf_op jit(solution)/shard_map/ppermute | solution.py:405
  39.9 4.3 %all-to-all-start = ((f32[4,75,8,128]{3,2,1,0:T(8,128)}), f32[4,75,8,128]{3,2,1,0:T(8,128)}, u32[]{:S(2)}, u32[]{:S(2)}) async-start(f32[4,75,8,128]{3,2,1,0:T(8,128)} %get-tuple-element.16), calls=%async_computation | async-start | bytes 2457600 | tf_op jit(solution)/shard_map/all_to_all | solution.py:396
  45.5 16.9 %wave_looks.3.own_cs = f32[2,1216,128]{2,1,0:T(8,128)S(1)} custom-call(s32[1]{0:T(128)} %bitcast.11.start, bf16[2400,16,128]{2,1,0:T(8,128)(2,1)} %bitcast.22, bf16[2400,16,128]{2,1,0:T(8,128)(2,1)} %bitcast.25, bf16[1024,128]{1,0:T(8,128)(2,1)S(1)} %fusion.pool, f32[2400,128]{1,0:T(8,128)S(1)} %get-tuple-element.12.look_weight), custom_call_target="tpu_custom_call" | custom-call | flops 99614720 | bytes 11206656 | tf_op jit(solution)/shard_map/wave_looks/pallas_call | solution.py:157
  62.3 6.2 %collective-permute-start.4 = (f32[2,1216,128]{2,1,0:T(8,128)S(1)}, f32[2,1216,128]{2,1,0:T(8,128)S(1)}, u32[]{:S(2)}, u32[]{:S(2)}) collective-permute-start(f32[2,1216,128]{2,1,0:T(8,128)S(1)} %wave_looks.3.own_cs), channel_id=1, source_target_pairs={{1,3},{2,0},{3,5},{4,2},{5,7},{6,4},{7,9},{8,6},{9,11},{10,8},{11,... | collective-permute-start | bytes 3735560 | tf_op jit(solution)/shard_map/ppermute | solution.py:408
  68.8 3.8 %collective-permute-start.1 = (f32[2,1216,128]{2,1,0:T(8,128)}, f32[2,1216,128]{2,1,0:T(8,128)}, u32[]{:S(2)}, u32[]{:S(2)}) collective-permute-start(f32[2,1216,128]{2,1,0:T(8,128)} %collective-permute-done.mate_cs), channel_id=1, source_target_pairs={{0,2},{2,4},{3,1},{4,6},{5,3},{6,8},{7,5},{8,10},{9,7},{10,12},{11... | collective-permute-start | bytes 3735560 | tf_op jit(solution)/shard_map/ppermute | solution.py:410
  72.7 19.8 %network_solve.1 = (f32[160,300]{1,0:T(8,128)S(1)}, f32[300,160]{1,0:T(8,128)S(1)}, bf16[768,256]{1,0:T(8,128)(2,1)S(1)}) custom-call(s32[9]{0:T(128)S(1)} %copy-done.2, s32[9]{0:T(128)S(1)} %copy-done.3, s32[1]{0:T(128)} %bitcast.12.flip, s32[1,300]{1,0:T(1,128)S(1)} %broadcast_in_dim.6.reference, s32[1,300]{1,0:T(1,128)S(1)} %broadcast_in_dim.7.secondary), custom_call_target="tpu_custom_call" | custom-call | flops 20000000 | bytes 80000000 | tf_op jit(solution)/shard_map/network_solve/pallas_call | solution.py:316
  94.9 5.0 %invert.1 = (f32[2400,128]{1,0:T(8,128)}, f32[1024,159]{1,0:T(8,128)}) custom-call(f32[2400,128]{1,0:T(8,128)} %bitcast.14.looked, f32[160,300]{1,0:T(8,128)S(1)} %get-tuple-element.17.inverse, f32[300,160]{1,0:T(8,128)S(1)} %copy-done.7), custom_call_target="tpu_custom_call" | custom-call | flops 1179648000 | bytes 3686400 | tf_op jit(solution)/shard_map/invert/pallas_call | solution.py:353
  99.9 10.4 %all-to-all-start.2 = ((f32[32,32,159]{2,1,0:T(8,128)}), f32[32,32,159]{2,1,0:T(8,128)}, u32[]{:S(2)}, u32[]{:S(2)}) async-start(f32[32,32,159]{2,1,0:T(8,128)} %bitcast.18), calls=%async_computation.2 | async-start | bytes 2097152 | tf_op jit(solution)/shard_map/all_to_all | solution.py:429
  110.3 4.9 %collective-permute-start.5 = (f32[1216,128]{1,0:T(8,128)S(1)}, f32[1216,128]{1,0:T(8,128)}, u32[]{:S(2)}, u32[]{:S(2)}) collective-permute-start(f32[1216,128]{1,0:T(8,128)S(1)} %get-tuple-element.27.own_w), channel_id=1, source_target_pairs={{1,3},{2,0},{3,5},{4,2},{5,7},{6,4},{7,9},{8,6},{9,11},{10,8},{11,... | collective-permute-start | bytes 1867784 | tf_op jit(solution)/shard_map/ppermute | solution.py:407
  115.2 1.9 %collective-permute-start.3 = (f32[1216,128]{1,0:T(8,128)}, f32[1216,128]{1,0:T(8,128)}, u32[]{:S(2)}, u32[]{:S(2)}) collective-permute-start(f32[1216,128]{1,0:T(8,128)} %collective-permute-done.2.mate_w), channel_id=1, source_target_pairs={{0,2},{2,4},{3,1},{4,6},{5,3},{6,8},{7,5},{8,10},{9,7},{10,12},{11... | collective-permute-start | bytes 1867784 | tf_op jit(solution)/shard_map/ppermute | solution.py:409
  117.1 9.0 %all-to-all-done.2 = f32[32,32,159]{2,1,0:T(8,128)} async-done(((f32[32,32,159]{2,1,0:T(8,128)}), f32[32,32,159]{2,1,0:T(8,128)}, u32[]{:S(2)}, u32[]{:S(2)}) %all-to-all-start.2) | async-done | bytes 651296 | tf_op jit(solution)/shard_map/all_to_all | solution.py:429
  126.2 4.3 %all-to-all-start.1 = ((f32[4,75,8,128]{3,2,1,0:T(8,128)}), f32[4,75,8,128]{3,2,1,0:T(8,128)}, u32[]{:S(2)}, u32[]{:S(2)}) async-start(f32[4,75,8,128]{3,2,1,0:T(8,128)} %bitcast.15), calls=%async_computation.1 | async-start | bytes 2457600 | tf_op jit(solution)/shard_map/all_to_all | solution.py:424
  130.4 4.5 %collective-permute-done.5.far_w = f32[1216,128]{1,0:T(8,128)} collective-permute-done((f32[1216,128]{1,0:T(8,128)S(1)}, f32[1216,128]{1,0:T(8,128)}, u32[]{:S(2)}, u32[]{:S(2)}) %collective-permute-start.5) | collective-permute-done | bytes 622624 | tf_op jit(solution)/shard_map/ppermute | solution.py:407
  134.9 3.0 %collective-permute-done.3.near_w = f32[1216,128]{1,0:T(8,128)} collective-permute-done((f32[1216,128]{1,0:T(8,128)}, f32[1216,128]{1,0:T(8,128)}, u32[]{:S(2)}, u32[]{:S(2)}) %collective-permute-start.3) | collective-permute-done | bytes 622624 | tf_op jit(solution)/shard_map/ppermute | solution.py:409
  137.9 1.0 copy-done
  139.0 1.3 copy-done.1
  141.3 6.6 %window_coherence.1 = (f32[1216,128]{1,0:T(8,128)S(1)}, f32[1216,128]{1,0:T(8,128)S(1)}) custom-call(f32[2,1216,128]{2,1,0:T(8,128)} %collective-permute-done.1.near_cs, f32[1216,128]{1,0:T(8,128)} %collective-permute-done.3.near_w, f32[2,1216,128]{2,1,0:T(8,128)S(1)} %wave_looks.3.own_cs, f32[1216,128]{1,0:T(8,128)S(1)} %get-tuple-element.27.own_w, ...), custom_call_target="tpu_custom_call" | custom-call | flops 2868903936 | bytes 8716288 | tf_op jit(solution)/shard_map/window_coherence/pallas_call | solution.py:231
  147.8 1.9 %collective-permute-start.6 = (f32[1216,128]{1,0:T(8,128)S(1)}, f32[1216,128]{1,0:T(8,128)S(1)}, u32[]{:S(2)}, u32[]{:S(2)}) collective-permute-start(f32[1216,128]{1,0:T(8,128)S(1)} %get-tuple-element.15), channel_id=1, source_target_pairs={{0,1},{1,0},{2,3},{3,2},{4,5},{5,4},{6,7},{7,6},{8,9},{9,8},{10,11... | collective-permute-start | bytes 1867784 | tf_op jit(solution)/shard_map/ppermute | solution.py:414
  149.8 2.5 %copy.15 = f32[75,4,8,128]{3,2,1,0:T(8,128)} copy(f32[75,4,8,128]{3,2,0,1:T(8,128)} %bitcast.16) | data formatting | bytes 2457600 | tf_op jit(solution)/shard_map/transpose | solution.py:427
  152.3 10.7 %collective-permute-done.6 = f32[1216,128]{1,0:T(8,128)S(1)} collective-permute-done((f32[1216,128]{1,0:T(8,128)S(1)}, f32[1216,128]{1,0:T(8,128)S(1)}, u32[]{:S(2)}, u32[]{:S(2)}) %collective-permute-start.6) | collective-permute-done | bytes 622624 | tf_op jit(solution)/shard_map/ppermute | solution.py:414
  163.0 1.2 maximum_select_fusion
  164.2 2.3 %copy.18 = f32[159,32,32]{0,2,1:T(8,128)} copy(f32[159,32,32]{0,2,1:T(8,128)} %bitcast.19) | data formatting | bytes 1302528
  (33 shorter events, 5.9 us)
Async XLA Ops:
  36.7 32.1 %collective-permute-start = (f32[2,1216,128]{2,1,0:T(8,128)}, f32[2,1216,128]{2,1,0:T(8,128)}, u32[]{:S(2)}, u32[]{:S(2)}) collective-permute-start(f32[2,1216,128]{2,1,0:T(8,128)} %wave_looks.2), channel_id=1, source_target_pairs={{0,1},{1,0},{2,3},{3,2},{4,5},{5,4},{6,7},{7,6},{8,9},{9,8},{10,11... | collective-permute-start | bytes 3735560 | tf_op jit(solution)/shard_map/ppermute | solution.py:405
  39.9 54.1 %all-to-all-start = ((f32[4,75,8,128]{3,2,1,0:T(8,128)}), f32[4,75,8,128]{3,2,1,0:T(8,128)}, u32[]{:S(2)}, u32[]{:S(2)}) async-start(f32[4,75,8,128]{3,2,1,0:T(8,128)} %get-tuple-element.16), calls=%async_computation | async-start | bytes 2457600 | tf_op jit(solution)/shard_map/all_to_all | solution.py:396
  45.1 70.1 %collective-permute-start.2 = (f32[1216,128]{1,0:T(8,128)}, f32[1216,128]{1,0:T(8,128)}, u32[]{:S(2)}, u32[]{:S(2)}) collective-permute-start(f32[1216,128]{1,0:T(8,128)} %get-tuple-element.28), channel_id=1, source_target_pairs={{0,1},{1,0},{2,3},{3,2},{4,5},{5,4},{6,7},{7,6},{8,9},{9,8},{10,11... | collective-permute-start | bytes 1867784 | tf_op jit(solution)/shard_map/ppermute | solution.py:403
  45.4 27.1 %copy-start.8 = (s32[300]{0:T(512)S(1)}, s32[300]{0:T(512)}, u32[]{:S(2)}) copy-start(s32[300]{0:T(512)} %param.8) | copy-start | bytes 3604
  45.4 27.2 %copy-start.9 = (s32[300]{0:T(512)S(1)}, s32[300]{0:T(512)}, u32[]{:S(2)}) copy-start(s32[300]{0:T(512)} %param.9) | copy-start | bytes 3604
  45.5 27.2 %copy-start.2 = (s32[9]{0:T(128)S(1)}, s32[9]{0:T(128)}, u32[]{:S(2)}) copy-start(s32[9]{0:T(128)} %row_off.1) | copy-start | bytes 112
  45.5 27.2 %copy-start.3 = (s32[9]{0:T(128)S(1)}, s32[9]{0:T(128)}, u32[]{:S(2)}) copy-start(s32[9]{0:T(128)} %col_off.1) | copy-start | bytes 112
  62.3 75.6 %collective-permute-start.4 = (f32[2,1216,128]{2,1,0:T(8,128)S(1)}, f32[2,1216,128]{2,1,0:T(8,128)S(1)}, u32[]{:S(2)}, u32[]{:S(2)}) collective-permute-start(f32[2,1216,128]{2,1,0:T(8,128)S(1)} %wave_looks.3.own_cs), channel_id=1, source_target_pairs={{1,3},{2,0},{3,5},{4,2},{5,7},{6,4},{7,9},{8,6},{9,11},{10,8},{11,... | collective-permute-start | bytes 3735560 | tf_op jit(solution)/shard_map/ppermute | solution.py:408
  68.8 70.2 %collective-permute-start.1 = (f32[2,1216,128]{2,1,0:T(8,128)}, f32[2,1216,128]{2,1,0:T(8,128)}, u32[]{:S(2)}, u32[]{:S(2)}) collective-permute-start(f32[2,1216,128]{2,1,0:T(8,128)} %collective-permute-done.mate_cs), channel_id=1, source_target_pairs={{0,2},{2,4},{3,1},{4,6},{5,3},{6,8},{7,5},{8,10},{9,7},{10,12},{11... | collective-permute-start | bytes 3735560 | tf_op jit(solution)/shard_map/ppermute | solution.py:410
  92.4 0.8 copy-start.4
  93.2 0.7 copy-start.6
  94.0 1.0 copy-start.7
  99.9 26.2 %all-to-all-start.2 = ((f32[32,32,159]{2,1,0:T(8,128)}), f32[32,32,159]{2,1,0:T(8,128)}, u32[]{:S(2)}, u32[]{:S(2)}) async-start(f32[32,32,159]{2,1,0:T(8,128)} %bitcast.18), calls=%async_computation.2 | async-start | bytes 2097152 | tf_op jit(solution)/shard_map/all_to_all | solution.py:429
  110.3 24.6 %collective-permute-start.5 = (f32[1216,128]{1,0:T(8,128)S(1)}, f32[1216,128]{1,0:T(8,128)}, u32[]{:S(2)}, u32[]{:S(2)}) collective-permute-start(f32[1216,128]{1,0:T(8,128)S(1)} %get-tuple-element.27.own_w), channel_id=1, source_target_pairs={{1,3},{2,0},{3,5},{4,2},{5,7},{6,4},{7,9},{8,6},{9,11},{10,8},{11,... | collective-permute-start | bytes 1867784 | tf_op jit(solution)/shard_map/ppermute | solution.py:407
  115.2 22.7 %collective-permute-start.3 = (f32[1216,128]{1,0:T(8,128)}, f32[1216,128]{1,0:T(8,128)}, u32[]{:S(2)}, u32[]{:S(2)}) collective-permute-start(f32[1216,128]{1,0:T(8,128)} %collective-permute-done.2.mate_w), channel_id=1, source_target_pairs={{0,2},{2,4},{3,1},{4,6},{5,3},{6,8},{7,5},{8,10},{9,7},{10,12},{11... | collective-permute-start | bytes 1867784 | tf_op jit(solution)/shard_map/ppermute | solution.py:409
  126.2 23.6 %all-to-all-start.1 = ((f32[4,75,8,128]{3,2,1,0:T(8,128)}), f32[4,75,8,128]{3,2,1,0:T(8,128)}, u32[]{:S(2)}, u32[]{:S(2)}) async-start(f32[4,75,8,128]{3,2,1,0:T(8,128)} %bitcast.15), calls=%async_computation.1 | async-start | bytes 2457600 | tf_op jit(solution)/shard_map/all_to_all | solution.py:424
  137.9 1.0 copy-start
  139.0 1.3 copy-start.1
  140.3 1.0 copy-start.5
  147.8 15.1 %collective-permute-start.6 = (f32[1216,128]{1,0:T(8,128)S(1)}, f32[1216,128]{1,0:T(8,128)S(1)}, u32[]{:S(2)}, u32[]{:S(2)}) collective-permute-start(f32[1216,128]{1,0:T(8,128)S(1)} %get-tuple-element.15), channel_id=1, source_target_pairs={{0,1},{1,0},{2,3},{3,2},{4,5},{5,4},{6,7},{7,6},{8,9},{9,8},{10,11... | collective-permute-start | bytes 1867784 | tf_op jit(solution)/shard_map/ppermute | solution.py:414

commit v3 on v2

v3 whole, which is shorter than its diff:
```python
import functools
import math

import jax
import jax.numpy as jnp
from jax import lax
from jax.experimental import pallas as pl
from jax.experimental.pallas import tpu as pltpu
from jax.sharding import PartitionSpec as P

DATES = 160
AZ_LOOKS = 2
RG_LOOKS = 8
REACH = 24
OFFSETS = 9
LANES = 128

damping = 0.25

SIN_QUARTER = (
    0.3535533845424652,
    -0.0036828448064625263,
    1.1508434909046628e-05,
    -1.7096880355893518e-08,
    1.4046378643550739e-11,
)
COS_QUARTER = (
    0.9999999403953552,
    -0.031249957159161568,
    0.00016275106463581324,
    -3.383578359716921e-07,
    3.553040917037009e-10,
)
SIN_SCALE = 2.0 * math.sqrt(2.0)

PIECES = 16
PITCH = 17
GROUPS = 4
FIRST = 20
GROUP = 16


def pooling_matrix():
    row = lax.broadcasted_iota(jnp.int32, (LANES * RG_LOOKS, LANES), 0)
    col = lax.broadcasted_iota(jnp.int32, (LANES * RG_LOOKS, LANES), 1)
    return (row // RG_LOOKS == col).astype(jnp.bfloat16)


def lasting(us):
    return pl.CostEstimate(flops=0, bytes_accessed=int(us * 3.6e6), transcendentals=0)


def horner(coefficients, z):
    total = coefficients[-1] * z + coefficients[-2]
    for c in coefficients[-3::-1]:
        total = total * z + c
    return total


def regroup(ref, held, rows):
    tiles = ref[rows].astype(jnp.float32)
    for m in range(GROUP):
        held[m * PITCH : m * PITCH + PIECES, :] = tiles[m]


def piece(held, q):
    return held[pl.ds(q, GROUP, stride=PITCH), :]


def split_store(high, low, rows, c, value):
    top = value.astype(jnp.bfloat16)
    high[rows, c * LANES : (c + 1) * LANES] = top
    low[rows, c * LANES : (c + 1) * LANES] = (value - top.astype(jnp.float32)).astype(jnp.bfloat16)


def pooled(high, low, pool):
    return jnp.dot(high[...], pool[...], preferred_element_type=jnp.float32) + jnp.dot(
        low[...], pool[...], preferred_element_type=jnp.float32
    )


def look_kernel(start, phase, weight, pool, *refs):
    out, looked, p_held, w_held, wh, wl, ph, plo, sh, sl, qh, ql = refs[-12:]
    block = phase.shape[0]

    def step(g, carry):
        rows = pl.ds(pl.multiple_of(g * GROUP, GROUP), GROUP)
        regroup(phase, p_held, rows)
        regroup(weight, w_held, rows)
        for c in range(RG_LOOKS):
            sums = None
            for a in range(AZ_LOOKS):
                x = piece(p_held, 2 * c + a)
                w = piece(w_held, 2 * c + a)
                z = x * x
                s = x * horner(SIN_QUARTER, z)
                k = horner(COS_QUARTER, z)
                half = s * k
                terms = (w, w * x, w * (half * (1.0 - s * s)), w * (half * half))
                sums = terms if sums is None else [t + u for t, u in zip(sums, terms)]
            for value, high, low in zip(sums, (wh, ph, sh, qh), (wl, plo, sl, ql)):
                split_store(high, low, rows, c, value)
        return carry

    lax.fori_loop(0, block // GROUP, step, 0)
    total = pooled(wh, wl, pool)
    mean = pooled(ph, plo, pool) / total
    looked[...] = jnp.transpose(mean.reshape(block // 32, GROUPS, 8, LANES), (1, 0, 2, 3))
    out[0] = total - 4.0 * pooled(qh, ql, pool)
    out[1] = SIN_SCALE * pooled(sh, sl, pool)
    out[2] = total


def look_sums(start, count, block, slot, slots, phase, weight, pool, looked=None, after=()):
    element = pl.Element
    rows = block * 32
    samples = pl.BlockSpec(
        (element(rows), element(PIECES), element(LANES)),
        lambda i, s: (pl.multiple_of(s[0] + i * rows, 16), 0, 0),
    )
    operands = [phase, weight, pool]
    in_specs = [samples, samples, pl.BlockSpec(pool.shape, lambda i, s: (0, 0))]
    aliases = {}
    if looked is not None:
        operands.append(looked)
        in_specs.append(pl.BlockSpec(memory_space=pl.ANY))
        aliases = {4: 1}
    operands.extend(after)
    in_specs.extend([pl.BlockSpec(memory_space=pl.ANY)] * len(after))
    return pl.pallas_call(
        look_kernel,
        grid_spec=pltpu.PrefetchScalarGridSpec(
            num_scalar_prefetch=1,
            grid=(count // block,),
            in_specs=in_specs,
            out_specs=[
                pl.BlockSpec((3, rows, LANES), lambda i, s: (0, i, 0)),
                pl.BlockSpec(
                    (element(GROUPS), element(block), element(8), element(LANES)),
                    lambda i, s: (0, slot + i * block, 0, 0),
                ),
            ],
            scratch_shapes=[pltpu.VMEM((GROUP * PITCH, LANES), jnp.float32)] * 2
            + [pltpu.VMEM((rows, RG_LOOKS * LANES), jnp.bfloat16)] * 8,
        ),
        out_shape=[
            jax.ShapeDtypeStruct((3, count * 32, LANES), jnp.float32),
            jax.ShapeDtypeStruct((GROUPS, slots, 8, LANES), jnp.float32),
        ],
        input_output_aliases=aliases,
        compiler_params=pltpu.CompilerParams(vmem_limit_bytes=56 * 1024 * 1024),
        cost_estimate=lasting(0.02),
        name="look_sums",
    )(start, *operands)


def window_kernel(near, own, mate, far, bands, *refs):
    own_out, mate_out, parts = refs[-3:]
    rows = own.shape[1]

    def divide(g, carry):
        r = pl.ds(pl.multiple_of(g * 32, 32), 32)
        for source, ref in enumerate((near, own, mate, far)):
            for quantity in range(3):
                value = ref[quantity, r, :]
                high = value.astype(jnp.bfloat16)
                low = (value - high.astype(jnp.float32)).astype(jnp.bfloat16)
                at = source * 2 * LANES
                parts[quantity, r, at : at + LANES] = high
                parts[quantity, r, at + LANES : at + 2 * LANES] = low
        return carry

    lax.fori_loop(0, rows // 32, divide, 0)
    lane = lax.broadcasted_iota(jnp.int32, (rows, LANES), 1)
    row = lax.rem(lax.broadcasted_iota(jnp.int32, (rows, LANES), 0), 32)
    upper = lane >= LANES // 2
    valid = (upper & (row < 31)) | (jnp.logical_not(upper) & (row > 0))
    for side, out in enumerate((own_out, mate_out)):
        sums = []
        for quantity in range(3):
            left = parts[quantity, :, side * 2 * LANES : (side + 3) * 2 * LANES]
            both = jnp.dot(left, bands[...], preferred_element_type=jnp.float32)
            edge = both[:, LANES:]
            edge = jnp.where(upper, pltpu.roll(edge, rows - 1, 0), pltpu.roll(edge, 1, 0))
            sums.append(both[:, :LANES] + jnp.where(valid, edge, 0.0))
        re, im, w = sums
        out[...] = jnp.sqrt(re * re + im * im) / w


def window_coherence(bands, near, own, mate, far, after=()):
    count = mate.shape[1]
    rows = count // 2
    part = pl.BlockSpec((3, rows, LANES), lambda i: (0, i, 0))
    out = pl.BlockSpec((rows, LANES), lambda i: (i, 0))
    return pl.pallas_call(
        window_kernel,
        grid=(2,),
        in_specs=[part] * 4
        + [pl.BlockSpec(bands.shape, lambda i: (0, 0))]
        + [pl.BlockSpec(memory_space=pl.ANY)] * len(after),
        out_specs=[out, out],
        out_shape=[jax.ShapeDtypeStruct((count, LANES), jnp.float32)] * 2,
        scratch_shapes=[pltpu.VMEM((3, rows, 8 * LANES), jnp.bfloat16)],
        compiler_params=pltpu.CompilerParams(vmem_limit_bytes=40 * 1024 * 1024),
        cost_estimate=lasting(0.02),
        name="window_coherence",
    )(near, own, mate, far, bands, *after)


def merge_kernel(odd, own_a, own_b, other_a, other_b, out):
    first, share = own_a.shape[0], own_a.shape[0] + own_b.shape[0]

    @pl.when(odd[0] == 0)
    def _():
        out[:first] = own_a[...]
        out[first:share] = own_b[...]
        out[share : share + first - 1] = other_a[1:]
        out[share + first - 1 :] = other_b[...]

    @pl.when(odd[0] != 0)
    def _():
        out[:first] = other_a[...]
        out[first:share] = other_b[...]
        out[share : share + first - 1] = own_a[1:]
        out[share + first - 1 :] = own_b[...]


def merge(odd, ifgs, *parts):
    vmem = pl.BlockSpec(memory_space=pltpu.VMEM)
    return pl.pallas_call(
        merge_kernel,
        in_specs=[pl.BlockSpec(memory_space=pltpu.SMEM)] + [vmem] * 4,
        out_specs=vmem,
        out_shape=jax.ShapeDtypeStruct((ifgs, *parts[0].shape[1:]), jnp.float32),
        compiler_params=pltpu.CompilerParams(vmem_limit_bytes=8 * 1024 * 1024),
        cost_estimate=lasting(0.3),
        name="merge",
    )(odd, *parts)


def unslot_kernel(where, *refs):
    parts, out = refs[:GROUPS], refs[-1]
    share = parts[0].shape[0] // 2
    rest = out.shape[0] - share
    odd = where[0]
    for d, part in enumerate(parts):
        chunk = pl.ds(jnp.bitwise_xor(where[1], d), 1)
        out[:share, chunk] = part[pl.ds(share * (1 - odd), share)][:, None]
        out[share:, chunk] = part[pl.ds(1 + share * odd, rest)][:, None]


def unslot(where, ifgs, parts, after):
    vmem = pl.BlockSpec(memory_space=pltpu.VMEM)
    return pl.pallas_call(
        unslot_kernel,
        in_specs=[pl.BlockSpec(memory_space=pltpu.SMEM)] + [vmem] * GROUPS
        + [pl.BlockSpec(memory_space=pl.ANY)] * len(after),
        out_specs=vmem,
        out_shape=jax.ShapeDtypeStruct((ifgs, GROUPS, *parts[0].shape[1:]), jnp.float32),
        compiler_params=pltpu.CompilerParams(vmem_limit_bytes=8 * 1024 * 1024),
        cost_estimate=lasting(50),
        name="unslot",
    )(where, *parts, *after)


def bands_kernel(row_off, col_off, flip, bands):
    gap = lax.broadcasted_iota(jnp.int32, (LANES, LANES), 1) - lax.broadcasted_iota(
        jnp.int32, (LANES, LANES), 0
    )
    for e in range(3):
        same = jnp.zeros((LANES, LANES), jnp.float32)
        next_to = jnp.zeros((LANES, LANES), jnp.float32)
        for k in range(OFFSETS):
            amount = jnp.where(row_off[k] * flip[0] == e - 1, 1.0, 0.0)
            moved = gap + col_off[k]
            same = same + jnp.where(moved == 0, amount, 0.0)
            next_to = next_to + jnp.where(jnp.abs(moved) == LANES, amount, 0.0)
        for half in range(2):
            rows = slice((2 * e + half) * LANES, (2 * e + half + 1) * LANES)
            bands[rows, :LANES] = same.astype(jnp.bfloat16)
            bands[rows, LANES:] = next_to.astype(jnp.bfloat16)


def window_bands(row_off, col_off, flip):
    return pl.pallas_call(
        bands_kernel,
        in_specs=[pl.BlockSpec(memory_space=pltpu.SMEM)] * 3,
        out_specs=pl.BlockSpec(memory_space=pltpu.VMEM),
        out_shape=jax.ShapeDtypeStruct((6 * LANES, 2 * LANES), jnp.bfloat16),
        cost_estimate=lasting(1),
        name="window_bands",
    )(row_off, col_off, flip)


def network_kernel(
    flip, dates, *refs, slots
):
    inverse, design, grid = refs[-3:]
    count = inverse.shape[0]
    date = lax.broadcasted_iota(jnp.int32, inverse.shape, 0) + 1
    signed = (dates[1:2] == date).astype(jnp.float32) - (dates[0:1] == date).astype(jnp.float32)
    design[...] = jnp.transpose(signed)
    slot = lax.rem(lax.broadcasted_iota(jnp.int32, inverse.shape, 1), slots)
    again = jnp.where(flip[0] > 0, 0, slots // 2 - 1)
    counted = jnp.where(slot == again, 0.0, signed)
    normal = lax.dot_general(
        counted.astype(jnp.bfloat16), signed.astype(jnp.bfloat16), (((1,), (1,)), ((), ())), preferred_element_type=jnp.float32
    )
    i = lax.broadcasted_iota(jnp.int32, (count, count), 0)
    j = lax.broadcasted_iota(jnp.int32, (count, count), 1)
    normal = normal + jnp.where(i == j, jnp.where(i == DATES - 1, 1.0, damping), 0.0)
    grid[0] = normal[:, :LANES]
    grid[1] = jnp.zeros((count, LANES), jnp.float32)
    grid[1, :, : count - LANES] = normal[:, LANES:]
    lane = lax.broadcasted_iota(jnp.int32, (1, LANES), 1)
    for first in range(0, count, 32):
        rows = min(first + 32 + REACH, count)
        tiles = range(1 if rows <= LANES else 2)
        half = first // LANES

        def sweep(k, carry):
            here = k - half * LANES
            picked = lane == here
            lines = [grid[t, pl.ds(k, 1), :] for t in tiles]
            values = [grid[t, :rows, :] for t in tiles]
            scale = 1.0 / jnp.sum(jnp.where(picked, lines[half], 0.0), axis=1, keepdims=True)
            lines = [line * scale for line in lines]
            lines[half] = jnp.where(picked, -scale, lines[half])
            index = jnp.full((rows, LANES), here, jnp.int32)
            column = jnp.take_along_axis(values[half], index, axis=1)
            values[half] = jnp.where(picked, 0.0, values[half])
            for t in tiles:
                grid[t, :rows, :] = values[t] - column * lines[t]
            for t in tiles:
                grid[t, pl.ds(k, 1), :] = lines[t]
            return carry

        lax.fori_loop(first, first + 32, sweep, 0)
    swept = jnp.concatenate([grid[0], grid[1, :, : count - LANES]], axis=1)
    inverse[...] = -jnp.dot(
        swept, counted, precision=lax.Precision.HIGHEST, preferred_element_type=jnp.float32
    )


def network_solve(flip, dates, slots, after=()):
    pairs = dates.shape[1]
    vmem = pl.BlockSpec(memory_space=pltpu.VMEM)
    smem = pl.BlockSpec(memory_space=pltpu.SMEM)
    return pl.pallas_call(
        functools.partial(network_kernel, slots=slots),
        in_specs=[smem, vmem] + [pl.BlockSpec(memory_space=pl.ANY)] * len(after),
        out_specs=[vmem] * 2,
        out_shape=[
            jax.ShapeDtypeStruct((DATES, pairs), jnp.float32),
            jax.ShapeDtypeStruct((pairs, DATES), jnp.float32),
        ],
        scratch_shapes=[pltpu.VMEM((2, DATES, LANES), jnp.float32)],
        compiler_params=pltpu.CompilerParams(vmem_limit_bytes=16 * 1024 * 1024),
        cost_estimate=lasting(0.02),
        name="network_solve",
    )(flip, dates, *after)


def invert_kernel(group, looked, inverse, design, *refs):
    *residuals, history, flat, held = refs[-GROUPS - 3 :]
    slots = residuals[0].shape[0]
    count = GROUPS * slots
    rows = looked.reshape(count * 8, LANES)
    for j in range(8):
        flat[:, j * LANES : (j + 1) * LANES] = rows[pl.ds(j, count, stride=8), :]
    phase = flat[...]

    def product(a, b):
        return jnp.dot(a, b, precision=lax.Precision.HIGHEST, preferred_element_type=jnp.float32)

    solved = product(inverse[...], phase)
    history[...] = jnp.transpose(solved)[:, : DATES - 1]
    rest = phase - product(design[...], solved)
    lines = held.reshape(count * 8, LANES)
    for j in range(8):
        lines[pl.ds(j, count, stride=8), :] = rest[:, j * LANES : (j + 1) * LANES]
    for d, residual in enumerate(residuals):
        residual[...] = held[pl.ds(jnp.bitwise_xor(group[0], d) * slots, slots)]


def invert(group, looked, inverse, design, after):
    slots = looked.shape[1]
    vmem = pl.BlockSpec(memory_space=pltpu.VMEM)
    part = jax.ShapeDtypeStruct((slots, 8, LANES), jnp.float32)
    return pl.pallas_call(
        invert_kernel,
        in_specs=[pl.BlockSpec(memory_space=pltpu.SMEM)]
        + [vmem] * 3
        + [pl.BlockSpec(memory_space=pl.ANY)] * len(after),
        out_specs=[vmem] * (GROUPS + 1),
        out_shape=[part] * GROUPS + [jax.ShapeDtypeStruct((8 * LANES, DATES - 1), jnp.float32)],
        scratch_shapes=[
            pltpu.VMEM((GROUPS * slots, 8 * LANES), jnp.float32),
            pltpu.VMEM((GROUPS * slots, 8, LANES), jnp.float32),
        ],
        compiler_params=pltpu.CompilerParams(vmem_limit_bytes=32 * 1024 * 1024),
        cost_estimate=lasting(0.02),
        name="invert",
    )(group, looked, inverse, design, *after)


def tiles(samples):
    ifgs, az, cols = samples.shape
    split = samples.reshape(ifgs, az, cols // LANES, LANES).transpose(0, 2, 1, 3)
    return split.reshape(ifgs * cols // (LANES * RG_LOOKS), PIECES, LANES)


def local(phase_samples, sample_weights, reference_date, secondary_date, window_rows, window_cols):
    ifgs = phase_samples.shape[0]
    row_count = lax.axis_size("rows")
    odd = lax.rem(lax.axis_index("rows"), 2)
    share = (ifgs + 1) // 2
    rest = ifgs - share
    mates = [(r, r ^ 1) for r in range(row_count)]
    outward = [(r, r + 2 if r % 2 else r - 2) for r in range(row_count)]
    outward = [(s, d) for s, d in outward if 0 <= d < row_count]
    across = [(r, r - 2 if r % 2 else r + 2) for r in range(row_count)]
    across = [(s, d) for s, d in across if 0 <= d < row_count]

    group = lax.axis_index("ifg")
    phase = tiles(phase_samples)
    weight = tiles(sample_weights)
    pool = pooling_matrix()
    flip = (1 - 2 * odd).reshape(1)
    side = odd.reshape(1)
    mine = rest * 32 * odd
    other = rest * 32 * (1 - odd)
    slots = 2 * share
    early = FIRST
    late = share - early

    sent_a, looked = look_sums(
        other.reshape(1), early, early // 2, 0, slots, phase, weight, pool
    )
    mate_a = lax.ppermute(sent_a, "rows", mates)
    sent_b, looked = look_sums(
        (other + early * 32).reshape(1), late, late // 2, early, slots, phase, weight, pool, looked
    )
    mate_b = lax.ppermute(sent_b, "rows", mates)
    own_a, looked = look_sums(
        mine.reshape(1), early, early // 2, share, slots, phase, weight, pool, looked
    )
    far_a = lax.ppermute(own_a, "rows", outward)
    own_b, looked = look_sums(
        (mine + early * 32).reshape(1), late, late // 2, share + early, slots,
        phase, weight, pool, looked, (mate_a,),
    )
    far_b = lax.ppermute(own_b, "rows", outward)
    near_a = lax.ppermute(mate_a, "rows", across)
    moved = lax.all_to_all(looked, "ifg", split_axis=0, concat_axis=0, tiled=True)

    dates = jnp.stack([reference_date, secondary_date]).reshape(2, GROUPS, ifgs)
    dates = jnp.where(
        odd == 0,
        jnp.concatenate([dates[:, :, rest:], dates[:, :, :share]], axis=2),
        jnp.concatenate([dates[:, :, :share], dates[:, :, rest:]], axis=2),
    ).reshape(2, -1)
    bands = window_bands(window_rows, window_cols, flip)
    near_b = lax.ppermute(mate_b, "rows", across)
    own_part_a, mate_part_a = window_coherence(
        bands, near_a, own_a, mate_a, far_a
    )
    back_a = lax.ppermute(mate_part_a, "rows", mates)
    inverse, design = network_solve(flip, dates, slots, (mate_b, mate_part_a))
    *residual, history = invert(
        group.reshape(1), moved, inverse, design, (back_a,)
    )
    residual = residual[:1] + [
        lax.ppermute(residual[d], "ifg", [(i, i ^ d) for i in range(GROUPS)])
        for d in range(1, GROUPS)
    ]
    own_part_b, mate_part_b = window_coherence(
        bands, near_b, own_b, mate_b, far_b, after=(residual[1], history)
    )
    back_b = lax.ppermute(mate_part_b, "rows", mates)

    by_ifg = (-1, 32, LANES)
    coherence = merge(
        side, ifgs, *[part.reshape(by_ifg) for part in (own_part_a, own_part_b, back_a, back_b)]
    )

    residual = unslot(jnp.stack([odd, group]), ifgs, residual, (coherence,))
    history = history.reshape(row_count, -1, DATES - 1)
    history = lax.all_to_all(history, "rows", split_axis=0, concat_axis=0, tiled=True)
    shape = (ifgs, 1, 32 * LANES)
    return (coherence.reshape(shape), residual.reshape(shape), history.transpose(2, 0, 1))


def solution(mesh):
    placed = (P("ifg", "rows", None), P("ifg", "rows", None), P(), P(), P(), P())
    return jax.shard_map(
        local,
        mesh=mesh,
        in_specs=placed,
        out_specs=(P("ifg", "rows", None), P("ifg", "rows", None), P(None, None, ("ifg", "rows"))),
        check_vma=False,
    )
```

time: 168 us -> 160 us (0.952)
  local copies, waits for them, and re-layouts: 11.6 us -> 7.82 us
  waiting for transfers between devices: 27.4 us -> 24.2 us
  Pallas kernels: 83.4 us -> 86.2 us
  starting transfers between devices: 41.2 us -> 38.5 us
    all_to_all x1, waiting for transfers between devices: 9.03 us -> 0.01 us  [local(): lax.all_to_all(history, 'rows', split_axis=0, concat_axis=0, tiled=True)]
    ppermute x7 -> x11, waiting for transfers between devices: 18.4 us -> 24.2 us  [the longest x1 24.1 us: local(): back_b = lax.ppermute(mate_part_b, 'rows', mates)]
    all_to_all x1 -> x0, starting transfers between devices: 4.28 us -> none  [local(): lax.all_to_all(residual.reshape(moved.shape), 'ifg', split_axis=0, concat...]
    ppermute x7 -> x11, starting transfers between devices: 22.3 us -> 26.4 us  [the longest x1 6.2 us: local(): far_a = lax.ppermute(own_a, 'rows', outward)]
    pallas_call x6 -> x11, Pallas kernels: 83.4 us -> 86.2 us  [the longest x4 50.3 us: look_sums(): pl.pallas_call(look_kernel, grid_spec=pltpu.PrefetchScalarGridSpec(num_sc...]
    transpose x1 -> x0, local copies, waits for them, and re-layouts: 2.48 us -> none  [local(): residual = residual.transpose(1, 0, 2, 3)]
    all_to_all x1, starting transfers between devices: 10.4 us -> 8.45 us  [local(): lax.all_to_all(history, 'rows', split_axis=0, concat_axis=0, tiled=True)]
    unnamed x21 -> x28, local copies, waits for them, and re-layouts: 8.12 us -> 7.49 us
  transfers between devices with their start and end apart: 10 -> 13, of which waited for: 5 -> 1; matrix products, arithmetic and copies ran while one was open for 2% -> 0% of each run, Pallas kernels for 29% -> 46%
where the time goes in v3:
time: 160 us; the launch traced here: 159 us
  Pallas kernels  86.2 us (54%)
  starting transfers between devices  38.5 us (24%)
  waiting for transfers between devices  24.2 us (15%)
  local copies, waits for them, and re-layouts  7.82 us (5%)
  other arithmetic  1.68 us (1%)
    pallas_call x4, Pallas kernels, look_sums(): pl.pallas_call(look_kernel, grid_spec=pltpu.PrefetchScalarGridSpec(num_sc...  50.3 us
    ppermute x1, waiting for transfers between devices, local(): back_b = lax.ppermute(mate_part_b, 'rows', mates)  24.1 us
    pallas_call x1, Pallas kernels, network_solve(): pl.pallas_call(functools.partial(network_kernel, slots=slots), in_specs=[...  18.9 us
    pallas_call x2, Pallas kernels, window_coherence(): pl.pallas_call(window_kernel, grid=(2,), in_specs=[part] * 4 + [pl.BlockS...  8.71 us
    all_to_all x1, starting transfers between devices, local(): lax.all_to_all(history, 'rows', split_axis=0, concat_axis=0, tiled=True)  8.45 us
    unnamed x28, local copies, waits for them, and re-layouts  7.49 us
    ppermute x1, starting transfers between devices, local(): far_a = lax.ppermute(own_a, 'rows', outward)  6.2 us
    ppermute x1, starting transfers between devices, local(): far_b = lax.ppermute(own_b, 'rows', outward)  6.03 us
  transfers between devices with their start and end apart: 13, of which 1 were waited for; matrix products, arithmetic and copies ran while one was open for 0% of the time, Pallas kernels for 46%

profile of v3, /device:TPU:6, one launch (start us, length us, event | category | flops | bytes accessed | tf_op | source)
XLA Modules:
  0.0 159.2 jit_solution(5963354021551520415)
XLA Ops:
  0.7 1.5 fusion.pool
  2.2 13.1 %look_sums.4 = (f32[3,640,128]{2,1,0:T(8,128)}, f32[4,76,8,128]{3,2,1,0:T(8,128)}) custom-call(s32[1]{0:T(128)} %bitcast.1.start, bf16[2400,16,128]{2,1,0:T(8,128)(2,1)} %bitcast.30, bf16[2400,16,128]{2,1,0:T(8,128)(2,1)} %bitcast.34, bf16[1024,128]{1,0:T(8,128)(2,1)} %fusion.pool), custom_call_target="tpu_custom_call" | custom-call | bytes 72000 | tf_op jit(solution)/shard_map/look_sums/pallas_call | solution.py:130
  15.3 3.2 %collective-permute-start = (f32[3,640,128]{2,1,0:T(8,128)}, f32[3,640,128]{2,1,0:T(8,128)}, u32[]{:S(2)}, u32[]{:S(2)}) collective-permute-start(f32[3,640,128]{2,1,0:T(8,128)} %get-tuple-element.22), channel_id=1, source_target_pairs={{0,1},{1,0},{2,3},{3,2},{4,5},{5,4},{6,7},{7,6},{8,9},{9,8},{10,11... | collective-permute-start | bytes 2949128 | tf_op jit(solution)/shard_map/ppermute | solution.py:440
  18.5 12.0 %look_sums.5 = (f32[3,576,128]{2,1,0:T(8,128)}, f32[4,76,8,128]{3,2,1,0:T(8,128)}) custom-call(s32[1]{0:T(128)} %bitcast.13.start, bf16[2400,16,128]{2,1,0:T(8,128)(2,1)} %bitcast.31, bf16[2400,16,128]{2,1,0:T(8,128)(2,1)} %bitcast.35, bf16[1024,128]{1,0:T(8,128)(2,1)} %fusion.pool, ...), custom_call_target="tpu_custom_call", output_to_operand_aliasing={{1}: (4, {})} | custom-call | bytes 72000 | tf_op jit(solution)/shard_map/look_sums/pallas_call | solution.py:130
  30.9 13.1 %look_sums.6 = (f32[3,640,128]{2,1,0:T(8,128)}, f32[4,76,8,128]{3,2,1,0:T(8,128)}) custom-call(s32[1]{0:T(128)} %bitcast.8.start, bf16[2400,16,128]{2,1,0:T(8,128)(2,1)} %bitcast.32, bf16[2400,16,128]{2,1,0:T(8,128)(2,1)} %bitcast.36, bf16[1024,128]{1,0:T(8,128)(2,1)} %fusion.pool, ...), custom_call_target="tpu_custom_call", output_to_operand_aliasing={{1}: (4, {})} | custom-call | bytes 72000 | tf_op jit(solution)/shard_map/look_sums/pallas_call | solution.py:130
  44.0 6.2 %collective-permute-start.2 = (f32[3,640,128]{2,1,0:T(8,128)}, f32[3,640,128]{2,1,0:T(8,128)}, u32[]{:S(2)}, u32[]{:S(2)}) collective-permute-start(f32[3,640,128]{2,1,0:T(8,128)} %get-tuple-element.25.own), channel_id=1, source_target_pairs={{1,3},{2,0},{3,5},{4,2},{5,7},{6,4},{7,9},{8,6},{9,11},{10,8},{11,... | collective-permute-start | bytes 2949128 | tf_op jit(solution)/shard_map/ppermute | solution.py:448
  50.2 1.9 %collective-permute-start.1 = (f32[3,640,128]{2,1,0:T(8,128)}, f32[3,640,128]{2,1,0:T(8,128)}, u32[]{:S(2)}, u32[]{:S(2)}) collective-permute-start(f32[3,640,128]{2,1,0:T(8,128)} %collective-permute-done.mate.refs_1_), channel_id=1, source_target_pairs={{0,2},{2,4},{3,1},{4,6},{5,3},{6,8},{7,5},{8,10},{9,7},{10,12},{11... | collective-permute-start | bytes 2949128 | tf_op jit(solution)/shard_map/ppermute | solution.py:454
  52.1 12.0 %look_sums.7 = (f32[3,576,128]{2,1,0:T(8,128)}, f32[4,76,8,128]{3,2,1,0:T(8,128)}) custom-call(s32[1]{0:T(128)} %bitcast.16.start, bf16[2400,16,128]{2,1,0:T(8,128)(2,1)} %bitcast.33, bf16[2400,16,128]{2,1,0:T(8,128)(2,1)} %bitcast.37, bf16[1024,128]{1,0:T(8,128)(2,1)} %fusion.pool, ...), custom_call_target="tpu_custom_call", output_to_operand_aliasing={{1}: (4, {})} | custom-call | bytes 72000 | tf_op jit(solution)/shard_map/look_sums/pallas_call | solution.py:130
  64.2 3.7 %all-to-all-start = ((f32[4,76,8,128]{3,2,1,0:T(8,128)}), f32[4,76,8,128]{3,2,1,0:T(8,128)S(1)}, u32[]{:S(2)}, u32[]{:S(2)}) async-start(f32[4,76,8,128]{3,2,1,0:T(8,128)} %get-tuple-element.30), calls=%async_computation | async-start | bytes 2490368 | tf_op jit(solution)/shard_map/all_to_all | solution.py:455
  68.1 2.0 %window_bands.1.bands = bf16[768,256]{1,0:T(8,128)(2,1)} custom-call(s32[9]{0:T(128)} %row_off.1, s32[9]{0:T(128)} %col_off.1, s32[1]{0:T(128)} %bitcast.14.flip), custom_call_target="tpu_custom_call" | custom-call | bytes 3600000 | tf_op jit(solution)/shard_map/window_bands/pallas_call | solution.py:285
  70.0 1.9 %collective-permute-start.4 = (f32[3,576,128]{2,1,0:T(8,128)S(1)}, f32[3,576,128]{2,1,0:T(8,128)}, u32[]{:S(2)}, u32[]{:S(2)}) collective-permute-start(f32[3,576,128]{2,1,0:T(8,128)S(1)} %collective-permute-done.3.refs_0_.mate), channel_id=1, source_target_pairs={{0,2},{2,4},{3,1},{4,6},{5,3},{6,8},{7,5},{8,10},{9,7},{10,12},{11... | collective-permute-start | bytes 2654216 | tf_op jit(solution)/shard_map/ppermute | solution.py:464
  71.9 6.0 %collective-permute-start.5 = (f32[3,576,128]{2,1,0:T(8,128)}, f32[3,576,128]{2,1,0:T(8,128)}, u32[]{:S(2)}, u32[]{:S(2)}) collective-permute-start(f32[3,576,128]{2,1,0:T(8,128)} %get-tuple-element.29.own), channel_id=1, source_target_pairs={{1,3},{2,0},{3,5},{4,2},{5,7},{6,4},{7,9},{8,6},{9,11},{10,8},{11,... | collective-permute-start | bytes 2654216 | tf_op jit(solution)/shard_map/ppermute | solution.py:453
  79.0 4.9 %window_coherence.2 = (f32[640,128]{1,0:T(8,128)S(1)}, f32[640,128]{1,0:T(8,128)}) custom-call(f32[3,640,128]{2,1,0:T(8,128)} %collective-permute-done.1.near, f32[3,640,128]{2,1,0:T(8,128)S(1)} %copy-done.3, f32[3,640,128]{2,1,0:T(8,128)} %collective-permute-done.mate.refs_1_, f32[3,640,128]{2,1,0:T(8,128)} %collective-permute-done.2.far, ...), custom_call_target="tpu_custom_call" | custom-call | bytes 72000 | tf_op jit(solution)/shard_map/window_coherence/pallas_call | solution.py:195
  86.0 18.9 %network_solve.1 = (f32[160,304]{1,0:T(8,128)S(1)}, f32[304,160]{1,0:T(8,128)S(1)}) custom-call(s32[1]{0:T(128)} %bitcast.14.flip, s32[2,304]{1,0:T(2,128)S(1)} %select_n.26.dates, f32[3,576,128]{2,1,0:T(8,128)S(1)} %collective-permute-done.3.refs_0_.mate, f32[640,128]{1,0:T(8,128)} %get-tuple-element.31.refs_1_), custom_call_target="tpu_custom_call" | custom-call | bytes 72000 | tf_op jit(solution)/shard_map/network_solve/pallas_call | solution.py:349
  105.0 3.4 %invert.1 = (f32[76,8,128]{2,1,0:T(8,128)S(1)}, f32[76,8,128]{2,1,0:T(8,128)S(1)}, f32[76,8,128]{2,1,0:T(8,128)S(1)}, f32[76,8,128]{2,1,0:T(8,128)S(1)}, f32[1024,159]{1,0:T(8,128)}) custom-call(s32[1]{0:T(128)} %bitcast.17.group, f32[4,76,8,128]{3,2,1,0:T(8,128)S(1)} %all-to-all-done.looked, f32[160,304]{1,0:T(8,128)S(1)} %get-tuple-element.32.inverse, ...), custom_call_target="tpu_custom_call" | custom-call | bytes 72000 | tf_op jit(solution)/shard_map/invert/pallas_call | solution.py:390
  110.5 8.5 %all-to-all-start.1 = ((f32[32,32,159]{2,1,0:T(8,128)}), f32[32,32,159]{2,1,0:T(8,128)}, u32[]{:S(2)}, u32[]{:S(2)}) async-start(f32[32,32,159]{2,1,0:T(8,128)} %bitcast.23), calls=%async_computation.1 | async-start | bytes 2097152 | tf_op jit(solution)/shard_map/all_to_all | solution.py:489
  119.1 1.9 %collective-permute-start.10 = (f32[76,8,128]{2,1,0:T(8,128)}, f32[76,8,128]{2,1,0:T(8,128)S(1)}, u32[]{:S(2)}, u32[]{:S(2)}) collective-permute-start(f32[76,8,128]{2,1,0:T(8,128)} %copy-done.9), channel_id=1, source_target_pairs={{0,96},{32,64},{64,32},{96,0},{1,97},{33,65},{65,33},{97,1},{2,98}... | collective-permute-start | bytes 933896 | tf_op jit(solution)/shard_map/ppermute | solution.py:474
  121.2 3.8 %window_coherence.3 = (f32[576,128]{1,0:T(8,128)S(1)}, f32[576,128]{1,0:T(8,128)S(1)}) custom-call(f32[3,576,128]{2,1,0:T(8,128)} %collective-permute-done.4.near, f32[3,576,128]{2,1,0:T(8,128)S(1)} %copy-done.4, f32[3,576,128]{2,1,0:T(8,128)S(1)} %collective-permute-done.3.refs_0_.mate, f32[3,576,128]{2,1,0:T(8,128)} %collective-permute-done.5.far, ...), custom_call_target="tpu_custom_call" | custom-call | bytes 72000 | tf_op jit(solution)/shard_map/window_coherence/pallas_call | solution.py:195
  125.0 3.5 %collective-permute-start.8 = (f32[576,128]{1,0:T(8,128)S(1)}, f32[576,128]{1,0:T(8,128)S(1)}, u32[]{:S(2)}, u32[]{:S(2)}) collective-permute-start(f32[576,128]{1,0:T(8,128)S(1)} %get-tuple-element.37), channel_id=1, source_target_pairs={{0,1},{1,0},{2,3},{3,2},{4,5},{5,4},{6,7},{7,6},{8,9},{9,8},{10,11... | collective-permute-start | bytes 884744 | tf_op jit(solution)/shard_map/ppermute | solution.py:480
  128.6 24.1 %collective-permute-done.8 = f32[576,128]{1,0:T(8,128)S(1)} collective-permute-done((f32[576,128]{1,0:T(8,128)S(1)}, f32[576,128]{1,0:T(8,128)S(1)}, u32[]{:S(2)}, u32[]{:S(2)}) %collective-permute-start.8) | collective-permute-done | bytes 294944 | tf_op jit(solution)/shard_map/ppermute | solution.py:480
  152.7 1.1 merge.1.refs_4_
  153.9 1.3 copy-done
  155.1 1.7 %unslot.1 = f32[75,4,8,128]{3,2,1,0:T(8,128)} custom-call(s32[2]{0:T(128)S(1)} %pad_add_fusion.where, f32[76,8,128]{2,1,0:T(8,128)S(1)} %get-tuple-element.38.refs_0_, f32[76,8,128]{2,1,0:T(8,128)S(1)} %collective-permute-done.7.refs_0_.refs_1_, f32[76,8,128]{2,1,0:T(8,128)S(1)} %collective-permute-done.9.refs_2_, ...), custom_call_target="tpu_custom_call" | custom-call | bytes 180000000 | tf_op jit(solution)/shard_map/unslot/pallas_call | solution.py:254
  156.9 2.3 %copy.25 = f32[159,32,32]{0,2,1:T(8,128)} copy(f32[159,32,32]{0,2,1:T(8,128)} %bitcast.24) | data formatting | bytes 1302528
  (51 shorter events, 6.2 us)
Async XLA Ops:
  15.3 34.9 %collective-permute-start = (f32[3,640,128]{2,1,0:T(8,128)}, f32[3,640,128]{2,1,0:T(8,128)}, u32[]{:S(2)}, u32[]{:S(2)}) collective-permute-start(f32[3,640,128]{2,1,0:T(8,128)} %get-tuple-element.22), channel_id=1, source_target_pairs={{0,1},{1,0},{2,3},{3,2},{4,5},{5,4},{6,7},{7,6},{8,9},{9,8},{10,11... | collective-permute-start | bytes 2949128 | tf_op jit(solution)/shard_map/ppermute | solution.py:440
  30.5 39.5 %collective-permute-start.3 = (f32[3,576,128]{2,1,0:T(8,128)}, f32[3,576,128]{2,1,0:T(8,128)S(1)}, u32[]{:S(2)}, u32[]{:S(2)}) collective-permute-start(f32[3,576,128]{2,1,0:T(8,128)} %get-tuple-element.27), channel_id=1, source_target_pairs={{0,1},{1,0},{2,3},{3,2},{4,5},{5,4},{6,7},{7,6},{8,9},{9,8},{10,11... | collective-permute-start | bytes 2654216 | tf_op jit(solution)/shard_map/ppermute | solution.py:444
  44.0 34.0 %collective-permute-start.2 = (f32[3,640,128]{2,1,0:T(8,128)}, f32[3,640,128]{2,1,0:T(8,128)}, u32[]{:S(2)}, u32[]{:S(2)}) collective-permute-start(f32[3,640,128]{2,1,0:T(8,128)} %get-tuple-element.25.own), channel_id=1, source_target_pairs={{1,3},{2,0},{3,5},{4,2},{5,7},{6,4},{7,9},{8,6},{9,11},{10,8},{11,... | collective-permute-start | bytes 2949128 | tf_op jit(solution)/shard_map/ppermute | solution.py:448
  50.2 27.8 %collective-permute-start.1 = (f32[3,640,128]{2,1,0:T(8,128)}, f32[3,640,128]{2,1,0:T(8,128)}, u32[]{:S(2)}, u32[]{:S(2)}) collective-permute-start(f32[3,640,128]{2,1,0:T(8,128)} %collective-permute-done.mate.refs_1_), channel_id=1, source_target_pairs={{0,2},{2,4},{3,1},{4,6},{5,3},{6,8},{7,5},{8,10},{9,7},{10,12},{11... | collective-permute-start | bytes 2949128 | tf_op jit(solution)/shard_map/ppermute | solution.py:454
  64.2 3.7 %copy-start.11 = (s32[300]{0:T(512)S(1)}, s32[300]{0:T(512)}, u32[]{:S(2)}) copy-start(s32[300]{0:T(512)} %param.8) | copy-start | bytes 3604
  64.2 3.8 %copy-start.12 = (s32[300]{0:T(512)S(1)}, s32[300]{0:T(512)}, u32[]{:S(2)}) copy-start(s32[300]{0:T(512)} %param.9) | copy-start | bytes 3604
  64.2 13.8 %copy-start.3 = (f32[3,640,128]{2,1,0:T(8,128)S(1)}, f32[3,640,128]{2,1,0:T(8,128)}, u32[]{:S(2)}) copy-start(f32[3,640,128]{2,1,0:T(8,128)} %get-tuple-element.25.own) | copy-start | bytes 2949124
  64.2 40.7 %all-to-all-start = ((f32[4,76,8,128]{3,2,1,0:T(8,128)}), f32[4,76,8,128]{3,2,1,0:T(8,128)S(1)}, u32[]{:S(2)}, u32[]{:S(2)}) async-start(f32[4,76,8,128]{3,2,1,0:T(8,128)} %get-tuple-element.30), calls=%async_computation | async-start | bytes 2490368 | tf_op jit(solution)/shard_map/all_to_all | solution.py:455
  70.0 51.2 %collective-permute-start.4 = (f32[3,576,128]{2,1,0:T(8,128)S(1)}, f32[3,576,128]{2,1,0:T(8,128)}, u32[]{:S(2)}, u32[]{:S(2)}) collective-permute-start(f32[3,576,128]{2,1,0:T(8,128)S(1)} %collective-permute-done.3.refs_0_.mate), channel_id=1, source_target_pairs={{0,2},{2,4},{3,1},{4,6},{5,3},{6,8},{7,5},{8,10},{9,7},{10,12},{11... | collective-permute-start | bytes 2654216 | tf_op jit(solution)/shard_map/ppermute | solution.py:464
  71.9 49.3 %collective-permute-start.5 = (f32[3,576,128]{2,1,0:T(8,128)}, f32[3,576,128]{2,1,0:T(8,128)}, u32[]{:S(2)}, u32[]{:S(2)}) collective-permute-start(f32[3,576,128]{2,1,0:T(8,128)} %get-tuple-element.29.own), channel_id=1, source_target_pairs={{1,3},{2,0},{3,5},{4,2},{5,7},{6,4},{7,9},{8,6},{9,11},{10,8},{11,... | collective-permute-start | bytes 2654216 | tf_op jit(solution)/shard_map/ppermute | solution.py:453
  78.0 1.0 copy-start.1
  84.0 0.7 copy-start.5
  84.7 20.3 %collective-permute-start.6 = (f32[640,128]{1,0:T(8,128)}, f32[640,128]{1,0:T(8,128)S(1)}, u32[]{:S(2)}, u32[]{:S(2)}) collective-permute-start(f32[640,128]{1,0:T(8,128)} %get-tuple-element.31.refs_1_), channel_id=1, source_target_pairs={{0,1},{1,0},{2,3},{3,2},{4,5},{5,4},{6,7},{7,6},{8,9},{9,8},{10,11... | collective-permute-start | bytes 983048 | tf_op jit(solution)/shard_map/ppermute | solution.py:468
  108.4 0.7 copy-start.7
  109.8 11.4 %copy-start.2 = (bf16[768,256]{1,0:T(8,128)(2,1)S(1)}, bf16[768,256]{1,0:T(8,128)(2,1)}, u32[]{:S(2)}) copy-start(bf16[768,256]{1,0:T(8,128)(2,1)} %window_bands.1.bands) | copy-start | bytes 1179652
  109.8 11.4 %copy-start.4 = (f32[3,576,128]{2,1,0:T(8,128)S(1)}, f32[3,576,128]{2,1,0:T(8,128)}, u32[]{:S(2)}) copy-start(f32[3,576,128]{2,1,0:T(8,128)} %get-tuple-element.29.own) | copy-start | bytes 2654212
  110.5 10.4 %copy-start.8 = (f32[76,8,128]{2,1,0:T(8,128)S(1)}, f32[76,8,128]{2,1,0:T(8,128)}, u32[]{:S(2)}) copy-start(f32[76,8,128]{2,1,0:T(8,128)} %copy-done.7) | copy-start | bytes 933892
  110.5 46.4 %all-to-all-start.1 = ((f32[32,32,159]{2,1,0:T(8,128)}), f32[32,32,159]{2,1,0:T(8,128)}, u32[]{:S(2)}, u32[]{:S(2)}) async-start(f32[32,32,159]{2,1,0:T(8,128)} %bitcast.23), calls=%async_computation.1 | async-start | bytes 2097152 | tf_op jit(solution)/shard_map/all_to_all | solution.py:489
  119.0 2.2 %collective-permute-start.7 = (f32[76,8,128]{2,1,0:T(8,128)}, f32[76,8,128]{2,1,0:T(8,128)S(1)}, u32[]{:S(2)}, u32[]{:S(2)}) collective-permute-start(f32[76,8,128]{2,1,0:T(8,128)} %copy-done.10), channel_id=1, source_target_pairs={{0,32},{32,0},{64,96},{96,64},{1,33},{33,1},{65,97},{97,65},{2,34}... | collective-permute-start | bytes 933896 | tf_op jit(solution)/shard_map/ppermute | solution.py:474
  119.1 34.8 %collective-permute-start.10 = (f32[76,8,128]{2,1,0:T(8,128)}, f32[76,8,128]{2,1,0:T(8,128)S(1)}, u32[]{:S(2)}, u32[]{:S(2)}) collective-permute-start(f32[76,8,128]{2,1,0:T(8,128)} %copy-done.9), channel_id=1, source_target_pairs={{0,96},{32,64},{64,32},{96,0},{1,97},{33,65},{65,33},{97,1},{2,98}... | collective-permute-start | bytes 933896 | tf_op jit(solution)/shard_map/ppermute | solution.py:474
  120.9 31.8 %copy-start.6 = (f32[640,128]{1,0:T(8,128)S(1)}, f32[640,128]{1,0:T(8,128)}, u32[]{:S(2)}) copy-start(f32[640,128]{1,0:T(8,128)} %copy-done.5) | copy-start | bytes 983044
  120.9 32.9 %collective-permute-start.9 = (f32[76,8,128]{2,1,0:T(8,128)S(1)}, f32[76,8,128]{2,1,0:T(8,128)S(1)}, u32[]{:S(2)}, u32[]{:S(2)}) collective-permute-start(f32[76,8,128]{2,1,0:T(8,128)S(1)} %copy-done.8), channel_id=1, source_target_pairs={{0,64},{32,96},{64,0},{96,32},{1,65},{33,97},{65,1},{97,33},{2,66}... | collective-permute-start | bytes 933896 | tf_op jit(solution)/shard_map/ppermute | solution.py:474
  125.0 27.7 %collective-permute-start.8 = (f32[576,128]{1,0:T(8,128)S(1)}, f32[576,128]{1,0:T(8,128)S(1)}, u32[]{:S(2)}, u32[]{:S(2)}) collective-permute-start(f32[576,128]{1,0:T(8,128)S(1)} %get-tuple-element.37), channel_id=1, source_target_pairs={{0,1},{1,0},{2,3},{3,2},{4,5},{5,4},{6,7},{7,6},{8,9},{9,8},{10,11... | collective-permute-start | bytes 884744 | tf_op jit(solution)/shard_map/ppermute | solution.py:480
  153.9 1.3 copy-start
  (2 other events, 1.4 us)

commit v4 on v3

--- a/solution.py
+++ b/solution.py
@@ -3,6 +3,7 @@
 
 import jax
 import jax.numpy as jnp
+import numpy as np
 from jax import lax
 from jax.experimental import pallas as pl
 from jax.experimental.pallas import tpu as pltpu
@@ -41,9 +42,8 @@
 
 
 def pooling_matrix():
-    row = lax.broadcasted_iota(jnp.int32, (LANES * RG_LOOKS, LANES), 0)
-    col = lax.broadcasted_iota(jnp.int32, (LANES * RG_LOOKS, LANES), 1)
-    return (row // RG_LOOKS == col).astype(jnp.bfloat16)
+    look = np.arange(LANES * RG_LOOKS) // RG_LOOKS
+    return jnp.asarray(look[:, None] == np.arange(LANES), jnp.bfloat16)
 
 
 def lasting(us):
@@ -154,9 +154,13 @@
     )(start, *operands)
 
 
-def window_kernel(near, own, mate, far, bands, *refs):
-    own_out, mate_out, parts = refs[-3:]
+def window_kernel(row_off, col_off, flip, near, own, mate, far, *refs):
+    own_out, mate_out, parts, bands = refs[-4:]
     rows = own.shape[1]
+
+    @pl.when(pl.program_id(0) == 0)
+    def _():
+        window_bands(row_off, col_off, flip, bands)
 
     def divide(g, carry):
         r = pl.ds(pl.multiple_of(g * 32, 32), 32)
@@ -187,7 +191,7 @@
         out[...] = jnp.sqrt(re * re + im * im) / w
 
 
-def window_coherence(bands, near, own, mate, far, after=()):
+def window_coherence(offsets, near, own, mate, far, after=()):
     count = mate.shape[1]
     rows = count // 2
     part = pl.BlockSpec((3, rows, LANES), lambda i: (0, i, 0))
@@ -195,19 +199,23 @@
     return pl.pallas_call(
         window_kernel,
         grid=(2,),
-        in_specs=[part] * 4
-        + [pl.BlockSpec(bands.shape, lambda i: (0, 0))]
+        in_specs=[pl.BlockSpec(memory_space=pltpu.SMEM)] * 3
+        + [part] * 4
         + [pl.BlockSpec(memory_space=pl.ANY)] * len(after),
         out_specs=[out, out],
         out_shape=[jax.ShapeDtypeStruct((count, LANES), jnp.float32)] * 2,
-        scratch_shapes=[pltpu.VMEM((3, rows, 8 * LANES), jnp.bfloat16)],
+        scratch_shapes=[
+            pltpu.VMEM((3, rows, 8 * LANES), jnp.bfloat16),
+            pltpu.VMEM((6 * LANES, 2 * LANES), jnp.bfloat16),
+        ],
         compiler_params=pltpu.CompilerParams(vmem_limit_bytes=40 * 1024 * 1024),
         cost_estimate=lasting(0.02),
         name="window_coherence",
-    )(near, own, mate, far, bands, *after)
-
-
-def merge_kernel(odd, own_a, own_b, other_a, other_b, out):
+    )(*offsets, near, own, mate, far, *after)
+
+
+def merge_kernel(odd, own_a, own_b, other_a, other_b, *refs):
+    out = refs[-1]
     first, share = own_a.shape[0], own_a.shape[0] + own_b.shape[0]
 
     @pl.when(odd[0] == 0)
@@ -225,17 +233,18 @@
         out[share + first - 1 :] = own_b[...]
 
 
-def merge(odd, ifgs, *parts):
+def merge(odd, ifgs, *parts, after):
     vmem = pl.BlockSpec(memory_space=pltpu.VMEM)
     return pl.pallas_call(
         merge_kernel,
-        in_specs=[pl.BlockSpec(memory_space=pltpu.SMEM)] + [vmem] * 4,
+        in_specs=[pl.BlockSpec(memory_space=pltpu.SMEM)] + [vmem] * 4
+        + [pl.BlockSpec(memory_space=pl.ANY)] * len(after),
         out_specs=vmem,
         out_shape=jax.ShapeDtypeStruct((ifgs, *parts[0].shape[1:]), jnp.float32),
         compiler_params=pltpu.CompilerParams(vmem_limit_bytes=8 * 1024 * 1024),
         cost_estimate=lasting(0.3),
         name="merge",
-    )(odd, *parts)
+    )(odd, *parts, *after)
 
 
 def unslot_kernel(where, *refs):
@@ -263,7 +272,7 @@
     )(where, *parts, *after)
 
 
-def bands_kernel(row_off, col_off, flip, bands):
+def window_bands(row_off, col_off, flip, bands):
     gap = lax.broadcasted_iota(jnp.int32, (LANES, LANES), 1) - lax.broadcasted_iota(
         jnp.int32, (LANES, LANES), 0
     )
@@ -279,17 +288,6 @@
             rows = slice((2 * e + half) * LANES, (2 * e + half + 1) * LANES)
             bands[rows, :LANES] = same.astype(jnp.bfloat16)
             bands[rows, LANES:] = next_to.astype(jnp.bfloat16)
-
-
-def window_bands(row_off, col_off, flip):
-    return pl.pallas_call(
-        bands_kernel,
-        in_specs=[pl.BlockSpec(memory_space=pltpu.SMEM)] * 3,
-        out_specs=pl.BlockSpec(memory_space=pltpu.VMEM),
-        out_shape=jax.ShapeDtypeStruct((6 * LANES, 2 * LANES), jnp.bfloat16),
-        cost_estimate=lasting(1),
-        name="window_bands",
-    )(row_off, col_off, flip)
 
 
 def network_kernel(
@@ -323,11 +321,11 @@
             picked = lane == here
             lines = [grid[t, pl.ds(k, 1), :] for t in tiles]
             values = [grid[t, :rows, :] for t in tiles]
-            scale = 1.0 / jnp.sum(jnp.where(picked, lines[half], 0.0), axis=1, keepdims=True)
+            index = jnp.full((rows, LANES), here, jnp.int32)
+            column = jnp.take_along_axis(values[half], index, axis=1)
+            scale = 1.0 / jnp.take_along_axis(jnp.broadcast_to(lines[half], (8, LANES)), index[:8], axis=1)[:1]
             lines = [line * scale for line in lines]
             lines[half] = jnp.where(picked, -scale, lines[half])
-            index = jnp.full((rows, LANES), here, jnp.int32)
-            column = jnp.take_along_axis(values[half], index, axis=1)
             values[half] = jnp.where(picked, 0.0, values[half])
             for t in tiles:
                 grid[t, :rows, :] = values[t] - column * lines[t]
@@ -374,7 +372,15 @@
         return jnp.dot(a, b, precision=lax.Precision.HIGHEST, preferred_element_type=jnp.float32)
 
     solved = product(inverse[...], phase)
-    history[...] = jnp.transpose(solved)[:, : DATES - 1]
+    blocks = history.shape[0]
+    history[:, :32] = jnp.transpose(solved[:LANES]).reshape(blocks, 32, LANES)
+    last = DATES - LANES
+    rest = jnp.concatenate([solved[LANES:], jnp.zeros((LANES - last, 8 * LANES), jnp.float32)])
+    rest = jnp.transpose(rest).reshape(blocks, 4, 8, LANES)
+    packed = rest[:, 0]
+    for b in range(1, 4):
+        packed = packed + pltpu.roll(rest[:, b], b * last, 2)
+    history[:, 32:] = packed
     rest = phase - product(design[...], solved)
     lines = held.reshape(count * 8, LANES)
     for j in range(8):
@@ -393,7 +399,7 @@
         + [vmem] * 3
         + [pl.BlockSpec(memory_space=pl.ANY)] * len(after),
         out_specs=[vmem] * (GROUPS + 1),
-        out_shape=[part] * GROUPS + [jax.ShapeDtypeStruct((8 * LANES, DATES - 1), jnp.float32)],
+        out_shape=[part] * GROUPS + [jax.ShapeDtypeStruct((8 * LANES // 32, 40, LANES), jnp.float32)],
         scratch_shapes=[
             pltpu.VMEM((GROUPS * slots, 8 * LANES), jnp.float32),
             pltpu.VMEM((GROUPS * slots, 8, LANES), jnp.float32),
@@ -402,6 +408,28 @@
         cost_estimate=lasting(0.02),
         name="invert",
     )(group, looked, inverse, design, *after)
+
+
+def unpack_kernel(held, out):
+    last = DATES - LANES
+    out[:, :, :LANES] = held[:, :32]
+    packed = held[:, 32:]
+    for b in range(4):
+        value = packed if b == 0 else pltpu.roll(packed, LANES - b * last, 2)
+        out[:, 8 * b : 8 * (b + 1), LANES:] = value[:, :, : last - 1]
+
+
+def unpack(held):
+    vmem = pl.BlockSpec(memory_space=pltpu.VMEM)
+    return pl.pallas_call(
+        unpack_kernel,
+        in_specs=[vmem],
+        out_specs=vmem,
+        out_shape=jax.ShapeDtypeStruct((held.shape[0], 32, DATES - 1), jnp.float32),
+        compiler_params=pltpu.CompilerParams(vmem_limit_bytes=8 * 1024 * 1024),
+        cost_estimate=lasting(0.3),
+        name="unpack",
+    )(held)
 
 
 def tiles(samples):
@@ -460,10 +488,10 @@
         jnp.concatenate([dates[:, :, rest:], dates[:, :, :share]], axis=2),
         jnp.concatenate([dates[:, :, :share], dates[:, :, rest:]], axis=2),
     ).reshape(2, -1)
-    bands = window_bands(window_rows, window_cols, flip)
+    offsets = (window_rows, window_cols, flip)
     near_b = lax.ppermute(mate_b, "rows", across)
     own_part_a, mate_part_a = window_coherence(
-        bands, near_a, own_a, mate_a, far_a
+        offsets, near_a, own_a, mate_a, far_a
     )
     back_a = lax.ppermute(mate_part_a, "rows", mates)
     inverse, design = network_solve(flip, dates, slots, (mate_b, mate_part_a))
@@ -475,20 +503,20 @@
         for d in range(1, GROUPS)
     ]
     own_part_b, mate_part_b = window_coherence(
-        bands, near_b, own_b, mate_b, far_b, after=(residual[1], history)
+        offsets, near_b, own_b, mate_b, far_b, after=(residual[1], history)
     )
     back_b = lax.ppermute(mate_part_b, "rows", mates)
 
+    residual = unslot(jnp.stack([odd, group]), ifgs, residual, ())
     by_ifg = (-1, 32, LANES)
     coherence = merge(
-        side, ifgs, *[part.reshape(by_ifg) for part in (own_part_a, own_part_b, back_a, back_b)]
-    )
-
-    residual = unslot(jnp.stack([odd, group]), ifgs, residual, (coherence,))
-    history = history.reshape(row_count, -1, DATES - 1)
+        side, ifgs, *[part.reshape(by_ifg) for part in (own_part_a, own_part_b, back_a, back_b)],
+        after=(residual,),
+    )
+
     history = lax.all_to_all(history, "rows", split_axis=0, concat_axis=0, tiled=True)
     shape = (ifgs, 1, 32 * LANES)
-    return (coherence.reshape(shape), residual.reshape(shape), history.transpose(2, 0, 1))
+    return (coherence.reshape(shape), residual.reshape(shape), unpack(history).transpose(2, 0, 1))
 
 
 def solution(mesh):

time: 160 us -> 150 us (0.938)
  waiting for transfers between devices: 24.2 us -> 19.5 us
  Pallas kernels: 86.2 us -> 82.8 us
  starting transfers between devices: 38.5 us -> 36.6 us
    ppermute x1, waiting for transfers between devices: 24.1 us -> 5.54 us  [local(): back_b = lax.ppermute(mate_part_b, 'rows', mates)]
    ppermute x3, waiting for transfers between devices: 0.01 us -> 11.3 us  [local(): lax.ppermute(residual[d], 'ifg', [(i, i ^ d) for i in range(GROUPS)])]
    pallas_call x1, Pallas kernels: 18.9 us -> 15.3 us  [network_solve(): pl.pallas_call(functools.partial(network_kernel, slots=slots), in_specs=[...]
    ppermute x1, waiting for transfers between devices: 0.01 us -> 2.65 us  [local(): near_a = lax.ppermute(mate_a, 'rows', across)]
    unnamed x28 -> x35, local copies, waits for them, and re-layouts: 7.49 us -> 7.54 us
  transfers between devices with their start and end apart: 13 -> 13, of which waited for: 1 -> 4; matrix products, arithmetic and copies ran while one was open for 0% -> 0% of each run, Pallas kernels for 46% -> 46%
where the time goes in v4:
time: 150 us; the launch traced here: 148 us
  Pallas kernels  82.8 us (55%)
  starting transfers between devices  36.6 us (24%)
  waiting for transfers between devices  19.5 us (13%)
  local copies, waits for them, and re-layouts  7.88 us (5%)
    pallas_call x4, Pallas kernels, look_sums(): pl.pallas_call(look_kernel, grid_spec=pltpu.PrefetchScalarGridSpec(num_sc...  50.3 us
    pallas_call x1, Pallas kernels, network_solve(): pl.pallas_call(functools.partial(network_kernel, slots=slots), in_specs=[...  15.3 us
    ppermute x3, waiting for transfers between devices, local(): lax.ppermute(residual[d], 'ifg', [(i, i ^ d) for i in range(GROUPS)])  11.3 us
    pallas_call x2, Pallas kernels, window_coherence(): pl.pallas_call(window_kernel, grid=(2,), in_specs=[pl.BlockSpec(memory_sp...  9.89 us
    all_to_all x1, starting transfers between devices, local(): lax.all_to_all(history, 'rows', split_axis=0, concat_axis=0, tiled=True)  7.67 us
    unnamed x35, local copies, waits for them, and re-layouts  7.54 us
    ppermute x1, starting transfers between devices, local(): far_a = lax.ppermute(own_a, 'rows', outward)  6.2 us
    ppermute x1, starting transfers between devices, local(): far_b = lax.ppermute(own_b, 'rows', outward)  6.03 us
  transfers between devices with their start and end apart: 13, of which 4 were waited for; matrix products, arithmetic and copies ran while one was open for 0% of the time, Pallas kernels for 46%

profile of v4, /device:TPU:6, one launch (start us, length us, event | category | flops | bytes accessed | tf_op | source)
XLA Modules:
  0.0 147.7 jit_solution(1319689410381284270)
XLA Ops:
  0.6 13.2 %look_sums.4 = (f32[3,640,128]{2,1,0:T(8,128)}, f32[4,76,8,128]{3,2,1,0:T(8,128)}) custom-call(s32[1]{0:T(128)} %bitcast.2.start, bf16[2400,16,128]{2,1,0:T(8,128)(2,1)} %bitcast.29, bf16[2400,16,128]{2,1,0:T(8,128)(2,1)} %bitcast.33, bf16[1024,128]{1,0:T(8,128)(2,1)} %constant.23.clone.pool), custom_call_target="tpu_custom_call" | custom-call | bytes 72000 | tf_op jit(solution)/shard_map/look_sums/pallas_call | solution.py:130
  13.8 3.2 %collective-permute-start = (f32[3,640,128]{2,1,0:T(8,128)}, f32[3,640,128]{2,1,0:T(8,128)}, u32[]{:S(2)}, u32[]{:S(2)}) collective-permute-start(f32[3,640,128]{2,1,0:T(8,128)} %get-tuple-element.22), channel_id=1, source_target_pairs={{0,1},{1,0},{2,3},{3,2},{4,5},{5,4},{6,7},{7,6},{8,9},{9,8},{10,11... | collective-permute-start | bytes 2949128 | tf_op jit(solution)/shard_map/ppermute | solution.py:468
  17.0 12.0 %look_sums.5 = (f32[3,576,128]{2,1,0:T(8,128)}, f32[4,76,8,128]{3,2,1,0:T(8,128)}) custom-call(s32[1]{0:T(128)} %bitcast.14.start, bf16[2400,16,128]{2,1,0:T(8,128)(2,1)} %bitcast.30, bf16[2400,16,128]{2,1,0:T(8,128)(2,1)} %bitcast.34, bf16[1024,128]{1,0:T(8,128)(2,1)} %constant.23.clone.pool, ...), custom_call_target="tpu_custom_call", output_to_operand_aliasing={{1}: (4, {})} | custom-call | bytes 72000 | tf_op jit(solution)/shard_map/look_sums/pallas_call | solution.py:130
  29.3 13.1 %look_sums.6 = (f32[3,640,128]{2,1,0:T(8,128)}, f32[4,76,8,128]{3,2,1,0:T(8,128)}) custom-call(s32[1]{0:T(128)} %bitcast.9.start, bf16[2400,16,128]{2,1,0:T(8,128)(2,1)} %bitcast.31, bf16[2400,16,128]{2,1,0:T(8,128)(2,1)} %bitcast.35, bf16[1024,128]{1,0:T(8,128)(2,1)} %constant.23.clone.pool, ...), custom_call_target="tpu_custom_call", output_to_operand_aliasing={{1}: (4, {})} | custom-call | bytes 72000 | tf_op jit(solution)/shard_map/look_sums/pallas_call | solution.py:130
  42.5 6.2 %collective-permute-start.2 = (f32[3,640,128]{2,1,0:T(8,128)}, f32[3,640,128]{2,1,0:T(8,128)}, u32[]{:S(2)}, u32[]{:S(2)}) collective-permute-start(f32[3,640,128]{2,1,0:T(8,128)} %get-tuple-element.25.own), channel_id=1, source_target_pairs={{1,3},{2,0},{3,5},{4,2},{5,7},{6,4},{7,9},{8,6},{9,11},{10,8},{11,... | collective-permute-start | bytes 2949128 | tf_op jit(solution)/shard_map/ppermute | solution.py:476
  48.7 1.9 %collective-permute-start.1 = (f32[3,640,128]{2,1,0:T(8,128)}, f32[3,640,128]{2,1,0:T(8,128)}, u32[]{:S(2)}, u32[]{:S(2)}) collective-permute-start(f32[3,640,128]{2,1,0:T(8,128)} %collective-permute-done.mate.refs_1_), channel_id=1, source_target_pairs={{0,2},{2,4},{3,1},{4,6},{5,3},{6,8},{7,5},{8,10},{9,7},{10,12},{11... | collective-permute-start | bytes 2949128 | tf_op jit(solution)/shard_map/ppermute | solution.py:482
  50.6 12.0 %look_sums.7 = (f32[3,576,128]{2,1,0:T(8,128)}, f32[4,76,8,128]{3,2,1,0:T(8,128)}) custom-call(s32[1]{0:T(128)} %bitcast.16.start, bf16[2400,16,128]{2,1,0:T(8,128)(2,1)} %bitcast.32, bf16[2400,16,128]{2,1,0:T(8,128)(2,1)} %bitcast.36, bf16[1024,128]{1,0:T(8,128)(2,1)} %constant.23.clone.pool, ...), custom_call_target="tpu_custom_call", output_to_operand_aliasing={{1}: (4, {})} | custom-call | bytes 72000 | tf_op jit(solution)/shard_map/look_sums/pallas_call | solution.py:130
  62.7 3.7 %all-to-all-start = ((f32[4,76,8,128]{3,2,1,0:T(8,128)}), f32[4,76,8,128]{3,2,1,0:T(8,128)S(1)}, u32[]{:S(2)}, u32[]{:S(2)}) async-start(f32[4,76,8,128]{3,2,1,0:T(8,128)} %get-tuple-element.30), calls=%async_computation | async-start | bytes 2490368 | tf_op jit(solution)/shard_map/all_to_all | solution.py:483
  66.6 1.9 %collective-permute-start.4 = (f32[3,576,128]{2,1,0:T(8,128)S(1)}, f32[3,576,128]{2,1,0:T(8,128)}, u32[]{:S(2)}, u32[]{:S(2)}) collective-permute-start(f32[3,576,128]{2,1,0:T(8,128)S(1)} %collective-permute-done.3.refs_0_.mate), channel_id=1, source_target_pairs={{0,2},{2,4},{3,1},{4,6},{5,3},{6,8},{7,5},{8,10},{9,7},{10,12},{11... | collective-permute-start | bytes 2654216 | tf_op jit(solution)/shard_map/ppermute | solution.py:492
  68.5 6.0 %collective-permute-start.5 = (f32[3,576,128]{2,1,0:T(8,128)}, f32[3,576,128]{2,1,0:T(8,128)}, u32[]{:S(2)}, u32[]{:S(2)}) collective-permute-start(f32[3,576,128]{2,1,0:T(8,128)} %get-tuple-element.29.own), channel_id=1, source_target_pairs={{1,3},{2,0},{3,5},{4,2},{5,7},{6,4},{7,9},{8,6},{9,11},{10,8},{11,... | collective-permute-start | bytes 2654216 | tf_op jit(solution)/shard_map/ppermute | solution.py:481
  74.6 2.7 %collective-permute-done.1.near = f32[3,640,128]{2,1,0:T(8,128)} collective-permute-done((f32[3,640,128]{2,1,0:T(8,128)}, f32[3,640,128]{2,1,0:T(8,128)}, u32[]{:S(2)}, u32[]{:S(2)}) %collective-permute-start.1) | collective-permute-done | bytes 983072 | tf_op jit(solution)/shard_map/ppermute | solution.py:482
  77.2 5.5 %window_coherence.2 = (f32[640,128]{1,0:T(8,128)S(1)}, f32[640,128]{1,0:T(8,128)}) custom-call(s32[9]{0:T(128)S(1)} %copy-done.11, s32[9]{0:T(128)S(1)} %copy-done.12, s32[1]{0:T(128)} %bitcast.1.flip, f32[3,640,128]{2,1,0:T(8,128)} %collective-permute-done.1.near, f32[3,640,128]{2,1,0:T(8,128)S(1)} %copy-done.1, ...), custom_call_target="tpu_custom_call" | custom-call | bytes 72000 | tf_op jit(solution)/shard_map/window_coherence/pallas_call | solution.py:199
  83.7 15.3 %network_solve.1 = (f32[160,304]{1,0:T(8,128)S(1)}, f32[304,160]{1,0:T(8,128)S(1)}) custom-call(s32[1]{0:T(128)} %bitcast.1.flip, s32[2,304]{1,0:T(2,128)S(1)} %select_n.14.dates, f32[3,576,128]{2,1,0:T(8,128)S(1)} %collective-permute-done.3.refs_0_.mate, f32[640,128]{1,0:T(8,128)} %get-tuple-element.31.refs_1_), custom_call_target="tpu_custom_call" | custom-call | bytes 72000 | tf_op jit(solution)/shard_map/network_solve/pallas_call | solution.py:347
  102.4 3.2 %invert.1 = (f32[76,8,128]{2,1,0:T(8,128)S(1)}, f32[76,8,128]{2,1,0:T(8,128)}, f32[76,8,128]{2,1,0:T(8,128)S(1)}, f32[76,8,128]{2,1,0:T(8,128)S(1)}, f32[32,40,128]{2,1,0:T(8,128)}) custom-call(s32[1]{0:T(128)} %bitcast.17.group, f32[4,76,8,128]{3,2,1,0:T(8,128)S(1)} %all-to-all-done.looked, f32[160,304]{1,0:T(8,128)S(1)} %copy-done.10, ...), custom_call_target="tpu_custom_call" | custom-call | bytes 72000 | tf_op jit(solution)/shard_map/invert/pallas_call | solution.py:396
  107.8 7.7 %all-to-all-start.1 = ((f32[32,40,128]{2,1,0:T(8,128)}), f32[32,40,128]{2,1,0:T(8,128)S(1)}, u32[]{:S(2)}, u32[]{:S(2)}) async-start(f32[32,40,128]{2,1,0:T(8,128)} %get-tuple-element.35.refs_1_), calls=%async_computation.1 | async-start | bytes 1310720 | tf_op jit(solution)/shard_map/all_to_all | solution.py:517
  115.6 1.6 %collective-permute-start.10 = (f32[76,8,128]{2,1,0:T(8,128)}, f32[76,8,128]{2,1,0:T(8,128)S(1)}, u32[]{:S(2)}, u32[]{:S(2)}) collective-permute-start(f32[76,8,128]{2,1,0:T(8,128)} %copy-done.14), channel_id=1, source_target_pairs={{0,96},{32,64},{64,32},{96,0},{1,97},{33,65},{65,33},{97,1},{2,98}... | collective-permute-start | bytes 933896 | tf_op jit(solution)/shard_map/ppermute | solution.py:502
  117.7 4.4 %window_coherence.3 = (f32[576,128]{1,0:T(8,128)S(1)}, f32[576,128]{1,0:T(8,128)S(1)}) custom-call(s32[9]{0:T(128)S(1)} %copy-done.11, s32[9]{0:T(128)S(1)} %copy-done.12, s32[1]{0:T(128)} %bitcast.1.flip, f32[3,576,128]{2,1,0:T(8,128)} %collective-permute-done.4.near, f32[3,576,128]{2,1,0:T(8,128)S(1)} %copy-done.2, ...), custom_call_target="tpu_custom_call" | custom-call | bytes 72000 | tf_op jit(solution)/shard_map/window_coherence/pallas_call | solution.py:199
  122.1 3.4 %collective-permute-start.8 = (f32[576,128]{1,0:T(8,128)S(1)}, f32[576,128]{1,0:T(8,128)S(1)}, u32[]{:S(2)}, u32[]{:S(2)}) collective-permute-start(f32[576,128]{1,0:T(8,128)S(1)} %get-tuple-element.37), channel_id=1, source_target_pairs={{0,1},{1,0},{2,3},{3,2},{4,5},{5,4},{6,7},{7,6},{8,9},{9,8},{10,11... | collective-permute-start | bytes 884744 | tf_op jit(solution)/shard_map/ppermute | solution.py:508
  125.6 3.2 %collective-permute-done.10.refs_3_ = f32[76,8,128]{2,1,0:T(8,128)S(1)} collective-permute-done((f32[76,8,128]{2,1,0:T(8,128)}, f32[76,8,128]{2,1,0:T(8,128)S(1)}, u32[]{:S(2)}, u32[]{:S(2)}) %collective-permute-start.10) | collective-permute-done | bytes 311328 | tf_op jit(solution)/shard_map/ppermute | solution.py:502
  128.7 8.1 %collective-permute-done.9.refs_2_ = f32[76,8,128]{2,1,0:T(8,128)S(1)} collective-permute-done((f32[76,8,128]{2,1,0:T(8,128)}, f32[76,8,128]{2,1,0:T(8,128)S(1)}, u32[]{:S(2)}, u32[]{:S(2)}) %collective-permute-start.9) | collective-permute-done | bytes 311328 | tf_op jit(solution)/shard_map/ppermute | solution.py:502
  136.8 1.7 %unslot.1.refs_0_ = f32[75,4,8,128]{3,2,1,0:T(8,128)} custom-call(s32[2]{0:T(128)S(1)} %pad_add_fusion.where, f32[76,8,128]{2,1,0:T(8,128)S(1)} %copy-done.8, f32[76,8,128]{2,1,0:T(8,128)S(1)} %collective-permute-done.7.refs_0_.refs_1_, f32[76,8,128]{2,1,0:T(8,128)S(1)} %collective-permute-done.9.refs_2_, f32[76,8,128]{2,1,0:T(8,128)S(1)} %collective-permute-done.10.refs_3_), custom_call_target="tpu_custom_call" | custom-call | bytes 180000000 | tf_op jit(solution)/shard_map/unslot/pallas_call | solution.py:263
  138.6 5.5 %collective-permute-done.8 = f32[576,128]{1,0:T(8,128)S(1)} collective-permute-done((f32[576,128]{1,0:T(8,128)S(1)}, f32[576,128]{1,0:T(8,128)S(1)}, u32[]{:S(2)}, u32[]{:S(2)}) %collective-permute-start.8) | collective-permute-done | bytes 294944 | tf_op jit(solution)/shard_map/ppermute | solution.py:508
  144.1 1.3 copy-done
  146.5 1.1 unpack.1
  (55 shorter events, 8.8 us)
Async XLA Ops:
  13.8 34.9 %collective-permute-start = (f32[3,640,128]{2,1,0:T(8,128)}, f32[3,640,128]{2,1,0:T(8,128)}, u32[]{:S(2)}, u32[]{:S(2)}) collective-permute-start(f32[3,640,128]{2,1,0:T(8,128)} %get-tuple-element.22), channel_id=1, source_target_pairs={{0,1},{1,0},{2,3},{3,2},{4,5},{5,4},{6,7},{7,6},{8,9},{9,8},{10,11... | collective-permute-start | bytes 2949128 | tf_op jit(solution)/shard_map/ppermute | solution.py:468
  29.0 37.6 %collective-permute-start.3 = (f32[3,576,128]{2,1,0:T(8,128)}, f32[3,576,128]{2,1,0:T(8,128)S(1)}, u32[]{:S(2)}, u32[]{:S(2)}) collective-permute-start(f32[3,576,128]{2,1,0:T(8,128)} %get-tuple-element.27), channel_id=1, source_target_pairs={{0,1},{1,0},{2,3},{3,2},{4,5},{5,4},{6,7},{7,6},{8,9},{9,8},{10,11... | collective-permute-start | bytes 2654216 | tf_op jit(solution)/shard_map/ppermute | solution.py:472
  42.5 32.1 %collective-permute-start.2 = (f32[3,640,128]{2,1,0:T(8,128)}, f32[3,640,128]{2,1,0:T(8,128)}, u32[]{:S(2)}, u32[]{:S(2)}) collective-permute-start(f32[3,640,128]{2,1,0:T(8,128)} %get-tuple-element.25.own), channel_id=1, source_target_pairs={{1,3},{2,0},{3,5},{4,2},{5,7},{6,4},{7,9},{8,6},{9,11},{10,8},{11,... | collective-permute-start | bytes 2949128 | tf_op jit(solution)/shard_map/ppermute | solution.py:476
  48.7 28.5 %collective-permute-start.1 = (f32[3,640,128]{2,1,0:T(8,128)}, f32[3,640,128]{2,1,0:T(8,128)}, u32[]{:S(2)}, u32[]{:S(2)}) collective-permute-start(f32[3,640,128]{2,1,0:T(8,128)} %collective-permute-done.mate.refs_1_), channel_id=1, source_target_pairs={{0,2},{2,4},{3,1},{4,6},{5,3},{6,8},{7,5},{8,10},{9,7},{10,12},{11... | collective-permute-start | bytes 2949128 | tf_op jit(solution)/shard_map/ppermute | solution.py:482
  62.7 3.7 %copy-start.15 = (s32[300]{0:T(512)S(1)}, s32[300]{0:T(512)}, u32[]{:S(2)}) copy-start(s32[300]{0:T(512)} %param.9) | copy-start | bytes 3604
  62.7 3.8 %copy-start.16 = (s32[300]{0:T(512)S(1)}, s32[300]{0:T(512)}, u32[]{:S(2)}) copy-start(s32[300]{0:T(512)} %param.10) | copy-start | bytes 3604
  62.7 14.6 %copy-start.1 = (f32[3,640,128]{2,1,0:T(8,128)S(1)}, f32[3,640,128]{2,1,0:T(8,128)}, u32[]{:S(2)}) copy-start(f32[3,640,128]{2,1,0:T(8,128)} %get-tuple-element.25.own) | copy-start | bytes 2949124
  62.7 14.6 %copy-start.11 = (s32[9]{0:T(128)S(1)}, s32[9]{0:T(128)}, u32[]{:S(2)}) copy-start(s32[9]{0:T(128)} %row_off.3) | copy-start | bytes 112
  62.7 14.5 %copy-start.12 = (s32[9]{0:T(128)S(1)}, s32[9]{0:T(128)}, u32[]{:S(2)}) copy-start(s32[9]{0:T(128)} %col_off.3) | copy-start | bytes 112
  62.7 37.8 %all-to-all-start = ((f32[4,76,8,128]{3,2,1,0:T(8,128)}), f32[4,76,8,128]{3,2,1,0:T(8,128)S(1)}, u32[]{:S(2)}, u32[]{:S(2)}) async-start(f32[4,76,8,128]{3,2,1,0:T(8,128)} %get-tuple-element.30), calls=%async_computation | async-start | bytes 2490368 | tf_op jit(solution)/shard_map/all_to_all | solution.py:483
  66.6 51.1 %collective-permute-start.4 = (f32[3,576,128]{2,1,0:T(8,128)S(1)}, f32[3,576,128]{2,1,0:T(8,128)}, u32[]{:S(2)}, u32[]{:S(2)}) collective-permute-start(f32[3,576,128]{2,1,0:T(8,128)S(1)} %collective-permute-done.3.refs_0_.mate), channel_id=1, source_target_pairs={{0,2},{2,4},{3,1},{4,6},{5,3},{6,8},{7,5},{8,10},{9,7},{10,12},{11... | collective-permute-start | bytes 2654216 | tf_op jit(solution)/shard_map/ppermute | solution.py:492
  68.5 49.2 %collective-permute-start.5 = (f32[3,576,128]{2,1,0:T(8,128)}, f32[3,576,128]{2,1,0:T(8,128)}, u32[]{:S(2)}, u32[]{:S(2)}) collective-permute-start(f32[3,576,128]{2,1,0:T(8,128)} %get-tuple-element.29.own), channel_id=1, source_target_pairs={{1,3},{2,0},{3,5},{4,2},{5,7},{6,4},{7,9},{8,6},{9,11},{10,8},{11,... | collective-permute-start | bytes 2654216 | tf_op jit(solution)/shard_map/ppermute | solution.py:481
  83.5 17.0 %collective-permute-start.6 = (f32[640,128]{1,0:T(8,128)}, f32[640,128]{1,0:T(8,128)S(1)}, u32[]{:S(2)}, u32[]{:S(2)}) collective-permute-start(f32[640,128]{1,0:T(8,128)} %get-tuple-element.31.refs_1_), channel_id=1, source_target_pairs={{0,1},{1,0},{2,3},{3,2},{4,5},{5,4},{6,7},{7,6},{8,9},{9,8},{10,11... | collective-permute-start | bytes 983048 | tf_op jit(solution)/shard_map/ppermute | solution.py:496
  100.5 1.0 copy-start.6
  101.4 0.9 copy-start.10
  102.4 15.3 %copy-start.2 = (f32[3,576,128]{2,1,0:T(8,128)S(1)}, f32[3,576,128]{2,1,0:T(8,128)}, u32[]{:S(2)}) copy-start(f32[3,576,128]{2,1,0:T(8,128)} %get-tuple-element.29.own) | copy-start | bytes 2654212
  107.8 38.7 %all-to-all-start.1 = ((f32[32,40,128]{2,1,0:T(8,128)}), f32[32,40,128]{2,1,0:T(8,128)S(1)}, u32[]{:S(2)}, u32[]{:S(2)}) async-start(f32[32,40,128]{2,1,0:T(8,128)} %get-tuple-element.35.refs_1_), calls=%async_computation.1 | async-start | bytes 1310720 | tf_op jit(solution)/shard_map/all_to_all | solution.py:517
  115.5 2.2 %collective-permute-start.7 = (f32[76,8,128]{2,1,0:T(8,128)}, f32[76,8,128]{2,1,0:T(8,128)S(1)}, u32[]{:S(2)}, u32[]{:S(2)}) collective-permute-start(f32[76,8,128]{2,1,0:T(8,128)} %get-tuple-element.34), channel_id=1, source_target_pairs={{0,32},{32,0},{64,96},{96,64},{1,33},{33,1},{65,97},{97,65},{2,34}... | collective-permute-start | bytes 933896 | tf_op jit(solution)/shard_map/ppermute | solution.py:502
  115.6 13.2 %collective-permute-start.10 = (f32[76,8,128]{2,1,0:T(8,128)}, f32[76,8,128]{2,1,0:T(8,128)S(1)}, u32[]{:S(2)}, u32[]{:S(2)}) collective-permute-start(f32[76,8,128]{2,1,0:T(8,128)} %copy-done.14), channel_id=1, source_target_pairs={{0,96},{32,64},{64,32},{96,0},{1,97},{33,65},{65,33},{97,1},{2,98}... | collective-permute-start | bytes 933896 | tf_op jit(solution)/shard_map/ppermute | solution.py:502
  117.2 19.7 %copy-start.8 = (f32[76,8,128]{2,1,0:T(8,128)S(1)}, f32[76,8,128]{2,1,0:T(8,128)}, u32[]{:S(2)}) copy-start(f32[76,8,128]{2,1,0:T(8,128)} %copy-done.7) | copy-start | bytes 933892
  117.2 19.7 %collective-permute-start.9 = (f32[76,8,128]{2,1,0:T(8,128)}, f32[76,8,128]{2,1,0:T(8,128)S(1)}, u32[]{:S(2)}, u32[]{:S(2)}) collective-permute-start(f32[76,8,128]{2,1,0:T(8,128)} %copy-done.13), channel_id=1, source_target_pairs={{0,64},{32,96},{64,0},{96,32},{1,65},{33,97},{65,1},{97,33},{2,66}... | collective-permute-start | bytes 933896 | tf_op jit(solution)/shard_map/ppermute | solution.py:502
  122.1 22.0 %collective-permute-start.8 = (f32[576,128]{1,0:T(8,128)S(1)}, f32[576,128]{1,0:T(8,128)S(1)}, u32[]{:S(2)}, u32[]{:S(2)}) collective-permute-start(f32[576,128]{1,0:T(8,128)S(1)} %get-tuple-element.37), channel_id=1, source_target_pairs={{0,1},{1,0},{2,3},{3,2},{4,5},{5,4},{6,7},{7,6},{8,9},{9,8},{10,11... | collective-permute-start | bytes 884744 | tf_op jit(solution)/shard_map/ppermute | solution.py:508
  125.5 18.6 %copy-start.4 = (f32[640,128]{1,0:T(8,128)S(1)}, f32[640,128]{1,0:T(8,128)}, u32[]{:S(2)}) copy-start(f32[640,128]{1,0:T(8,128)} %copy-done.3) | copy-start | bytes 983044
  144.1 1.3 copy-start
  (6 other events, 4.3 us)

commit v5 on v4

--- a/solution.py
+++ b/solution.py
@@ -36,6 +36,7 @@
 
 PIECES = 16
 PITCH = 17
+VMEM_BYTES = 60 * 1024 * 1024
 GROUPS = 4
 FIRST = 20
 GROUP = 16
@@ -48,6 +49,11 @@
 
 def lasting(us):
     return pl.CostEstimate(flops=0, bytes_accessed=int(us * 3.6e6), transcendentals=0)
+
+
+def whole(x):
+    zeros = (0,) * len(x.shape)
+    return pl.BlockSpec(x.shape, lambda i: zeros)
 
 
 def horner(coefficients, z):
@@ -208,7 +214,7 @@
             pltpu.VMEM((3, rows, 8 * LANES), jnp.bfloat16),
             pltpu.VMEM((6 * LANES, 2 * LANES), jnp.bfloat16),
         ],
-        compiler_params=pltpu.CompilerParams(vmem_limit_bytes=40 * 1024 * 1024),
+        compiler_params=pltpu.CompilerParams(vmem_limit_bytes=24 * 1024 * 1024),
         cost_estimate=lasting(0.02),
         name="window_coherence",
     )(*offsets, near, own, mate, far, *after)
@@ -234,14 +240,16 @@
 
 
 def merge(odd, ifgs, *parts, after):
-    vmem = pl.BlockSpec(memory_space=pltpu.VMEM)
+    output = jax.ShapeDtypeStruct((ifgs, *parts[0].shape[1:]), jnp.float32)
     return pl.pallas_call(
         merge_kernel,
-        in_specs=[pl.BlockSpec(memory_space=pltpu.SMEM)] + [vmem] * 4
+        grid=(1,),
+        in_specs=[pl.BlockSpec(memory_space=pltpu.SMEM)]
+        + [whole(x) for x in parts]
         + [pl.BlockSpec(memory_space=pl.ANY)] * len(after),
-        out_specs=vmem,
-        out_shape=jax.ShapeDtypeStruct((ifgs, *parts[0].shape[1:]), jnp.float32),
-        compiler_params=pltpu.CompilerParams(vmem_limit_bytes=8 * 1024 * 1024),
+        out_specs=whole(output),
+        out_shape=output,
+        compiler_params=pltpu.CompilerParams(vmem_limit_bytes=24 * 1024 * 1024),
         cost_estimate=lasting(0.3),
         name="merge",
     )(odd, *parts, *after)
@@ -259,14 +267,16 @@
 
 
 def unslot(where, ifgs, parts, after):
-    vmem = pl.BlockSpec(memory_space=pltpu.VMEM)
+    output = jax.ShapeDtypeStruct((ifgs, GROUPS, *parts[0].shape[1:]), jnp.float32)
     return pl.pallas_call(
         unslot_kernel,
-        in_specs=[pl.BlockSpec(memory_space=pltpu.SMEM)] + [vmem] * GROUPS
+        grid=(1,),
+        in_specs=[pl.BlockSpec(memory_space=pltpu.SMEM)]
+        + [whole(x) for x in parts]
         + [pl.BlockSpec(memory_space=pl.ANY)] * len(after),
-        out_specs=vmem,
-        out_shape=jax.ShapeDtypeStruct((ifgs, GROUPS, *parts[0].shape[1:]), jnp.float32),
-        compiler_params=pltpu.CompilerParams(vmem_limit_bytes=8 * 1024 * 1024),
+        out_specs=whole(output),
+        out_shape=output,
+        compiler_params=pltpu.CompilerParams(vmem_limit_bytes=24 * 1024 * 1024),
         cost_estimate=lasting(50),
         name="unslot",
     )(where, *parts, *after)
@@ -342,18 +352,19 @@
 
 def network_solve(flip, dates, slots, after=()):
     pairs = dates.shape[1]
-    vmem = pl.BlockSpec(memory_space=pltpu.VMEM)
     smem = pl.BlockSpec(memory_space=pltpu.SMEM)
+    outputs = [
+        jax.ShapeDtypeStruct((DATES, pairs), jnp.float32),
+        jax.ShapeDtypeStruct((pairs, DATES), jnp.float32),
+    ]
     return pl.pallas_call(
         functools.partial(network_kernel, slots=slots),
-        in_specs=[smem, vmem] + [pl.BlockSpec(memory_space=pl.ANY)] * len(after),
-        out_specs=[vmem] * 2,
-        out_shape=[
-            jax.ShapeDtypeStruct((DATES, pairs), jnp.float32),
-            jax.ShapeDtypeStruct((pairs, DATES), jnp.float32),
-        ],
+        grid=(1,),
+        in_specs=[smem, whole(dates)] + [pl.BlockSpec(memory_space=pl.ANY)] * len(after),
+        out_specs=[whole(x) for x in outputs],
+        out_shape=outputs,
         scratch_shapes=[pltpu.VMEM((2, DATES, LANES), jnp.float32)],
-        compiler_params=pltpu.CompilerParams(vmem_limit_bytes=16 * 1024 * 1024),
+        compiler_params=pltpu.CompilerParams(vmem_limit_bytes=VMEM_BYTES),
         cost_estimate=lasting(0.02),
         name="network_solve",
     )(flip, dates, *after)
@@ -375,13 +386,18 @@
     blocks = history.shape[0]
     history[:, :32] = jnp.transpose(solved[:LANES]).reshape(blocks, 32, LANES)
     last = DATES - LANES
-    rest = jnp.concatenate([solved[LANES:], jnp.zeros((LANES - last, 8 * LANES), jnp.float32)])
-    rest = jnp.transpose(rest).reshape(blocks, 4, 8, LANES)
-    packed = rest[:, 0]
+    tail = jnp.concatenate([solved[LANES:], jnp.zeros((LANES - last, 8 * LANES), jnp.float32)])
+    tail = jnp.transpose(tail).reshape(blocks, 4, 8, LANES)
+    packed = tail[:, 0]
     for b in range(1, 4):
-        packed = packed + pltpu.roll(rest[:, b], b * last, 2)
+        packed = packed + pltpu.roll(tail[:, b], b * last, 2)
     history[:, 32:] = packed
-    rest = phase - product(design[...], solved)
+    signs = design[...].astype(jnp.bfloat16)
+    rest, left = phase, solved
+    for _ in range(3):
+        part = left.astype(jnp.bfloat16)
+        left = left - part.astype(jnp.float32)
+        rest = rest - jnp.dot(signs, part, preferred_element_type=jnp.float32)
     lines = held.reshape(count * 8, LANES)
     for j in range(8):
         lines[pl.ds(j, count, stride=8), :] = rest[:, j * LANES : (j + 1) * LANES]
@@ -391,20 +407,21 @@
 
 def invert(group, looked, inverse, design, after):
     slots = looked.shape[1]
-    vmem = pl.BlockSpec(memory_space=pltpu.VMEM)
     part = jax.ShapeDtypeStruct((slots, 8, LANES), jnp.float32)
+    outputs = [part] * GROUPS + [jax.ShapeDtypeStruct((8 * LANES // 32, 40, LANES), jnp.float32)]
     return pl.pallas_call(
         invert_kernel,
+        grid=(1,),
         in_specs=[pl.BlockSpec(memory_space=pltpu.SMEM)]
-        + [vmem] * 3
+        + [whole(x) for x in (looked, inverse, design)]
         + [pl.BlockSpec(memory_space=pl.ANY)] * len(after),
-        out_specs=[vmem] * (GROUPS + 1),
-        out_shape=[part] * GROUPS + [jax.ShapeDtypeStruct((8 * LANES // 32, 40, LANES), jnp.float32)],
+        out_specs=[whole(x) for x in outputs],
+        out_shape=outputs,
         scratch_shapes=[
             pltpu.VMEM((GROUPS * slots, 8 * LANES), jnp.float32),
             pltpu.VMEM((GROUPS * slots, 8, LANES), jnp.float32),
         ],
-        compiler_params=pltpu.CompilerParams(vmem_limit_bytes=32 * 1024 * 1024),
+        compiler_params=pltpu.CompilerParams(vmem_limit_bytes=VMEM_BYTES),
         cost_estimate=lasting(0.02),
         name="invert",
     )(group, looked, inverse, design, *after)
@@ -420,12 +437,13 @@
 
 
 def unpack(held):
-    vmem = pl.BlockSpec(memory_space=pltpu.VMEM)
+    output = jax.ShapeDtypeStruct((held.shape[0], 32, DATES - 1), jnp.float32)
     return pl.pallas_call(
         unpack_kernel,
-        in_specs=[vmem],
-        out_specs=vmem,
-        out_shape=jax.ShapeDtypeStruct((held.shape[0], 32, DATES - 1), jnp.float32),
+        grid=(1,),
+        in_specs=[whole(held)],
+        out_specs=whole(output),
+        out_shape=output,
         compiler_params=pltpu.CompilerParams(vmem_limit_bytes=8 * 1024 * 1024),
         cost_estimate=lasting(0.3),
         name="unpack",

time: 150 us -> 148 us (0.987)
  local copies, waits for them, and re-layouts: 7.88 us -> 3.67 us
  Pallas kernels: 82.8 us -> 84.9 us
  starting transfers between devices: 36.6 us -> 38.4 us
    unnamed x35 -> x33, local copies, waits for them, and re-layouts: 7.54 us -> 2.77 us
    pallas_call x5, Pallas kernels: 22.5 us -> 25.4 us  [the longest x1 16.6 us: network_solve(): pl.pallas_call(functools.partial(network_kernel, slots=slots), grid=(1,),...]
    ppermute x1, waiting for transfers between devices: 2.65 us -> 0.86 us  [local(): near_a = lax.ppermute(mate_a, 'rows', across)]
  transfers between devices with their start and end apart: 13 -> 13, of which waited for: 4 -> 4; matrix products, arithmetic and copies ran while one was open for 0% -> 1% of each run, Pallas kernels for 46% -> 48%
where the time goes in v5:
time: 148 us; the launch traced here: 146 us
  Pallas kernels  84.9 us (57%)
  starting transfers between devices  38.4 us (26%)
  waiting for transfers between devices  18.4 us (12%)
  local copies, waits for them, and re-layouts  3.67 us (2%)
    pallas_call x4, Pallas kernels, look_sums(): pl.pallas_call(look_kernel, grid_spec=pltpu.PrefetchScalarGridSpec(num_sc...  50.4 us
    pallas_call x1, Pallas kernels, network_solve(): pl.pallas_call(functools.partial(network_kernel, slots=slots), grid=(1,),...  16.6 us
    ppermute x3, waiting for transfers between devices, local(): lax.ppermute(residual[d], 'ifg', [(i, i ^ d) for i in range(GROUPS)])  11.9 us
    pallas_call x2, Pallas kernels, window_coherence(): pl.pallas_call(window_kernel, grid=(2,), in_specs=[pl.BlockSpec(memory_sp...  9.12 us
    all_to_all x1, starting transfers between devices, local(): lax.all_to_all(history, 'rows', split_axis=0, concat_axis=0, tiled=True)  8.41 us
    ppermute x1, starting transfers between devices, local(): far_a = lax.ppermute(own_a, 'rows', outward)  6.2 us
    ppermute x1, starting transfers between devices, local(): far_b = lax.ppermute(own_b, 'rows', outward)  6.03 us
    ppermute x1, waiting for transfers between devices, local(): back_b = lax.ppermute(mate_part_b, 'rows', mates)  5.62 us
  transfers between devices with their start and end apart: 13, of which 4 were waited for; matrix products, arithmetic and copies ran while one was open for 1% of the time, Pallas kernels for 48%

profile of v5, /device:TPU:6, one launch (start us, length us, event | category | flops | bytes accessed | tf_op | source)
XLA Modules:
  0.0 146.4 jit_solution(17353692300891064305)
XLA Ops:
  0.6 13.2 %look_sums.4 = (f32[3,640,128]{2,1,0:T(8,128)}, f32[4,76,8,128]{3,2,1,0:T(8,128)}) custom-call(s32[1]{0:T(128)} %bitcast.2.start, bf16[2400,16,128]{2,1,0:T(8,128)(2,1)} %bitcast.29, bf16[2400,16,128]{2,1,0:T(8,128)(2,1)} %bitcast.33, bf16[1024,128]{1,0:T(8,128)(2,1)} %constant.23.clone.pool), custom_call_target="tpu_custom_call" | custom-call | bytes 72000 | tf_op jit(solution)/shard_map/look_sums/pallas_call | solution.py:136
  13.8 3.2 %collective-permute-start = (f32[3,640,128]{2,1,0:T(8,128)}, f32[3,640,128]{2,1,0:T(8,128)}, u32[]{:S(2)}, u32[]{:S(2)}) collective-permute-start(f32[3,640,128]{2,1,0:T(8,128)} %get-tuple-element.22), channel_id=1, source_target_pairs={{0,1},{1,0},{2,3},{3,2},{4,5},{5,4},{6,7},{7,6},{8,9},{9,8},{10,11... | collective-permute-start | bytes 2949128 | tf_op jit(solution)/shard_map/ppermute | solution.py:486
  17.0 12.0 %look_sums.5 = (f32[3,576,128]{2,1,0:T(8,128)}, f32[4,76,8,128]{3,2,1,0:T(8,128)}) custom-call(s32[1]{0:T(128)} %bitcast.14.start, bf16[2400,16,128]{2,1,0:T(8,128)(2,1)} %bitcast.30, bf16[2400,16,128]{2,1,0:T(8,128)(2,1)} %bitcast.34, bf16[1024,128]{1,0:T(8,128)(2,1)} %constant.23.clone.pool, ...), custom_call_target="tpu_custom_call", output_to_operand_aliasing={{1}: (4, {})} | custom-call | bytes 72000 | tf_op jit(solution)/shard_map/look_sums/pallas_call | solution.py:136
  29.4 13.1 %look_sums.6 = (f32[3,640,128]{2,1,0:T(8,128)}, f32[4,76,8,128]{3,2,1,0:T(8,128)}) custom-call(s32[1]{0:T(128)} %bitcast.9.start, bf16[2400,16,128]{2,1,0:T(8,128)(2,1)} %bitcast.31, bf16[2400,16,128]{2,1,0:T(8,128)(2,1)} %bitcast.35, bf16[1024,128]{1,0:T(8,128)(2,1)} %constant.23.clone.pool, ...), custom_call_target="tpu_custom_call", output_to_operand_aliasing={{1}: (4, {})} | custom-call | bytes 72000 | tf_op jit(solution)/shard_map/look_sums/pallas_call | solution.py:136
  42.5 6.2 %collective-permute-start.2 = (f32[3,640,128]{2,1,0:T(8,128)}, f32[3,640,128]{2,1,0:T(8,128)S(1)}, u32[]{:S(2)}, u32[]{:S(2)}) collective-permute-start(f32[3,640,128]{2,1,0:T(8,128)} %get-tuple-element.25.own), channel_id=1, source_target_pairs={{1,3},{2,0},{3,5},{4,2},{5,7},{6,4},{7,9},{8,6},{9,11},{10,8},{11,... | collective-permute-start | bytes 2949128 | tf_op jit(solution)/shard_map/ppermute | solution.py:494
  48.7 1.9 %collective-permute-start.1 = (f32[3,640,128]{2,1,0:T(8,128)}, f32[3,640,128]{2,1,0:T(8,128)S(1)}, u32[]{:S(2)}, u32[]{:S(2)}) collective-permute-start(f32[3,640,128]{2,1,0:T(8,128)} %collective-permute-done.mate.refs_1_), channel_id=1, source_target_pairs={{0,2},{2,4},{3,1},{4,6},{5,3},{6,8},{7,5},{8,10},{9,7},{10,12},{11... | collective-permute-start | bytes 2949128 | tf_op jit(solution)/shard_map/ppermute | solution.py:500
  50.6 12.0 %look_sums.7 = (f32[3,576,128]{2,1,0:T(8,128)}, f32[4,76,8,128]{3,2,1,0:T(8,128)}) custom-call(s32[1]{0:T(128)} %bitcast.16.start, bf16[2400,16,128]{2,1,0:T(8,128)(2,1)} %bitcast.32, bf16[2400,16,128]{2,1,0:T(8,128)(2,1)} %bitcast.36, bf16[1024,128]{1,0:T(8,128)(2,1)} %constant.23.clone.pool, ...), custom_call_target="tpu_custom_call", output_to_operand_aliasing={{1}: (4, {})} | custom-call | bytes 72000 | tf_op jit(solution)/shard_map/look_sums/pallas_call | solution.py:136
  62.7 4.4 %all-to-all-start = ((f32[4,76,8,128]{3,2,1,0:T(8,128)}), f32[4,76,8,128]{3,2,1,0:T(8,128)}, u32[]{:S(2)}, u32[]{:S(2)}) async-start(f32[4,76,8,128]{3,2,1,0:T(8,128)} %get-tuple-element.30), calls=%async_computation | async-start | bytes 2490368 | tf_op jit(solution)/shard_map/all_to_all | solution.py:501
  67.4 1.9 %collective-permute-start.4 = (f32[3,576,128]{2,1,0:T(8,128)}, f32[3,576,128]{2,1,0:T(8,128)}, u32[]{:S(2)}, u32[]{:S(2)}) collective-permute-start(f32[3,576,128]{2,1,0:T(8,128)} %collective-permute-done.3.refs_0_.mate), channel_id=1, source_target_pairs={{0,2},{2,4},{3,1},{4,6},{5,3},{6,8},{7,5},{8,10},{9,7},{10,12},{11... | collective-permute-start | bytes 2654216 | tf_op jit(solution)/shard_map/ppermute | solution.py:510
  69.3 6.0 %collective-permute-start.5 = (f32[3,576,128]{2,1,0:T(8,128)}, f32[3,576,128]{2,1,0:T(8,128)}, u32[]{:S(2)}, u32[]{:S(2)}) collective-permute-start(f32[3,576,128]{2,1,0:T(8,128)} %get-tuple-element.29.own), channel_id=1, source_target_pairs={{1,3},{2,0},{3,5},{4,2},{5,7},{6,4},{7,9},{8,6},{9,11},{10,8},{11,... | collective-permute-start | bytes 2654216 | tf_op jit(solution)/shard_map/ppermute | solution.py:499
  76.2 4.6 %window_coherence.2 = (f32[640,128]{1,0:T(8,128)S(1)}, f32[640,128]{1,0:T(8,128)S(1)}) custom-call(s32[9]{0:T(128)S(1)} %copy-done.10, s32[9]{0:T(128)S(1)} %copy-done.11, s32[1]{0:T(128)} %bitcast.1.flip, f32[3,640,128]{2,1,0:T(8,128)S(1)} %collective-permute-done.1.near, f32[3,640,128]{2,1,0:T(8,128)S(1)} %copy-done.4, ...), custom_call_target="tpu_custom_call" | custom-call | bytes 72000 | tf_op jit(solution)/shard_map/window_coherence/pallas_call | solution.py:205
  82.7 16.6 %network_solve.1 = (f32[160,304]{1,0:T(8,128)}, f32[304,160]{1,0:T(8,128)}) custom-call(s32[1]{0:T(128)} %bitcast.1.flip, s32[2,304]{1,0:T(2,128)} %select_n.14.dates, f32[3,576,128]{2,1,0:T(8,128)} %collective-permute-done.3.refs_0_.mate, f32[640,128]{1,0:T(8,128)} %copy-done.6), custom_call_target="tpu_custom_call" | custom-call | bytes 72000 | tf_op jit(solution)/shard_map/network_solve/pallas_call | solution.py:360
  100.0 4.8 %invert.1 = (f32[76,8,128]{2,1,0:T(8,128)}, f32[76,8,128]{2,1,0:T(8,128)}, f32[76,8,128]{2,1,0:T(8,128)}, f32[76,8,128]{2,1,0:T(8,128)}, f32[32,40,128]{2,1,0:T(8,128)}) custom-call(s32[1]{0:T(128)} %bitcast.17.group, f32[4,76,8,128]{3,2,1,0:T(8,128)} %all-to-all-done.looked, f32[160,304]{1,0:T(8,128)} %get-tuple-element.32.inverse, ...), custom_call_target="tpu_custom_call" | custom-call | bytes 72000 | tf_op jit(solution)/shard_map/invert/pallas_call | solution.py:412
  104.8 8.4 %all-to-all-start.1 = ((f32[32,40,128]{2,1,0:T(8,128)}), f32[32,40,128]{2,1,0:T(8,128)S(1)}, u32[]{:S(2)}, u32[]{:S(2)}) async-start(f32[32,40,128]{2,1,0:T(8,128)} %get-tuple-element.35.refs_1_), calls=%async_computation.1 | async-start | bytes 1310720 | tf_op jit(solution)/shard_map/all_to_all | solution.py:535
  113.3 1.8 %collective-permute-start.10 = (f32[76,8,128]{2,1,0:T(8,128)S(1)}, f32[76,8,128]{2,1,0:T(8,128)S(1)}, u32[]{:S(2)}, u32[]{:S(2)}) collective-permute-start(f32[76,8,128]{2,1,0:T(8,128)S(1)} %copy-done.15), channel_id=1, source_target_pairs={{0,96},{32,64},{64,32},{96,0},{1,97},{33,65},{65,33},{97,1},{2,98}... | collective-permute-start | bytes 933896 | tf_op jit(solution)/shard_map/ppermute | solution.py:520
  115.5 4.5 %window_coherence.3 = (f32[576,128]{1,0:T(8,128)S(1)}, f32[576,128]{1,0:T(8,128)S(1)}) custom-call(s32[9]{0:T(128)S(1)} %copy-done.10, s32[9]{0:T(128)S(1)} %copy-done.11, s32[1]{0:T(128)} %bitcast.1.flip, f32[3,576,128]{2,1,0:T(8,128)} %collective-permute-done.4.near, f32[3,576,128]{2,1,0:T(8,128)S(1)} %copy-done.5, ...), custom_call_target="tpu_custom_call" | custom-call | bytes 72000 | tf_op jit(solution)/shard_map/window_coherence/pallas_call | solution.py:205
  120.0 3.4 %collective-permute-start.8 = (f32[576,128]{1,0:T(8,128)S(1)}, f32[576,128]{1,0:T(8,128)S(1)}, u32[]{:S(2)}, u32[]{:S(2)}) collective-permute-start(f32[576,128]{1,0:T(8,128)S(1)} %get-tuple-element.37), channel_id=1, source_target_pairs={{0,1},{1,0},{2,3},{3,2},{4,5},{5,4},{6,7},{7,6},{8,9},{9,8},{10,11... | collective-permute-start | bytes 884744 | tf_op jit(solution)/shard_map/ppermute | solution.py:526
  123.5 4.0 %collective-permute-done.10.refs_3_ = f32[76,8,128]{2,1,0:T(8,128)S(1)} collective-permute-done((f32[76,8,128]{2,1,0:T(8,128)S(1)}, f32[76,8,128]{2,1,0:T(8,128)S(1)}, u32[]{:S(2)}, u32[]{:S(2)}) %collective-permute-start.10) | collective-permute-done | bytes 311328 | tf_op jit(solution)/shard_map/ppermute | solution.py:520
  127.5 8.0 %collective-permute-done.9.refs_2_ = f32[76,8,128]{2,1,0:T(8,128)S(1)} collective-permute-done((f32[76,8,128]{2,1,0:T(8,128)S(1)}, f32[76,8,128]{2,1,0:T(8,128)S(1)}, u32[]{:S(2)}, u32[]{:S(2)}) %collective-permute-start.9) | collective-permute-done | bytes 311328 | tf_op jit(solution)/shard_map/ppermute | solution.py:520
  135.5 1.7 %unslot.1.refs_0_ = f32[75,4,8,128]{3,2,1,0:T(8,128)} custom-call(s32[2]{0:T(128)S(1)} %pad_add_fusion.where, f32[76,8,128]{2,1,0:T(8,128)S(1)} %copy-done.9, f32[76,8,128]{2,1,0:T(8,128)S(1)} %collective-permute-done.7.refs_0_.refs_1_, f32[76,8,128]{2,1,0:T(8,128)S(1)} %collective-permute-done.9.refs_2_, f32[76,8,128]{2,1,0:T(8,128)S(1)} %collective-permute-done.10.refs_3_), custom_call_target="tpu_custom_call" | custom-call | bytes 180000000 | tf_op jit(solution)/shard_map/unslot/pallas_call | solution.py:271
  137.2 5.6 %collective-permute-done.8 = f32[576,128]{1,0:T(8,128)S(1)} collective-permute-done((f32[576,128]{1,0:T(8,128)S(1)}, f32[576,128]{1,0:T(8,128)S(1)}, u32[]{:S(2)}, u32[]{:S(2)}) %collective-permute-start.8) | collective-permute-done | bytes 294944 | tf_op jit(solution)/shard_map/ppermute | solution.py:526
  142.8 1.3 copy-done
  144.1 1.1 merge.1
  145.2 1.1 unpack.1
  (53 shorter events, 4.4 us)
Async XLA Ops:
  13.8 34.9 %collective-permute-start = (f32[3,640,128]{2,1,0:T(8,128)}, f32[3,640,128]{2,1,0:T(8,128)}, u32[]{:S(2)}, u32[]{:S(2)}) collective-permute-start(f32[3,640,128]{2,1,0:T(8,128)} %get-tuple-element.22), channel_id=1, source_target_pairs={{0,1},{1,0},{2,3},{3,2},{4,5},{5,4},{6,7},{7,6},{8,9},{9,8},{10,11... | collective-permute-start | bytes 2949128 | tf_op jit(solution)/shard_map/ppermute | solution.py:486
  29.0 38.3 %collective-permute-start.3 = (f32[3,576,128]{2,1,0:T(8,128)}, f32[3,576,128]{2,1,0:T(8,128)}, u32[]{:S(2)}, u32[]{:S(2)}) collective-permute-start(f32[3,576,128]{2,1,0:T(8,128)} %get-tuple-element.27), channel_id=1, source_target_pairs={{0,1},{1,0},{2,3},{3,2},{4,5},{5,4},{6,7},{7,6},{8,9},{9,8},{10,11... | collective-permute-start | bytes 2654216 | tf_op jit(solution)/shard_map/ppermute | solution.py:490
  42.5 32.8 %collective-permute-start.2 = (f32[3,640,128]{2,1,0:T(8,128)}, f32[3,640,128]{2,1,0:T(8,128)S(1)}, u32[]{:S(2)}, u32[]{:S(2)}) collective-permute-start(f32[3,640,128]{2,1,0:T(8,128)} %get-tuple-element.25.own), channel_id=1, source_target_pairs={{1,3},{2,0},{3,5},{4,2},{5,7},{6,4},{7,9},{8,6},{9,11},{10,8},{11,... | collective-permute-start | bytes 2949128 | tf_op jit(solution)/shard_map/ppermute | solution.py:494
  48.7 27.5 %collective-permute-start.1 = (f32[3,640,128]{2,1,0:T(8,128)}, f32[3,640,128]{2,1,0:T(8,128)S(1)}, u32[]{:S(2)}, u32[]{:S(2)}) collective-permute-start(f32[3,640,128]{2,1,0:T(8,128)} %collective-permute-done.mate.refs_1_), channel_id=1, source_target_pairs={{0,2},{2,4},{3,1},{4,6},{5,3},{6,8},{7,5},{8,10},{9,7},{10,12},{11... | collective-permute-start | bytes 2949128 | tf_op jit(solution)/shard_map/ppermute | solution.py:500
  62.7 4.6 %copy-start.13 = (s32[300]{0:T(512)S(1)}, s32[300]{0:T(512)}, u32[]{:S(2)}) copy-start(s32[300]{0:T(512)} %param.10) | copy-start | bytes 3604
  62.7 13.5 %copy-start.4 = (f32[3,640,128]{2,1,0:T(8,128)S(1)}, f32[3,640,128]{2,1,0:T(8,128)}, u32[]{:S(2)}) copy-start(f32[3,640,128]{2,1,0:T(8,128)} %get-tuple-element.25.own) | copy-start | bytes 2949124
  62.7 13.5 %copy-start.10 = (s32[9]{0:T(128)S(1)}, s32[9]{0:T(128)}, u32[]{:S(2)}) copy-start(s32[9]{0:T(128)} %row_off.3) | copy-start | bytes 112
  62.7 13.5 %copy-start.11 = (s32[9]{0:T(128)S(1)}, s32[9]{0:T(128)}, u32[]{:S(2)}) copy-start(s32[9]{0:T(128)} %col_off.3) | copy-start | bytes 112
  62.7 36.6 %all-to-all-start = ((f32[4,76,8,128]{3,2,1,0:T(8,128)}), f32[4,76,8,128]{3,2,1,0:T(8,128)}, u32[]{:S(2)}, u32[]{:S(2)}) async-start(f32[4,76,8,128]{3,2,1,0:T(8,128)} %get-tuple-element.30), calls=%async_computation | async-start | bytes 2490368 | tf_op jit(solution)/shard_map/all_to_all | solution.py:501
  67.4 48.1 %collective-permute-start.4 = (f32[3,576,128]{2,1,0:T(8,128)}, f32[3,576,128]{2,1,0:T(8,128)}, u32[]{:S(2)}, u32[]{:S(2)}) collective-permute-start(f32[3,576,128]{2,1,0:T(8,128)} %collective-permute-done.3.refs_0_.mate), channel_id=1, source_target_pairs={{0,2},{2,4},{3,1},{4,6},{5,3},{6,8},{7,5},{8,10},{9,7},{10,12},{11... | collective-permute-start | bytes 2654216 | tf_op jit(solution)/shard_map/ppermute | solution.py:510
  69.3 46.2 %collective-permute-start.5 = (f32[3,576,128]{2,1,0:T(8,128)}, f32[3,576,128]{2,1,0:T(8,128)}, u32[]{:S(2)}, u32[]{:S(2)}) collective-permute-start(f32[3,576,128]{2,1,0:T(8,128)} %get-tuple-element.29.own), channel_id=1, source_target_pairs={{1,3},{2,0},{3,5},{4,2},{5,7},{6,4},{7,9},{8,6},{9,11},{10,8},{11,... | collective-permute-start | bytes 2654216 | tf_op jit(solution)/shard_map/ppermute | solution.py:499
  81.6 17.7 %collective-permute-start.6 = (f32[640,128]{1,0:T(8,128)S(1)}, f32[640,128]{1,0:T(8,128)S(1)}, u32[]{:S(2)}, u32[]{:S(2)}) collective-permute-start(f32[640,128]{1,0:T(8,128)S(1)} %get-tuple-element.31.refs_1_), channel_id=1, source_target_pairs={{0,1},{1,0},{2,3},{3,2},{4,5},{5,4},{6,7},{7,6},{8,9},{9,8},{10,11... | collective-permute-start | bytes 983048 | tf_op jit(solution)/shard_map/ppermute | solution.py:514
  100.0 15.5 %copy-start.5 = (f32[3,576,128]{2,1,0:T(8,128)S(1)}, f32[3,576,128]{2,1,0:T(8,128)}, u32[]{:S(2)}) copy-start(f32[3,576,128]{2,1,0:T(8,128)} %get-tuple-element.29.own) | copy-start | bytes 2654212
  104.8 8.5 %copy-start.15 = (f32[76,8,128]{2,1,0:T(8,128)S(1)}, f32[76,8,128]{2,1,0:T(8,128)}, u32[]{:S(2)}) copy-start(f32[76,8,128]{2,1,0:T(8,128)} %get-tuple-element.40) | copy-start | bytes 933892
  104.8 10.4 %copy-start.14 = (f32[76,8,128]{2,1,0:T(8,128)S(1)}, f32[76,8,128]{2,1,0:T(8,128)}, u32[]{:S(2)}) copy-start(f32[76,8,128]{2,1,0:T(8,128)} %get-tuple-element.39) | copy-start | bytes 933892
  104.8 10.7 %copy-start.1 = (f32[32,40,128]{2,1,0:T(8,128)S(1)}, f32[32,40,128]{2,1,0:T(8,128)}, u32[]{:S(2)}) copy-start(f32[32,40,128]{2,1,0:T(8,128)} %get-tuple-element.35.refs_1_) | copy-start | bytes 1966084
  104.8 40.4 %all-to-all-start.1 = ((f32[32,40,128]{2,1,0:T(8,128)}), f32[32,40,128]{2,1,0:T(8,128)S(1)}, u32[]{:S(2)}, u32[]{:S(2)}) async-start(f32[32,40,128]{2,1,0:T(8,128)} %get-tuple-element.35.refs_1_), calls=%async_computation.1 | async-start | bytes 1310720 | tf_op jit(solution)/shard_map/all_to_all | solution.py:535
  113.2 2.3 %collective-permute-start.7 = (f32[76,8,128]{2,1,0:T(8,128)}, f32[76,8,128]{2,1,0:T(8,128)S(1)}, u32[]{:S(2)}, u32[]{:S(2)}) collective-permute-start(f32[76,8,128]{2,1,0:T(8,128)} %get-tuple-element.34), channel_id=1, source_target_pairs={{0,32},{32,0},{64,96},{96,64},{1,33},{33,1},{65,97},{97,65},{2,34}... | collective-permute-start | bytes 933896 | tf_op jit(solution)/shard_map/ppermute | solution.py:520
  113.3 14.1 %collective-permute-start.10 = (f32[76,8,128]{2,1,0:T(8,128)S(1)}, f32[76,8,128]{2,1,0:T(8,128)S(1)}, u32[]{:S(2)}, u32[]{:S(2)}) collective-permute-start(f32[76,8,128]{2,1,0:T(8,128)S(1)} %copy-done.15), channel_id=1, source_target_pairs={{0,96},{32,64},{64,32},{96,0},{1,97},{33,65},{65,33},{97,1},{2,98}... | collective-permute-start | bytes 933896 | tf_op jit(solution)/shard_map/ppermute | solution.py:520
  115.2 20.3 %copy-start.9 = (f32[76,8,128]{2,1,0:T(8,128)S(1)}, f32[76,8,128]{2,1,0:T(8,128)}, u32[]{:S(2)}) copy-start(f32[76,8,128]{2,1,0:T(8,128)} %get-tuple-element.38.refs_0_) | copy-start | bytes 933892
  115.2 20.3 %collective-permute-start.9 = (f32[76,8,128]{2,1,0:T(8,128)S(1)}, f32[76,8,128]{2,1,0:T(8,128)S(1)}, u32[]{:S(2)}, u32[]{:S(2)}) collective-permute-start(f32[76,8,128]{2,1,0:T(8,128)S(1)} %copy-done.14), channel_id=1, source_target_pairs={{0,64},{32,96},{64,0},{96,32},{1,65},{33,97},{65,1},{97,33},{2,66}... | collective-permute-start | bytes 933896 | tf_op jit(solution)/shard_map/ppermute | solution.py:520
  120.0 22.8 %collective-permute-start.8 = (f32[576,128]{1,0:T(8,128)S(1)}, f32[576,128]{1,0:T(8,128)S(1)}, u32[]{:S(2)}, u32[]{:S(2)}) collective-permute-start(f32[576,128]{1,0:T(8,128)S(1)} %get-tuple-element.37), channel_id=1, source_target_pairs={{0,1},{1,0},{2,3},{3,2},{4,5},{5,4},{6,7},{7,6},{8,9},{9,8},{10,11... | collective-permute-start | bytes 884744 | tf_op jit(solution)/shard_map/ppermute | solution.py:526
  123.4 19.4 %copy-start.3 = (f32[640,128]{1,0:T(8,128)S(1)}, f32[640,128]{1,0:T(8,128)}, u32[]{:S(2)}) copy-start(f32[640,128]{1,0:T(8,128)} %copy-done.2) | copy-start | bytes 983044
  123.5 19.4 %copy-start.8 = (f32[640,128]{1,0:T(8,128)S(1)}, f32[640,128]{1,0:T(8,128)}, u32[]{:S(2)}) copy-start(f32[640,128]{1,0:T(8,128)} %copy-done.7) | copy-start | bytes 983044
  (5 other events, 8.3 us)

commit v6 on v5

--- a/solution.py
+++ b/solution.py
@@ -146,7 +146,7 @@
                     lambda i, s: (0, slot + i * block, 0, 0),
                 ),
             ],
-            scratch_shapes=[pltpu.VMEM((GROUP * PITCH, LANES), jnp.float32)] * 2
+            scratch_shapes=[pltpu.VMEM((GROUP * PITCH + 16, LANES), jnp.float32)] * 2
             + [pltpu.VMEM((rows, RG_LOOKS * LANES), jnp.bfloat16)] * 8,
         ),
         out_shape=[

time: 148 us -> 148 us (level)
  no operation moved by 1% of the time
where the time goes in v6:
time: 148 us; the launch traced here: 146 us
  Pallas kernels  84.9 us (57%)
  starting transfers between devices  38.4 us (26%)
  waiting for transfers between devices  18.4 us (12%)
  local copies, waits for them, and re-layouts  3.67 us (2%)
    pallas_call x4, Pallas kernels, look_sums(): pl.pallas_call(look_kernel, grid_spec=pltpu.PrefetchScalarGridSpec(num_sc...  50.4 us
    pallas_call x1, Pallas kernels, network_solve(): pl.pallas_call(functools.partial(network_kernel, slots=slots), grid=(1,),...  16.6 us
    ppermute x3, waiting for transfers between devices, local(): lax.ppermute(residual[d], 'ifg', [(i, i ^ d) for i in range(GROUPS)])  11.9 us
    pallas_call x2, Pallas kernels, window_coherence(): pl.pallas_call(window_kernel, grid=(2,), in_specs=[pl.BlockSpec(memory_sp...  9.12 us
    all_to_all x1, starting transfers between devices, local(): lax.all_to_all(history, 'rows', split_axis=0, concat_axis=0, tiled=True)  8.41 us
    ppermute x1, starting transfers between devices, local(): far_a = lax.ppermute(own_a, 'rows', outward)  6.2 us
    ppermute x1, starting transfers between devices, local(): far_b = lax.ppermute(own_b, 'rows', outward)  6.03 us
    ppermute x1, waiting for transfers between devices, local(): back_b = lax.ppermute(mate_part_b, 'rows', mates)  5.62 us
  transfers between devices with their start and end apart: 13, of which 4 were waited for; matrix products, arithmetic and copies ran while one was open for 1% of the time, Pallas kernels for 48%

profile of v6, /device:TPU:6, one launch (start us, length us, event | category | flops | bytes accessed | tf_op | source)
XLA Modules:
  0.0 146.4 jit_solution(14378070875661488953)
XLA Ops:
  0.6 13.2 %look_sums.4 = (f32[3,640,128]{2,1,0:T(8,128)}, f32[4,76,8,128]{3,2,1,0:T(8,128)}) custom-call(s32[1]{0:T(128)} %bitcast.2.start, bf16[2400,16,128]{2,1,0:T(8,128)(2,1)} %bitcast.29, bf16[2400,16,128]{2,1,0:T(8,128)(2,1)} %bitcast.33, bf16[1024,128]{1,0:T(8,128)(2,1)} %constant.23.clone.pool), custom_call_target="tpu_custom_call" | custom-call | bytes 72000 | tf_op jit(solution)/shard_map/look_sums/pallas_call | solution.py:136
  13.8 3.2 %collective-permute-start = (f32[3,640,128]{2,1,0:T(8,128)}, f32[3,640,128]{2,1,0:T(8,128)}, u32[]{:S(2)}, u32[]{:S(2)}) collective-permute-start(f32[3,640,128]{2,1,0:T(8,128)} %get-tuple-element.22), channel_id=1, source_target_pairs={{0,1},{1,0},{2,3},{3,2},{4,5},{5,4},{6,7},{7,6},{8,9},{9,8},{10,11... | collective-permute-start | bytes 2949128 | tf_op jit(solution)/shard_map/ppermute | solution.py:486
  17.0 12.0 %look_sums.5 = (f32[3,576,128]{2,1,0:T(8,128)}, f32[4,76,8,128]{3,2,1,0:T(8,128)}) custom-call(s32[1]{0:T(128)} %bitcast.14.start, bf16[2400,16,128]{2,1,0:T(8,128)(2,1)} %bitcast.30, bf16[2400,16,128]{2,1,0:T(8,128)(2,1)} %bitcast.34, bf16[1024,128]{1,0:T(8,128)(2,1)} %constant.23.clone.pool, ...), custom_call_target="tpu_custom_call", output_to_operand_aliasing={{1}: (4, {})} | custom-call | bytes 72000 | tf_op jit(solution)/shard_map/look_sums/pallas_call | solution.py:136
  29.4 13.1 %look_sums.6 = (f32[3,640,128]{2,1,0:T(8,128)}, f32[4,76,8,128]{3,2,1,0:T(8,128)}) custom-call(s32[1]{0:T(128)} %bitcast.9.start, bf16[2400,16,128]{2,1,0:T(8,128)(2,1)} %bitcast.31, bf16[2400,16,128]{2,1,0:T(8,128)(2,1)} %bitcast.35, bf16[1024,128]{1,0:T(8,128)(2,1)} %constant.23.clone.pool, ...), custom_call_target="tpu_custom_call", output_to_operand_aliasing={{1}: (4, {})} | custom-call | bytes 72000 | tf_op jit(solution)/shard_map/look_sums/pallas_call | solution.py:136
  42.5 6.2 %collective-permute-start.2 = (f32[3,640,128]{2,1,0:T(8,128)}, f32[3,640,128]{2,1,0:T(8,128)S(1)}, u32[]{:S(2)}, u32[]{:S(2)}) collective-permute-start(f32[3,640,128]{2,1,0:T(8,128)} %get-tuple-element.25.own), channel_id=1, source_target_pairs={{1,3},{2,0},{3,5},{4,2},{5,7},{6,4},{7,9},{8,6},{9,11},{10,8},{11,... | collective-permute-start | bytes 2949128 | tf_op jit(solution)/shard_map/ppermute | solution.py:494
  48.7 1.9 %collective-permute-start.1 = (f32[3,640,128]{2,1,0:T(8,128)}, f32[3,640,128]{2,1,0:T(8,128)S(1)}, u32[]{:S(2)}, u32[]{:S(2)}) collective-permute-start(f32[3,640,128]{2,1,0:T(8,128)} %collective-permute-done.mate.refs_1_), channel_id=1, source_target_pairs={{0,2},{2,4},{3,1},{4,6},{5,3},{6,8},{7,5},{8,10},{9,7},{10,12},{11... | collective-permute-start | bytes 2949128 | tf_op jit(solution)/shard_map/ppermute | solution.py:500
  50.6 12.0 %look_sums.7 = (f32[3,576,128]{2,1,0:T(8,128)}, f32[4,76,8,128]{3,2,1,0:T(8,128)}) custom-call(s32[1]{0:T(128)} %bitcast.16.start, bf16[2400,16,128]{2,1,0:T(8,128)(2,1)} %bitcast.32, bf16[2400,16,128]{2,1,0:T(8,128)(2,1)} %bitcast.36, bf16[1024,128]{1,0:T(8,128)(2,1)} %constant.23.clone.pool, ...), custom_call_target="tpu_custom_call", output_to_operand_aliasing={{1}: (4, {})} | custom-call | bytes 72000 | tf_op jit(solution)/shard_map/look_sums/pallas_call | solution.py:136
  62.7 4.4 %all-to-all-start = ((f32[4,76,8,128]{3,2,1,0:T(8,128)}), f32[4,76,8,128]{3,2,1,0:T(8,128)}, u32[]{:S(2)}, u32[]{:S(2)}) async-start(f32[4,76,8,128]{3,2,1,0:T(8,128)} %get-tuple-element.30), calls=%async_computation | async-start | bytes 2490368 | tf_op jit(solution)/shard_map/all_to_all | solution.py:501
  67.4 1.9 %collective-permute-start.4 = (f32[3,576,128]{2,1,0:T(8,128)}, f32[3,576,128]{2,1,0:T(8,128)}, u32[]{:S(2)}, u32[]{:S(2)}) collective-permute-start(f32[3,576,128]{2,1,0:T(8,128)} %collective-permute-done.3.refs_0_.mate), channel_id=1, source_target_pairs={{0,2},{2,4},{3,1},{4,6},{5,3},{6,8},{7,5},{8,10},{9,7},{10,12},{11... | collective-permute-start | bytes 2654216 | tf_op jit(solution)/shard_map/ppermute | solution.py:510
  69.3 6.0 %collective-permute-start.5 = (f32[3,576,128]{2,1,0:T(8,128)}, f32[3,576,128]{2,1,0:T(8,128)}, u32[]{:S(2)}, u32[]{:S(2)}) collective-permute-start(f32[3,576,128]{2,1,0:T(8,128)} %get-tuple-element.29.own), channel_id=1, source_target_pairs={{1,3},{2,0},{3,5},{4,2},{5,7},{6,4},{7,9},{8,6},{9,11},{10,8},{11,... | collective-permute-start | bytes 2654216 | tf_op jit(solution)/shard_map/ppermute | solution.py:499
  76.2 4.6 %window_coherence.2 = (f32[640,128]{1,0:T(8,128)S(1)}, f32[640,128]{1,0:T(8,128)S(1)}) custom-call(s32[9]{0:T(128)S(1)} %copy-done.10, s32[9]{0:T(128)S(1)} %copy-done.11, s32[1]{0:T(128)} %bitcast.1.flip, f32[3,640,128]{2,1,0:T(8,128)S(1)} %collective-permute-done.1.near, f32[3,640,128]{2,1,0:T(8,128)S(1)} %copy-done.4, ...), custom_call_target="tpu_custom_call" | custom-call | bytes 72000 | tf_op jit(solution)/shard_map/window_coherence/pallas_call | solution.py:205
  82.7 16.6 %network_solve.1 = (f32[160,304]{1,0:T(8,128)}, f32[304,160]{1,0:T(8,128)}) custom-call(s32[1]{0:T(128)} %bitcast.1.flip, s32[2,304]{1,0:T(2,128)} %select_n.14.dates, f32[3,576,128]{2,1,0:T(8,128)} %collective-permute-done.3.refs_0_.mate, f32[640,128]{1,0:T(8,128)} %copy-done.6), custom_call_target="tpu_custom_call" | custom-call | bytes 72000 | tf_op jit(solution)/shard_map/network_solve/pallas_call | solution.py:360
  100.0 4.8 %invert.1 = (f32[76,8,128]{2,1,0:T(8,128)}, f32[76,8,128]{2,1,0:T(8,128)}, f32[76,8,128]{2,1,0:T(8,128)}, f32[76,8,128]{2,1,0:T(8,128)}, f32[32,40,128]{2,1,0:T(8,128)}) custom-call(s32[1]{0:T(128)} %bitcast.17.group, f32[4,76,8,128]{3,2,1,0:T(8,128)} %all-to-all-done.looked, f32[160,304]{1,0:T(8,128)} %get-tuple-element.32.inverse, ...), custom_call_target="tpu_custom_call" | custom-call | bytes 72000 | tf_op jit(solution)/shard_map/invert/pallas_call | solution.py:412
  104.8 8.4 %all-to-all-start.1 = ((f32[32,40,128]{2,1,0:T(8,128)}), f32[32,40,128]{2,1,0:T(8,128)S(1)}, u32[]{:S(2)}, u32[]{:S(2)}) async-start(f32[32,40,128]{2,1,0:T(8,128)} %get-tuple-element.35.refs_1_), calls=%async_computation.1 | async-start | bytes 1310720 | tf_op jit(solution)/shard_map/all_to_all | solution.py:535
  113.3 1.8 %collective-permute-start.10 = (f32[76,8,128]{2,1,0:T(8,128)S(1)}, f32[76,8,128]{2,1,0:T(8,128)S(1)}, u32[]{:S(2)}, u32[]{:S(2)}) collective-permute-start(f32[76,8,128]{2,1,0:T(8,128)S(1)} %copy-done.15), channel_id=1, source_target_pairs={{0,96},{32,64},{64,32},{96,0},{1,97},{33,65},{65,33},{97,1},{2,98}... | collective-permute-start | bytes 933896 | tf_op jit(solution)/shard_map/ppermute | solution.py:520
  115.5 4.5 %window_coherence.3 = (f32[576,128]{1,0:T(8,128)S(1)}, f32[576,128]{1,0:T(8,128)S(1)}) custom-call(s32[9]{0:T(128)S(1)} %copy-done.10, s32[9]{0:T(128)S(1)} %copy-done.11, s32[1]{0:T(128)} %bitcast.1.flip, f32[3,576,128]{2,1,0:T(8,128)} %collective-permute-done.4.near, f32[3,576,128]{2,1,0:T(8,128)S(1)} %copy-done.5, ...), custom_call_target="tpu_custom_call" | custom-call | bytes 72000 | tf_op jit(solution)/shard_map/window_coherence/pallas_call | solution.py:205
  120.0 3.4 %collective-permute-start.8 = (f32[576,128]{1,0:T(8,128)S(1)}, f32[576,128]{1,0:T(8,128)S(1)}, u32[]{:S(2)}, u32[]{:S(2)}) collective-permute-start(f32[576,128]{1,0:T(8,128)S(1)} %get-tuple-element.37), channel_id=1, source_target_pairs={{0,1},{1,0},{2,3},{3,2},{4,5},{5,4},{6,7},{7,6},{8,9},{9,8},{10,11... | collective-permute-start | bytes 884744 | tf_op jit(solution)/shard_map/ppermute | solution.py:526
  123.5 4.0 %collective-permute-done.10.refs_3_ = f32[76,8,128]{2,1,0:T(8,128)S(1)} collective-permute-done((f32[76,8,128]{2,1,0:T(8,128)S(1)}, f32[76,8,128]{2,1,0:T(8,128)S(1)}, u32[]{:S(2)}, u32[]{:S(2)}) %collective-permute-start.10) | collective-permute-done | bytes 311328 | tf_op jit(solution)/shard_map/ppermute | solution.py:520
  127.5 8.0 %collective-permute-done.9.refs_2_ = f32[76,8,128]{2,1,0:T(8,128)S(1)} collective-permute-done((f32[76,8,128]{2,1,0:T(8,128)S(1)}, f32[76,8,128]{2,1,0:T(8,128)S(1)}, u32[]{:S(2)}, u32[]{:S(2)}) %collective-permute-start.9) | collective-permute-done | bytes 311328 | tf_op jit(solution)/shard_map/ppermute | solution.py:520
  135.5 1.7 %unslot.1.refs_0_ = f32[75,4,8,128]{3,2,1,0:T(8,128)} custom-call(s32[2]{0:T(128)S(1)} %pad_add_fusion.where, f32[76,8,128]{2,1,0:T(8,128)S(1)} %copy-done.9, f32[76,8,128]{2,1,0:T(8,128)S(1)} %collective-permute-done.7.refs_0_.refs_1_, f32[76,8,128]{2,1,0:T(8,128)S(1)} %collective-permute-done.9.refs_2_, f32[76,8,128]{2,1,0:T(8,128)S(1)} %collective-permute-done.10.refs_3_), custom_call_target="tpu_custom_call" | custom-call | bytes 180000000 | tf_op jit(solution)/shard_map/unslot/pallas_call | solution.py:271
  137.2 5.6 %collective-permute-done.8 = f32[576,128]{1,0:T(8,128)S(1)} collective-permute-done((f32[576,128]{1,0:T(8,128)S(1)}, f32[576,128]{1,0:T(8,128)S(1)}, u32[]{:S(2)}, u32[]{:S(2)}) %collective-permute-start.8) | collective-permute-done | bytes 294944 | tf_op jit(solution)/shard_map/ppermute | solution.py:526
  142.8 1.3 copy-done
  144.1 1.1 merge.1
  145.2 1.1 unpack.1
  (53 shorter events, 4.4 us)
Async XLA Ops:
  13.8 34.9 %collective-permute-start = (f32[3,640,128]{2,1,0:T(8,128)}, f32[3,640,128]{2,1,0:T(8,128)}, u32[]{:S(2)}, u32[]{:S(2)}) collective-permute-start(f32[3,640,128]{2,1,0:T(8,128)} %get-tuple-element.22), channel_id=1, source_target_pairs={{0,1},{1,0},{2,3},{3,2},{4,5},{5,4},{6,7},{7,6},{8,9},{9,8},{10,11... | collective-permute-start | bytes 2949128 | tf_op jit(solution)/shard_map/ppermute | solution.py:486
  29.0 38.3 %collective-permute-start.3 = (f32[3,576,128]{2,1,0:T(8,128)}, f32[3,576,128]{2,1,0:T(8,128)}, u32[]{:S(2)}, u32[]{:S(2)}) collective-permute-start(f32[3,576,128]{2,1,0:T(8,128)} %get-tuple-element.27), channel_id=1, source_target_pairs={{0,1},{1,0},{2,3},{3,2},{4,5},{5,4},{6,7},{7,6},{8,9},{9,8},{10,11... | collective-permute-start | bytes 2654216 | tf_op jit(solution)/shard_map/ppermute | solution.py:490
  42.5 32.8 %collective-permute-start.2 = (f32[3,640,128]{2,1,0:T(8,128)}, f32[3,640,128]{2,1,0:T(8,128)S(1)}, u32[]{:S(2)}, u32[]{:S(2)}) collective-permute-start(f32[3,640,128]{2,1,0:T(8,128)} %get-tuple-element.25.own), channel_id=1, source_target_pairs={{1,3},{2,0},{3,5},{4,2},{5,7},{6,4},{7,9},{8,6},{9,11},{10,8},{11,... | collective-permute-start | bytes 2949128 | tf_op jit(solution)/shard_map/ppermute | solution.py:494
  48.7 27.5 %collective-permute-start.1 = (f32[3,640,128]{2,1,0:T(8,128)}, f32[3,640,128]{2,1,0:T(8,128)S(1)}, u32[]{:S(2)}, u32[]{:S(2)}) collective-permute-start(f32[3,640,128]{2,1,0:T(8,128)} %collective-permute-done.mate.refs_1_), channel_id=1, source_target_pairs={{0,2},{2,4},{3,1},{4,6},{5,3},{6,8},{7,5},{8,10},{9,7},{10,12},{11... | collective-permute-start | bytes 2949128 | tf_op jit(solution)/shard_map/ppermute | solution.py:500
  62.7 4.6 %copy-start.13 = (s32[300]{0:T(512)S(1)}, s32[300]{0:T(512)}, u32[]{:S(2)}) copy-start(s32[300]{0:T(512)} %param.10) | copy-start | bytes 3604
  62.7 13.5 %copy-start.4 = (f32[3,640,128]{2,1,0:T(8,128)S(1)}, f32[3,640,128]{2,1,0:T(8,128)}, u32[]{:S(2)}) copy-start(f32[3,640,128]{2,1,0:T(8,128)} %get-tuple-element.25.own) | copy-start | bytes 2949124
  62.7 13.5 %copy-start.10 = (s32[9]{0:T(128)S(1)}, s32[9]{0:T(128)}, u32[]{:S(2)}) copy-start(s32[9]{0:T(128)} %row_off.3) | copy-start | bytes 112
  62.7 13.5 %copy-start.11 = (s32[9]{0:T(128)S(1)}, s32[9]{0:T(128)}, u32[]{:S(2)}) copy-start(s32[9]{0:T(128)} %col_off.3) | copy-start | bytes 112
  62.7 36.6 %all-to-all-start = ((f32[4,76,8,128]{3,2,1,0:T(8,128)}), f32[4,76,8,128]{3,2,1,0:T(8,128)}, u32[]{:S(2)}, u32[]{:S(2)}) async-start(f32[4,76,8,128]{3,2,1,0:T(8,128)} %get-tuple-element.30), calls=%async_computation | async-start | bytes 2490368 | tf_op jit(solution)/shard_map/all_to_all | solution.py:501
  67.4 48.1 %collective-permute-start.4 = (f32[3,576,128]{2,1,0:T(8,128)}, f32[3,576,128]{2,1,0:T(8,128)}, u32[]{:S(2)}, u32[]{:S(2)}) collective-permute-start(f32[3,576,128]{2,1,0:T(8,128)} %collective-permute-done.3.refs_0_.mate), channel_id=1, source_target_pairs={{0,2},{2,4},{3,1},{4,6},{5,3},{6,8},{7,5},{8,10},{9,7},{10,12},{11... | collective-permute-start | bytes 2654216 | tf_op jit(solution)/shard_map/ppermute | solution.py:510
  69.3 46.2 %collective-permute-start.5 = (f32[3,576,128]{2,1,0:T(8,128)}, f32[3,576,128]{2,1,0:T(8,128)}, u32[]{:S(2)}, u32[]{:S(2)}) collective-permute-start(f32[3,576,128]{2,1,0:T(8,128)} %get-tuple-element.29.own), channel_id=1, source_target_pairs={{1,3},{2,0},{3,5},{4,2},{5,7},{6,4},{7,9},{8,6},{9,11},{10,8},{11,... | collective-permute-start | bytes 2654216 | tf_op jit(solution)/shard_map/ppermute | solution.py:499
  81.6 17.7 %collective-permute-start.6 = (f32[640,128]{1,0:T(8,128)S(1)}, f32[640,128]{1,0:T(8,128)S(1)}, u32[]{:S(2)}, u32[]{:S(2)}) collective-permute-start(f32[640,128]{1,0:T(8,128)S(1)} %get-tuple-element.31.refs_1_), channel_id=1, source_target_pairs={{0,1},{1,0},{2,3},{3,2},{4,5},{5,4},{6,7},{7,6},{8,9},{9,8},{10,11... | collective-permute-start | bytes 983048 | tf_op jit(solution)/shard_map/ppermute | solution.py:514
  100.0 15.5 %copy-start.5 = (f32[3,576,128]{2,1,0:T(8,128)S(1)}, f32[3,576,128]{2,1,0:T(8,128)}, u32[]{:S(2)}) copy-start(f32[3,576,128]{2,1,0:T(8,128)} %get-tuple-element.29.own) | copy-start | bytes 2654212
  104.8 8.5 %copy-start.15 = (f32[76,8,128]{2,1,0:T(8,128)S(1)}, f32[76,8,128]{2,1,0:T(8,128)}, u32[]{:S(2)}) copy-start(f32[76,8,128]{2,1,0:T(8,128)} %get-tuple-element.40) | copy-start | bytes 933892
  104.8 10.4 %copy-start.14 = (f32[76,8,128]{2,1,0:T(8,128)S(1)}, f32[76,8,128]{2,1,0:T(8,128)}, u32[]{:S(2)}) copy-start(f32[76,8,128]{2,1,0:T(8,128)} %get-tuple-element.39) | copy-start | bytes 933892
  104.8 10.7 %copy-start.1 = (f32[32,40,128]{2,1,0:T(8,128)S(1)}, f32[32,40,128]{2,1,0:T(8,128)}, u32[]{:S(2)}) copy-start(f32[32,40,128]{2,1,0:T(8,128)} %get-tuple-element.35.refs_1_) | copy-start | bytes 1966084
  104.8 40.4 %all-to-all-start.1 = ((f32[32,40,128]{2,1,0:T(8,128)}), f32[32,40,128]{2,1,0:T(8,128)S(1)}, u32[]{:S(2)}, u32[]{:S(2)}) async-start(f32[32,40,128]{2,1,0:T(8,128)} %get-tuple-element.35.refs_1_), calls=%async_computation.1 | async-start | bytes 1310720 | tf_op jit(solution)/shard_map/all_to_all | solution.py:535
  113.2 2.3 %collective-permute-start.7 = (f32[76,8,128]{2,1,0:T(8,128)}, f32[76,8,128]{2,1,0:T(8,128)S(1)}, u32[]{:S(2)}, u32[]{:S(2)}) collective-permute-start(f32[76,8,128]{2,1,0:T(8,128)} %get-tuple-element.34), channel_id=1, source_target_pairs={{0,32},{32,0},{64,96},{96,64},{1,33},{33,1},{65,97},{97,65},{2,34}... | collective-permute-start | bytes 933896 | tf_op jit(solution)/shard_map/ppermute | solution.py:520
  113.3 14.1 %collective-permute-start.10 = (f32[76,8,128]{2,1,0:T(8,128)S(1)}, f32[76,8,128]{2,1,0:T(8,128)S(1)}, u32[]{:S(2)}, u32[]{:S(2)}) collective-permute-start(f32[76,8,128]{2,1,0:T(8,128)S(1)} %copy-done.15), channel_id=1, source_target_pairs={{0,96},{32,64},{64,32},{96,0},{1,97},{33,65},{65,33},{97,1},{2,98}... | collective-permute-start | bytes 933896 | tf_op jit(solution)/shard_map/ppermute | solution.py:520
  115.2 20.3 %copy-start.9 = (f32[76,8,128]{2,1,0:T(8,128)S(1)}, f32[76,8,128]{2,1,0:T(8,128)}, u32[]{:S(2)}) copy-start(f32[76,8,128]{2,1,0:T(8,128)} %get-tuple-element.38.refs_0_) | copy-start | bytes 933892
  115.2 20.3 %collective-permute-start.9 = (f32[76,8,128]{2,1,0:T(8,128)S(1)}, f32[76,8,128]{2,1,0:T(8,128)S(1)}, u32[]{:S(2)}, u32[]{:S(2)}) collective-permute-start(f32[76,8,128]{2,1,0:T(8,128)S(1)} %copy-done.14), channel_id=1, source_target_pairs={{0,64},{32,96},{64,0},{96,32},{1,65},{33,97},{65,1},{97,33},{2,66}... | collective-permute-start | bytes 933896 | tf_op jit(solution)/shard_map/ppermute | solution.py:520
  120.0 22.8 %collective-permute-start.8 = (f32[576,128]{1,0:T(8,128)S(1)}, f32[576,128]{1,0:T(8,128)S(1)}, u32[]{:S(2)}, u32[]{:S(2)}) collective-permute-start(f32[576,128]{1,0:T(8,128)S(1)} %get-tuple-element.37), channel_id=1, source_target_pairs={{0,1},{1,0},{2,3},{3,2},{4,5},{5,4},{6,7},{7,6},{8,9},{9,8},{10,11... | collective-permute-start | bytes 884744 | tf_op jit(solution)/shard_map/ppermute | solution.py:526
  123.4 19.4 %copy-start.3 = (f32[640,128]{1,0:T(8,128)S(1)}, f32[640,128]{1,0:T(8,128)}, u32[]{:S(2)}) copy-start(f32[640,128]{1,0:T(8,128)} %copy-done.2) | copy-start | bytes 983044
  123.5 19.4 %copy-start.8 = (f32[640,128]{1,0:T(8,128)S(1)}, f32[640,128]{1,0:T(8,128)}, u32[]{:S(2)}) copy-start(f32[640,128]{1,0:T(8,128)} %copy-done.7) | copy-start | bytes 983044
  (5 other events, 8.3 us)

commit v7 on v6

--- a/solution.py
+++ b/solution.py
@@ -481,19 +481,19 @@
     late = share - early
 
     sent_a, looked = look_sums(
-        other.reshape(1), early, early // 2, 0, slots, phase, weight, pool
+        other.reshape(1), early, early // 4, 0, slots, phase, weight, pool
     )
     mate_a = lax.ppermute(sent_a, "rows", mates)
     sent_b, looked = look_sums(
-        (other + early * 32).reshape(1), late, late // 2, early, slots, phase, weight, pool, looked
+        (other + early * 32).reshape(1), late, late // 3, early, slots, phase, weight, pool, looked
     )
     mate_b = lax.ppermute(sent_b, "rows", mates)
     own_a, looked = look_sums(
-        mine.reshape(1), early, early // 2, share, slots, phase, weight, pool, looked
+        mine.reshape(1), early, early // 4, share, slots, phase, weight, pool, looked
     )
     far_a = lax.ppermute(own_a, "rows", outward)
     own_b, looked = look_sums(
-        (mine + early * 32).reshape(1), late, late // 2, share + early, slots,
+        (mine + early * 32).reshape(1), late, late // 3, share + early, slots,
         phase, weight, pool, looked, (mate_a,),
     )
     far_b = lax.ppermute(own_b, "rows", outward)

time: 148 us -> 148 us (level)
  no operation moved by 1% of the time
where the time goes in v7:
time: 148 us; the launch traced here: 146 us
  Pallas kernels  84.4 us (57%)
  starting transfers between devices  38.2 us (26%)
  waiting for transfers between devices  18.7 us (13%)
  local copies, waits for them, and re-layouts  3.67 us (2%)
    pallas_call x4, Pallas kernels, look_sums(): pl.pallas_call(look_kernel, grid_spec=pltpu.PrefetchScalarGridSpec(num_sc...  49.9 us
    pallas_call x1, Pallas kernels, network_solve(): pl.pallas_call(functools.partial(network_kernel, slots=slots), grid=(1,),...  16.6 us
    ppermute x3, waiting for transfers between devices, local(): lax.ppermute(residual[d], 'ifg', [(i, i ^ d) for i in range(GROUPS)])  11.9 us
    pallas_call x2, Pallas kernels, window_coherence(): pl.pallas_call(window_kernel, grid=(2,), in_specs=[pl.BlockSpec(memory_sp...  9.12 us
    all_to_all x1, starting transfers between devices, local(): lax.all_to_all(history, 'rows', split_axis=0, concat_axis=0, tiled=True)  8.42 us
    ppermute x1, starting transfers between devices, local(): far_a = lax.ppermute(own_a, 'rows', outward)  6.19 us
    ppermute x1, starting transfers between devices, local(): far_b = lax.ppermute(own_b, 'rows', outward)  6.04 us
    ppermute x1, waiting for transfers between devices, local(): back_b = lax.ppermute(mate_part_b, 'rows', mates)  5.62 us
  transfers between devices with their start and end apart: 13, of which 4 were waited for; matrix products, arithmetic and copies ran while one was open for 1% of the time, Pallas kernels for 48%

profile of v7, /device:TPU:6, one launch (start us, length us, event | category | flops | bytes accessed | tf_op | source)
XLA Modules:
  0.0 145.9 jit_solution(11035755501060414552)
XLA Ops:
  0.6 13.1 %look_sums.4 = (f32[3,640,128]{2,1,0:T(8,128)}, f32[4,76,8,128]{3,2,1,0:T(8,128)}) custom-call(s32[1]{0:T(128)} %bitcast.2.start, bf16[2400,16,128]{2,1,0:T(8,128)(2,1)} %bitcast.29, bf16[2400,16,128]{2,1,0:T(8,128)(2,1)} %bitcast.33, bf16[1024,128]{1,0:T(8,128)(2,1)} %constant.23.clone.pool), custom_call_target="tpu_custom_call" | custom-call | bytes 72000 | tf_op jit(solution)/shard_map/look_sums/pallas_call | solution.py:136
  13.7 3.2 %collective-permute-start = (f32[3,640,128]{2,1,0:T(8,128)}, f32[3,640,128]{2,1,0:T(8,128)}, u32[]{:S(2)}, u32[]{:S(2)}) collective-permute-start(f32[3,640,128]{2,1,0:T(8,128)} %get-tuple-element.22), channel_id=1, source_target_pairs={{0,1},{1,0},{2,3},{3,2},{4,5},{5,4},{6,7},{7,6},{8,9},{9,8},{10,11... | collective-permute-start | bytes 2949128 | tf_op jit(solution)/shard_map/ppermute | solution.py:486
  16.9 11.9 %look_sums.5 = (f32[3,576,128]{2,1,0:T(8,128)}, f32[4,76,8,128]{3,2,1,0:T(8,128)}) custom-call(s32[1]{0:T(128)} %bitcast.14.start, bf16[2400,16,128]{2,1,0:T(8,128)(2,1)} %bitcast.30, bf16[2400,16,128]{2,1,0:T(8,128)(2,1)} %bitcast.34, bf16[1024,128]{1,0:T(8,128)(2,1)} %constant.23.clone.pool, ...), custom_call_target="tpu_custom_call", output_to_operand_aliasing={{1}: (4, {})} | custom-call | bytes 72000 | tf_op jit(solution)/shard_map/look_sums/pallas_call | solution.py:136
  29.1 13.0 %look_sums.6 = (f32[3,640,128]{2,1,0:T(8,128)}, f32[4,76,8,128]{3,2,1,0:T(8,128)}) custom-call(s32[1]{0:T(128)} %bitcast.9.start, bf16[2400,16,128]{2,1,0:T(8,128)(2,1)} %bitcast.31, bf16[2400,16,128]{2,1,0:T(8,128)(2,1)} %bitcast.35, bf16[1024,128]{1,0:T(8,128)(2,1)} %constant.23.clone.pool, ...), custom_call_target="tpu_custom_call", output_to_operand_aliasing={{1}: (4, {})} | custom-call | bytes 72000 | tf_op jit(solution)/shard_map/look_sums/pallas_call | solution.py:136
  42.1 6.2 %collective-permute-start.2 = (f32[3,640,128]{2,1,0:T(8,128)}, f32[3,640,128]{2,1,0:T(8,128)S(1)}, u32[]{:S(2)}, u32[]{:S(2)}) collective-permute-start(f32[3,640,128]{2,1,0:T(8,128)} %get-tuple-element.25.own), channel_id=1, source_target_pairs={{1,3},{2,0},{3,5},{4,2},{5,7},{6,4},{7,9},{8,6},{9,11},{10,8},{11,... | collective-permute-start | bytes 2949128 | tf_op jit(solution)/shard_map/ppermute | solution.py:494
  48.3 1.9 %collective-permute-start.1 = (f32[3,640,128]{2,1,0:T(8,128)}, f32[3,640,128]{2,1,0:T(8,128)S(1)}, u32[]{:S(2)}, u32[]{:S(2)}) collective-permute-start(f32[3,640,128]{2,1,0:T(8,128)} %collective-permute-done.mate.refs_1_), channel_id=1, source_target_pairs={{0,2},{2,4},{3,1},{4,6},{5,3},{6,8},{7,5},{8,10},{9,7},{10,12},{11... | collective-permute-start | bytes 2949128 | tf_op jit(solution)/shard_map/ppermute | solution.py:500
  50.3 11.9 %look_sums.7 = (f32[3,576,128]{2,1,0:T(8,128)}, f32[4,76,8,128]{3,2,1,0:T(8,128)}) custom-call(s32[1]{0:T(128)} %bitcast.16.start, bf16[2400,16,128]{2,1,0:T(8,128)(2,1)} %bitcast.32, bf16[2400,16,128]{2,1,0:T(8,128)(2,1)} %bitcast.36, bf16[1024,128]{1,0:T(8,128)(2,1)} %constant.23.clone.pool, ...), custom_call_target="tpu_custom_call", output_to_operand_aliasing={{1}: (4, {})} | custom-call | bytes 72000 | tf_op jit(solution)/shard_map/look_sums/pallas_call | solution.py:136
  62.2 4.4 %all-to-all-start = ((f32[4,76,8,128]{3,2,1,0:T(8,128)}), f32[4,76,8,128]{3,2,1,0:T(8,128)}, u32[]{:S(2)}, u32[]{:S(2)}) async-start(f32[4,76,8,128]{3,2,1,0:T(8,128)} %get-tuple-element.30), calls=%async_computation | async-start | bytes 2490368 | tf_op jit(solution)/shard_map/all_to_all | solution.py:501
  66.9 1.9 %collective-permute-start.4 = (f32[3,576,128]{2,1,0:T(8,128)}, f32[3,576,128]{2,1,0:T(8,128)}, u32[]{:S(2)}, u32[]{:S(2)}) collective-permute-start(f32[3,576,128]{2,1,0:T(8,128)} %collective-permute-done.3.refs_0_.mate), channel_id=1, source_target_pairs={{0,2},{2,4},{3,1},{4,6},{5,3},{6,8},{7,5},{8,10},{9,7},{10,12},{11... | collective-permute-start | bytes 2654216 | tf_op jit(solution)/shard_map/ppermute | solution.py:510
  68.8 6.0 %collective-permute-start.5 = (f32[3,576,128]{2,1,0:T(8,128)}, f32[3,576,128]{2,1,0:T(8,128)}, u32[]{:S(2)}, u32[]{:S(2)}) collective-permute-start(f32[3,576,128]{2,1,0:T(8,128)} %get-tuple-element.29.own), channel_id=1, source_target_pairs={{1,3},{2,0},{3,5},{4,2},{5,7},{6,4},{7,9},{8,6},{9,11},{10,8},{11,... | collective-permute-start | bytes 2654216 | tf_op jit(solution)/shard_map/ppermute | solution.py:499
  75.9 4.6 %window_coherence.2 = (f32[640,128]{1,0:T(8,128)S(1)}, f32[640,128]{1,0:T(8,128)S(1)}) custom-call(s32[9]{0:T(128)S(1)} %copy-done.10, s32[9]{0:T(128)S(1)} %copy-done.11, s32[1]{0:T(128)} %bitcast.1.flip, f32[3,640,128]{2,1,0:T(8,128)S(1)} %collective-permute-done.1.near, f32[3,640,128]{2,1,0:T(8,128)S(1)} %copy-done.4, ...), custom_call_target="tpu_custom_call" | custom-call | bytes 72000 | tf_op jit(solution)/shard_map/window_coherence/pallas_call | solution.py:205
  82.2 16.6 %network_solve.1 = (f32[160,304]{1,0:T(8,128)}, f32[304,160]{1,0:T(8,128)}) custom-call(s32[1]{0:T(128)} %bitcast.1.flip, s32[2,304]{1,0:T(2,128)} %select_n.14.dates, f32[3,576,128]{2,1,0:T(8,128)} %collective-permute-done.3.refs_0_.mate, f32[640,128]{1,0:T(8,128)} %copy-done.6), custom_call_target="tpu_custom_call" | custom-call | bytes 72000 | tf_op jit(solution)/shard_map/network_solve/pallas_call | solution.py:360
  99.5 4.8 %invert.1 = (f32[76,8,128]{2,1,0:T(8,128)}, f32[76,8,128]{2,1,0:T(8,128)}, f32[76,8,128]{2,1,0:T(8,128)}, f32[76,8,128]{2,1,0:T(8,128)}, f32[32,40,128]{2,1,0:T(8,128)}) custom-call(s32[1]{0:T(128)} %bitcast.17.group, f32[4,76,8,128]{3,2,1,0:T(8,128)} %all-to-all-done.looked, f32[160,304]{1,0:T(8,128)} %get-tuple-element.32.inverse, ...), custom_call_target="tpu_custom_call" | custom-call | bytes 72000 | tf_op jit(solution)/shard_map/invert/pallas_call | solution.py:412
  104.3 8.4 %all-to-all-start.1 = ((f32[32,40,128]{2,1,0:T(8,128)}), f32[32,40,128]{2,1,0:T(8,128)S(1)}, u32[]{:S(2)}, u32[]{:S(2)}) async-start(f32[32,40,128]{2,1,0:T(8,128)} %get-tuple-element.35.refs_1_), calls=%async_computation.1 | async-start | bytes 1310720 | tf_op jit(solution)/shard_map/all_to_all | solution.py:535
  112.9 1.8 %collective-permute-start.10 = (f32[76,8,128]{2,1,0:T(8,128)S(1)}, f32[76,8,128]{2,1,0:T(8,128)S(1)}, u32[]{:S(2)}, u32[]{:S(2)}) collective-permute-start(f32[76,8,128]{2,1,0:T(8,128)S(1)} %copy-done.15), channel_id=1, source_target_pairs={{0,96},{32,64},{64,32},{96,0},{1,97},{33,65},{65,33},{97,1},{2,98}... | collective-permute-start | bytes 933896 | tf_op jit(solution)/shard_map/ppermute | solution.py:520
  115.0 4.5 %window_coherence.3 = (f32[576,128]{1,0:T(8,128)S(1)}, f32[576,128]{1,0:T(8,128)S(1)}) custom-call(s32[9]{0:T(128)S(1)} %copy-done.10, s32[9]{0:T(128)S(1)} %copy-done.11, s32[1]{0:T(128)} %bitcast.1.flip, f32[3,576,128]{2,1,0:T(8,128)} %collective-permute-done.4.near, f32[3,576,128]{2,1,0:T(8,128)S(1)} %copy-done.5, ...), custom_call_target="tpu_custom_call" | custom-call | bytes 72000 | tf_op jit(solution)/shard_map/window_coherence/pallas_call | solution.py:205
  119.5 3.4 %collective-permute-start.8 = (f32[576,128]{1,0:T(8,128)S(1)}, f32[576,128]{1,0:T(8,128)S(1)}, u32[]{:S(2)}, u32[]{:S(2)}) collective-permute-start(f32[576,128]{1,0:T(8,128)S(1)} %get-tuple-element.37), channel_id=1, source_target_pairs={{0,1},{1,0},{2,3},{3,2},{4,5},{5,4},{6,7},{7,6},{8,9},{9,8},{10,11... | collective-permute-start | bytes 884744 | tf_op jit(solution)/shard_map/ppermute | solution.py:526
  123.1 3.9 %collective-permute-done.10.refs_3_ = f32[76,8,128]{2,1,0:T(8,128)S(1)} collective-permute-done((f32[76,8,128]{2,1,0:T(8,128)S(1)}, f32[76,8,128]{2,1,0:T(8,128)S(1)}, u32[]{:S(2)}, u32[]{:S(2)}) %collective-permute-start.10) | collective-permute-done | bytes 311328 | tf_op jit(solution)/shard_map/ppermute | solution.py:520
  127.0 8.0 %collective-permute-done.9.refs_2_ = f32[76,8,128]{2,1,0:T(8,128)S(1)} collective-permute-done((f32[76,8,128]{2,1,0:T(8,128)S(1)}, f32[76,8,128]{2,1,0:T(8,128)S(1)}, u32[]{:S(2)}, u32[]{:S(2)}) %collective-permute-start.9) | collective-permute-done | bytes 311328 | tf_op jit(solution)/shard_map/ppermute | solution.py:520
  135.0 1.7 %unslot.1.refs_0_ = f32[75,4,8,128]{3,2,1,0:T(8,128)} custom-call(s32[2]{0:T(128)S(1)} %pad_add_fusion.where, f32[76,8,128]{2,1,0:T(8,128)S(1)} %copy-done.9, f32[76,8,128]{2,1,0:T(8,128)S(1)} %collective-permute-done.7.refs_0_.refs_1_, f32[76,8,128]{2,1,0:T(8,128)S(1)} %collective-permute-done.9.refs_2_, f32[76,8,128]{2,1,0:T(8,128)S(1)} %collective-permute-done.10.refs_3_), custom_call_target="tpu_custom_call" | custom-call | bytes 180000000 | tf_op jit(solution)/shard_map/unslot/pallas_call | solution.py:271
  136.7 5.6 %collective-permute-done.8 = f32[576,128]{1,0:T(8,128)S(1)} collective-permute-done((f32[576,128]{1,0:T(8,128)S(1)}, f32[576,128]{1,0:T(8,128)S(1)}, u32[]{:S(2)}, u32[]{:S(2)}) %collective-permute-start.8) | collective-permute-done | bytes 294944 | tf_op jit(solution)/shard_map/ppermute | solution.py:526
  142.4 1.3 copy-done
  143.7 1.1 merge.1
  144.8 1.1 unpack.1
  (53 shorter events, 4.4 us)
Async XLA Ops:
  13.7 34.6 %collective-permute-start = (f32[3,640,128]{2,1,0:T(8,128)}, f32[3,640,128]{2,1,0:T(8,128)}, u32[]{:S(2)}, u32[]{:S(2)}) collective-permute-start(f32[3,640,128]{2,1,0:T(8,128)} %get-tuple-element.22), channel_id=1, source_target_pairs={{0,1},{1,0},{2,3},{3,2},{4,5},{5,4},{6,7},{7,6},{8,9},{9,8},{10,11... | collective-permute-start | bytes 2949128 | tf_op jit(solution)/shard_map/ppermute | solution.py:486
  28.8 38.1 %collective-permute-start.3 = (f32[3,576,128]{2,1,0:T(8,128)}, f32[3,576,128]{2,1,0:T(8,128)}, u32[]{:S(2)}, u32[]{:S(2)}) collective-permute-start(f32[3,576,128]{2,1,0:T(8,128)} %get-tuple-element.27), channel_id=1, source_target_pairs={{0,1},{1,0},{2,3},{3,2},{4,5},{5,4},{6,7},{7,6},{8,9},{9,8},{10,11... | collective-permute-start | bytes 2654216 | tf_op jit(solution)/shard_map/ppermute | solution.py:490
  42.1 32.7 %collective-permute-start.2 = (f32[3,640,128]{2,1,0:T(8,128)}, f32[3,640,128]{2,1,0:T(8,128)S(1)}, u32[]{:S(2)}, u32[]{:S(2)}) collective-permute-start(f32[3,640,128]{2,1,0:T(8,128)} %get-tuple-element.25.own), channel_id=1, source_target_pairs={{1,3},{2,0},{3,5},{4,2},{5,7},{6,4},{7,9},{8,6},{9,11},{10,8},{11,... | collective-permute-start | bytes 2949128 | tf_op jit(solution)/shard_map/ppermute | solution.py:494
  48.3 27.6 %collective-permute-start.1 = (f32[3,640,128]{2,1,0:T(8,128)}, f32[3,640,128]{2,1,0:T(8,128)S(1)}, u32[]{:S(2)}, u32[]{:S(2)}) collective-permute-start(f32[3,640,128]{2,1,0:T(8,128)} %collective-permute-done.mate.refs_1_), channel_id=1, source_target_pairs={{0,2},{2,4},{3,1},{4,6},{5,3},{6,8},{7,5},{8,10},{9,7},{10,12},{11... | collective-permute-start | bytes 2949128 | tf_op jit(solution)/shard_map/ppermute | solution.py:500
  62.2 4.6 %copy-start.13 = (s32[300]{0:T(512)S(1)}, s32[300]{0:T(512)}, u32[]{:S(2)}) copy-start(s32[300]{0:T(512)} %param.10) | copy-start | bytes 3604
  62.2 13.7 %copy-start.4 = (f32[3,640,128]{2,1,0:T(8,128)S(1)}, f32[3,640,128]{2,1,0:T(8,128)}, u32[]{:S(2)}) copy-start(f32[3,640,128]{2,1,0:T(8,128)} %get-tuple-element.25.own) | copy-start | bytes 2949124
  62.2 13.7 %copy-start.10 = (s32[9]{0:T(128)S(1)}, s32[9]{0:T(128)}, u32[]{:S(2)}) copy-start(s32[9]{0:T(128)} %row_off.3) | copy-start | bytes 112
  62.2 13.7 %copy-start.11 = (s32[9]{0:T(128)S(1)}, s32[9]{0:T(128)}, u32[]{:S(2)}) copy-start(s32[9]{0:T(128)} %col_off.3) | copy-start | bytes 112
  62.2 36.6 %all-to-all-start = ((f32[4,76,8,128]{3,2,1,0:T(8,128)}), f32[4,76,8,128]{3,2,1,0:T(8,128)}, u32[]{:S(2)}, u32[]{:S(2)}) async-start(f32[4,76,8,128]{3,2,1,0:T(8,128)} %get-tuple-element.30), calls=%async_computation | async-start | bytes 2490368 | tf_op jit(solution)/shard_map/all_to_all | solution.py:501
  66.9 48.2 %collective-permute-start.4 = (f32[3,576,128]{2,1,0:T(8,128)}, f32[3,576,128]{2,1,0:T(8,128)}, u32[]{:S(2)}, u32[]{:S(2)}) collective-permute-start(f32[3,576,128]{2,1,0:T(8,128)} %collective-permute-done.3.refs_0_.mate), channel_id=1, source_target_pairs={{0,2},{2,4},{3,1},{4,6},{5,3},{6,8},{7,5},{8,10},{9,7},{10,12},{11... | collective-permute-start | bytes 2654216 | tf_op jit(solution)/shard_map/ppermute | solution.py:510
  68.8 46.2 %collective-permute-start.5 = (f32[3,576,128]{2,1,0:T(8,128)}, f32[3,576,128]{2,1,0:T(8,128)}, u32[]{:S(2)}, u32[]{:S(2)}) collective-permute-start(f32[3,576,128]{2,1,0:T(8,128)} %get-tuple-element.29.own), channel_id=1, source_target_pairs={{1,3},{2,0},{3,5},{4,2},{5,7},{6,4},{7,9},{8,6},{9,11},{10,8},{11,... | collective-permute-start | bytes 2654216 | tf_op jit(solution)/shard_map/ppermute | solution.py:499
  81.3 17.5 %collective-permute-start.6 = (f32[640,128]{1,0:T(8,128)S(1)}, f32[640,128]{1,0:T(8,128)S(1)}, u32[]{:S(2)}, u32[]{:S(2)}) collective-permute-start(f32[640,128]{1,0:T(8,128)S(1)} %get-tuple-element.31.refs_1_), channel_id=1, source_target_pairs={{0,1},{1,0},{2,3},{3,2},{4,5},{5,4},{6,7},{7,6},{8,9},{9,8},{10,11... | collective-permute-start | bytes 983048 | tf_op jit(solution)/shard_map/ppermute | solution.py:514
  99.5 15.5 %copy-start.5 = (f32[3,576,128]{2,1,0:T(8,128)S(1)}, f32[3,576,128]{2,1,0:T(8,128)}, u32[]{:S(2)}) copy-start(f32[3,576,128]{2,1,0:T(8,128)} %get-tuple-element.29.own) | copy-start | bytes 2654212
  104.3 8.5 %copy-start.15 = (f32[76,8,128]{2,1,0:T(8,128)S(1)}, f32[76,8,128]{2,1,0:T(8,128)}, u32[]{:S(2)}) copy-start(f32[76,8,128]{2,1,0:T(8,128)} %get-tuple-element.40) | copy-start | bytes 933892
  104.3 10.4 %copy-start.14 = (f32[76,8,128]{2,1,0:T(8,128)S(1)}, f32[76,8,128]{2,1,0:T(8,128)}, u32[]{:S(2)}) copy-start(f32[76,8,128]{2,1,0:T(8,128)} %get-tuple-element.39) | copy-start | bytes 933892
  104.3 10.7 %copy-start.1 = (f32[32,40,128]{2,1,0:T(8,128)S(1)}, f32[32,40,128]{2,1,0:T(8,128)}, u32[]{:S(2)}) copy-start(f32[32,40,128]{2,1,0:T(8,128)} %get-tuple-element.35.refs_1_) | copy-start | bytes 1966084
  104.3 40.4 %all-to-all-start.1 = ((f32[32,40,128]{2,1,0:T(8,128)}), f32[32,40,128]{2,1,0:T(8,128)S(1)}, u32[]{:S(2)}, u32[]{:S(2)}) async-start(f32[32,40,128]{2,1,0:T(8,128)} %get-tuple-element.35.refs_1_), calls=%async_computation.1 | async-start | bytes 1310720 | tf_op jit(solution)/shard_map/all_to_all | solution.py:535
  112.8 2.3 %collective-permute-start.7 = (f32[76,8,128]{2,1,0:T(8,128)}, f32[76,8,128]{2,1,0:T(8,128)S(1)}, u32[]{:S(2)}, u32[]{:S(2)}) collective-permute-start(f32[76,8,128]{2,1,0:T(8,128)} %get-tuple-element.34), channel_id=1, source_target_pairs={{0,32},{32,0},{64,96},{96,64},{1,33},{33,1},{65,97},{97,65},{2,34}... | collective-permute-start | bytes 933896 | tf_op jit(solution)/shard_map/ppermute | solution.py:520
  112.9 14.1 %collective-permute-start.10 = (f32[76,8,128]{2,1,0:T(8,128)S(1)}, f32[76,8,128]{2,1,0:T(8,128)S(1)}, u32[]{:S(2)}, u32[]{:S(2)}) collective-permute-start(f32[76,8,128]{2,1,0:T(8,128)S(1)} %copy-done.15), channel_id=1, source_target_pairs={{0,96},{32,64},{64,32},{96,0},{1,97},{33,65},{65,33},{97,1},{2,98}... | collective-permute-start | bytes 933896 | tf_op jit(solution)/shard_map/ppermute | solution.py:520
  114.7 20.3 %copy-start.9 = (f32[76,8,128]{2,1,0:T(8,128)S(1)}, f32[76,8,128]{2,1,0:T(8,128)}, u32[]{:S(2)}) copy-start(f32[76,8,128]{2,1,0:T(8,128)} %get-tuple-element.38.refs_0_) | copy-start | bytes 933892
  114.7 20.3 %collective-permute-start.9 = (f32[76,8,128]{2,1,0:T(8,128)S(1)}, f32[76,8,128]{2,1,0:T(8,128)S(1)}, u32[]{:S(2)}, u32[]{:S(2)}) collective-permute-start(f32[76,8,128]{2,1,0:T(8,128)S(1)} %copy-done.14), channel_id=1, source_target_pairs={{0,64},{32,96},{64,0},{96,32},{1,65},{33,97},{65,1},{97,33},{2,66}... | collective-permute-start | bytes 933896 | tf_op jit(solution)/shard_map/ppermute | solution.py:520
  119.5 22.8 %collective-permute-start.8 = (f32[576,128]{1,0:T(8,128)S(1)}, f32[576,128]{1,0:T(8,128)S(1)}, u32[]{:S(2)}, u32[]{:S(2)}) collective-permute-start(f32[576,128]{1,0:T(8,128)S(1)} %get-tuple-element.37), channel_id=1, source_target_pairs={{0,1},{1,0},{2,3},{3,2},{4,5},{5,4},{6,7},{7,6},{8,9},{9,8},{10,11... | collective-permute-start | bytes 884744 | tf_op jit(solution)/shard_map/ppermute | solution.py:526
  123.0 19.4 %copy-start.3 = (f32[640,128]{1,0:T(8,128)S(1)}, f32[640,128]{1,0:T(8,128)}, u32[]{:S(2)}) copy-start(f32[640,128]{1,0:T(8,128)} %copy-done.2) | copy-start | bytes 983044
  123.0 19.4 %copy-start.8 = (f32[640,128]{1,0:T(8,128)S(1)}, f32[640,128]{1,0:T(8,128)}, u32[]{:S(2)}) copy-start(f32[640,128]{1,0:T(8,128)} %copy-done.7) | copy-start | bytes 983044
  (5 other events, 8.1 us)
